TPU v7x, 32 devices: a whole 2x2x4 slice. The times are simulated.
32 devices in a mesh: fsdp: 8 (over z, y), dp: 4 (over x, core).
Axes of the slice: x: 2, y: 2, z: 4, core: 2. Of those that a mesh axis runs over, the one named last changes fastest.
Arguments:
- tokens: bfloat16 [16, 1024, 768], P('fsdp', 'dp'), may hold values from -6 to 6
- condition: bfloat16 [16, 128], P('fsdp'), may hold values from -6 to 6
- segments: int32 [16, 1024], P('fsdp'), may hold values from 0 to 7, as said below
- w_ada: bfloat16 [128, 4608], P(None, 'fsdp'), may hold values from -0.5 to 0.5
- b_ada: bfloat16 [4608], P('fsdp'), may hold values from -1.5 to 1.5
- gain_attn: bfloat16 [768], P('fsdp'), may hold values from 0.5 to 1.5
- w_qkv: bfloat16 [768, 2304], P(None, 'fsdp'), may hold values from -0.21875 to 0.21875
- w_out: bfloat16 [768, 768], P(None, 'fsdp'), may hold values from -0.875 to 0.875
- gain_mlp: bfloat16 [768], P('fsdp'), may hold values from 0.5 to 1.5
- w_up: bfloat16 [768, 3072], P(None, 'fsdp'), may hold values from -0.21875 to 0.21875
- b_up: bfloat16 [3072], P('fsdp'), may hold values from -3 to 3
- w_down: bfloat16 [3072, 768], P(None, 'fsdp'), may hold values from -0.109375 to 0.109375
- b_down: bfloat16 [768], P('fsdp'), may hold values from -3 to 3
- cotangent: bfloat16 [16, 1024, 768], P('fsdp', 'dp'), may hold values from -8 to 8
Outputs:
- outputs: bfloat16 [16, 1024, 768], P('fsdp', 'dp')
- d_tokens: bfloat16 [16, 1024, 768], P('fsdp', 'dp')
- d_condition: bfloat16 [16, 128], P('fsdp')
- d_w_ada: float32 [128, 4608], P(None, 'fsdp')
- d_b_ada: float32 [4608], P('fsdp')
- d_gain_attn: float32 [768], P('fsdp')
- d_w_qkv: float32 [768, 2304], P(None, 'fsdp')
- d_w_out: float32 [768, 768], P(None, 'fsdp')
- d_gain_mlp: float32 [768], P('fsdp')
- d_w_up: float32 [768, 3072], P(None, 'fsdp')
- d_b_up: float32 [3072], P('fsdp')
- d_w_down: float32 [3072, 768], P(None, 'fsdp')
- d_b_down: float32 [768], P('fsdp')
Inputs may be any that keep to these rules, and one draw needn't show every extreme that they name: `segments`: within each slot the ids never fall, are 0 at the first position and 7 at the last; of each aligned run of 2 slots, one holds a document that covers positions 128 to 895.
All inputs are finite; a program needn't handle non-finite values.
Results may differ from a plain program's by a relative error of at most 0.018.
Values may be sent and summed in bfloat16 or wider, within the bound.
A program may use at most 192 MiB of HBM per device.

v0:
```python
import math

import jax
import jax.numpy as jnp
from jax import lax
from jax.sharding import PartitionSpec as P

HEAD = 64


epsilon = 1e-05
rope_base = 10000.0
masked_fill = -1e30


def norm_mod(stream, gain_row, shift_rows, scale_rows):
    average = jnp.mean(stream, axis=-1, keepdims=True)
    centered = stream - average
    variance = jnp.mean(centered * centered, axis=-1, keepdims=True)
    normal = centered * lax.rsqrt(variance + epsilon)
    return normal * gain_row * (1.0 + scale_rows[..., None, :]) + shift_rows[..., None, :]


def doc_positions(segments):
    length = segments.shape[-1]
    places = jnp.broadcast_to(jnp.arange(length, dtype=jnp.int32), segments.shape)
    starts_here = jnp.concatenate(
        [jnp.ones(segments.shape[:-1] + (1,), jnp.bool_), segments[..., 1:] != segments[..., :-1]],
        axis=-1,
    )
    openings = jnp.where(starts_here, places, jnp.zeros_like(places))
    return places - lax.cummax(openings, axis=segments.ndim - 1)


def rope_tables(positions, head_size):
    half_steps = jnp.arange(head_size // 2, dtype=jnp.float32)
    inverse = rope_base ** (-2.0 * half_steps / head_size)
    angles = positions.astype(jnp.float32)[..., None] * inverse
    return (jnp.cos(angles), jnp.sin(angles))


def rotate(vectors, cosine, sine_table):
    half_size = vectors.shape[-1] // 2
    former = vectors[..., :half_size]
    latter = vectors[..., half_size:]
    cosine_wide = cosine[..., None, :]
    sine_wide = sine_table[..., None, :]
    return jnp.concatenate(
        [former * cosine_wide - latter * sine_wide, latter * cosine_wide + former * sine_wide],
        axis=-1,
    )


def tanh_gelu(values):
    return jax.nn.gelu(values, approximate=True)


def attention_front(tokens, condition, attn_params, cosine, sine_table):
    w_ada_full, b_ada_full, gain_full, w_qkv_full, w_out_full = attn_params
    modulation = jnp.dot(
        condition, w_ada_full, preferred_element_type=jnp.float32
    ) + b_ada_full.astype(jnp.float32)
    groups = jnp.split(modulation, 6, axis=-1)
    normed = norm_mod(
        tokens.astype(jnp.float32), gain_full.astype(jnp.float32), groups[0], groups[1]
    ).astype(jnp.bfloat16)
    projected = jnp.einsum("sqd,de->sqe", normed, w_qkv_full, preferred_element_type=jnp.float32)
    slot_count, quarter, model_width = tokens.shape
    head_shape = (slot_count, quarter, model_width // HEAD, HEAD)
    queries = (
        rotate(projected[..., :model_width].reshape(head_shape), cosine, sine_table)
        .astype(jnp.bfloat16)
        .reshape(tokens.shape)
    )
    keys = (
        rotate(
            projected[..., model_width : 2 * model_width].reshape(head_shape), cosine, sine_table
        )
        .astype(jnp.bfloat16)
        .reshape(tokens.shape)
    )
    values = projected[..., 2 * model_width :].astype(jnp.bfloat16)
    return (modulation, normed, queries, keys, values)


def attend_forward(queries, keys_all, values_all, same_doc):
    slot_count, quarter, model_width = queries.shape
    score_scale = 1.0 / math.sqrt(HEAD)

    def one_head(head_index, carry):
        results, log_totals = carry
        start_col = head_index * HEAD
        query_head = lax.dynamic_slice_in_dim(queries, start_col, HEAD, 2)
        key_head = lax.dynamic_slice_in_dim(keys_all, start_col, HEAD, 2)
        value_head = lax.dynamic_slice_in_dim(values_all, start_col, HEAD, 2)
        scores = (
            jnp.einsum("sqd,skd->sqk", query_head, key_head, preferred_element_type=jnp.float32)
            * score_scale
        )
        masked = jnp.where(same_doc, scores, masked_fill)
        largest = jnp.max(masked, axis=-1, keepdims=True)
        weights = jnp.exp(masked - largest)
        totals = jnp.sum(weights, axis=-1, keepdims=True)
        weights_low = (weights / totals).astype(jnp.bfloat16)
        head_result = jnp.einsum(
            "sqk,skd->sqd", weights_low, value_head, preferred_element_type=jnp.float32
        )
        results = lax.dynamic_update_slice_in_dim(results, head_result, start_col, 2)
        log_totals = lax.dynamic_update_slice_in_dim(
            log_totals, largest + jnp.log(totals), head_index, 2
        )
        return (results, log_totals)

    initial = (
        jnp.zeros((slot_count, quarter, model_width), jnp.float32),
        jnp.zeros((slot_count, quarter, model_width // HEAD), jnp.float32),
    )
    results, log_totals = lax.fori_loop(0, model_width // HEAD, one_head, initial)
    return (results.astype(jnp.bfloat16), log_totals)


def attend_backward(queries, keys_all, values_all, grad_attended, log_totals, same_doc):
    slot_count, quarter, model_width = queries.shape
    score_scale = 1.0 / math.sqrt(HEAD)

    def one_head(head_index, carry):
        grad_query, grad_key, grad_value = carry
        start_col = head_index * HEAD
        query_head = lax.dynamic_slice_in_dim(queries, start_col, HEAD, 2)
        key_head = lax.dynamic_slice_in_dim(keys_all, start_col, HEAD, 2)
        value_head = lax.dynamic_slice_in_dim(values_all, start_col, HEAD, 2)
        grad_head = lax.dynamic_slice_in_dim(grad_attended, start_col, HEAD, 2)
        log_head = lax.dynamic_slice_in_dim(log_totals, head_index, 1, 2)
        scores = (
            jnp.einsum("sqd,skd->sqk", query_head, key_head, preferred_element_type=jnp.float32)
            * score_scale
        )
        weights = jnp.exp(jnp.where(same_doc, scores - log_head, masked_fill))
        value_dots = jnp.einsum(
            "sqd,skd->sqk", grad_head, value_head, preferred_element_type=jnp.float32
        )
        inner_sum = jnp.sum(weights * value_dots, axis=-1, keepdims=True)
        grad_scores = (weights * (value_dots - inner_sum)).astype(jnp.bfloat16)
        query_part = (
            jnp.einsum("sqk,skd->sqd", grad_scores, key_head, preferred_element_type=jnp.float32)
            * score_scale
        )
        key_part = (
            jnp.einsum("sqk,sqd->skd", grad_scores, query_head, preferred_element_type=jnp.float32)
            * score_scale
        )
        value_part = jnp.einsum(
            "sqk,sqd->skd",
            weights.astype(jnp.bfloat16),
            grad_head,
            preferred_element_type=jnp.float32,
        )
        grad_query = lax.dynamic_update_slice_in_dim(grad_query, query_part, start_col, 2)
        grad_key = lax.dynamic_update_slice_in_dim(grad_key, key_part, start_col, 2)
        grad_value = lax.dynamic_update_slice_in_dim(grad_value, value_part, start_col, 2)
        return (grad_query, grad_key, grad_value)

    initial = (
        jnp.zeros(queries.shape, jnp.float32),
        jnp.zeros(keys_all.shape, jnp.float32),
        jnp.zeros(values_all.shape, jnp.float32),
    )
    return lax.fori_loop(0, model_width // HEAD, one_head, initial)


def complete_forward(tokens, front_parts, key_pairs, same_doc, attn_params, mlp_params):
    modulation, normed, queries, keys, values = front_parts
    keys_all, values_all = key_pairs
    attended, log_totals = attend_forward(queries, keys_all, values_all, same_doc)
    groups = jnp.split(modulation, 6, axis=-1)
    w_up_full, b_up_full, w_down_full, b_down_full, gain_mlp_full = mlp_params
    branch_attn = jnp.einsum(
        "sqd,de->sqe", attended, attn_params[4], preferred_element_type=jnp.float32
    )
    middle = tokens.astype(jnp.float32) + groups[2][:, None, :] * branch_attn
    normed_mlp = norm_mod(middle, gain_mlp_full.astype(jnp.float32), groups[3], groups[4]).astype(
        jnp.bfloat16
    )
    hidden = jnp.einsum(
        "sqd,df->sqf", normed_mlp, w_up_full, preferred_element_type=jnp.float32
    ) + b_up_full.astype(jnp.float32)
    activated = tanh_gelu(hidden).astype(jnp.bfloat16)
    branch_mlp = jnp.einsum(
        "sqf,fd->sqd", activated, w_down_full, preferred_element_type=jnp.float32
    ) + b_down_full.astype(jnp.float32)
    result = middle + groups[5][:, None, :] * branch_mlp
    return (
        attended,
        log_totals,
        branch_attn,
        middle,
        normed_mlp,
        hidden,
        activated,
        branch_mlp,
        result,
    )


def shards(
    tokens,
    condition,
    segments,
    w_ada,
    b_ada,
    gain_attn,
    w_qkv,
    w_out,
    gain_mlp,
    w_up,
    b_up,
    w_down,
    b_down,
    cotangent,
):
    slot_count, quarter, model_width = tokens.shape
    quarter_start = lax.axis_index("dp") * quarter
    positions_all = doc_positions(segments)
    own_positions = lax.dynamic_slice_in_dim(positions_all, quarter_start, quarter, 1)
    own_segments = lax.dynamic_slice_in_dim(segments, quarter_start, quarter, 1)
    cosine, sine_table = rope_tables(own_positions, HEAD)
    same_doc = own_segments[:, :, None] == segments[:, None, :]
    attn_full = (
        lax.all_gather(w_ada, "fsdp", axis=1, tiled=True),
        lax.all_gather(b_ada, "fsdp", axis=0, tiled=True),
        lax.all_gather(gain_attn, "fsdp", axis=0, tiled=True),
        lax.all_gather(w_qkv, "fsdp", axis=1, tiled=True),
        lax.all_gather(w_out, "fsdp", axis=1, tiled=True),
    )
    mlp_full = (
        lax.all_gather(w_up, "fsdp", axis=1, tiled=True),
        lax.all_gather(b_up, "fsdp", axis=0, tiled=True),
        lax.all_gather(w_down, "fsdp", axis=1, tiled=True),
        lax.all_gather(b_down, "fsdp", axis=0, tiled=True),
        lax.all_gather(gain_mlp, "fsdp", axis=0, tiled=True),
    )
    front_parts = attention_front(tokens, condition, attn_full, cosine, sine_table)
    key_pairs = (
        lax.all_gather(front_parts[3], "dp", axis=1, tiled=True),
        lax.all_gather(front_parts[4], "dp", axis=1, tiled=True),
    )
    forward_state = complete_forward(tokens, front_parts, key_pairs, same_doc, attn_full, mlp_full)
    outputs = forward_state[8].astype(jnp.bfloat16)
    attn_back = (
        lax.all_gather(w_ada, "fsdp", axis=1, tiled=True),
        lax.all_gather(b_ada, "fsdp", axis=0, tiled=True),
        lax.all_gather(gain_attn, "fsdp", axis=0, tiled=True),
        lax.all_gather(w_qkv, "fsdp", axis=1, tiled=True),
        lax.all_gather(w_out, "fsdp", axis=1, tiled=True),
    )
    mlp_back = (
        lax.all_gather(w_up, "fsdp", axis=1, tiled=True),
        lax.all_gather(b_up, "fsdp", axis=0, tiled=True),
        lax.all_gather(w_down, "fsdp", axis=1, tiled=True),
        lax.all_gather(b_down, "fsdp", axis=0, tiled=True),
        lax.all_gather(gain_mlp, "fsdp", axis=0, tiled=True),
    )
    front_back = attention_front(tokens, condition, attn_back, cosine, sine_table)
    pairs_back = (
        lax.all_gather(front_back[3], "dp", axis=1, tiled=True),
        lax.all_gather(front_back[4], "dp", axis=1, tiled=True),
    )
    saved_state = complete_forward(tokens, front_back, pairs_back, same_doc, attn_back, mlp_back)
    modulation, normed, queries, keys, values = front_back
    keys_all, values_all = pairs_back
    attended, log_totals, branch_attn, middle, normed_mlp, hidden, activated, branch_mlp, result = (
        saved_state
    )
    w_ada_full, b_ada_full, gain_attn_full, w_qkv_full, w_out_full = attn_back
    w_up_full, b_up_full, w_down_full, b_down_full, gain_mlp_full = mlp_back
    groups = jnp.split(modulation, 6, axis=-1)
    grad_out = cotangent.astype(jnp.float32)
    grad_gate_mlp = jnp.sum(grad_out * branch_mlp, axis=1)
    grad_branch_mlp = (grad_out * groups[5][:, None, :]).astype(jnp.bfloat16)
    grad_w_down = jnp.einsum(
        "sqf,sqd->fd", activated, grad_branch_mlp, preferred_element_type=jnp.float32
    )
    grad_b_down = jnp.sum(grad_branch_mlp.astype(jnp.float32), axis=(0, 1))
    grad_activated = jnp.einsum(
        "sqd,fd->sqf", grad_branch_mlp, w_down_full, preferred_element_type=jnp.float32
    )
    gelu_pull = jax.vjp(tanh_gelu, hidden)[1]
    grad_hidden = gelu_pull(grad_activated)[0].astype(jnp.bfloat16)
    grad_w_up = jnp.einsum(
        "sqd,sqf->df", normed_mlp, grad_hidden, preferred_element_type=jnp.float32
    )
    grad_b_up = jnp.sum(grad_hidden.astype(jnp.float32), axis=(0, 1))
    grad_normed_mlp = jnp.einsum(
        "sqf,df->sqd", grad_hidden, w_up_full, preferred_element_type=jnp.float32
    )
    mlp_pull = jax.vjp(norm_mod, middle, gain_mlp_full.astype(jnp.float32), groups[3], groups[4])[1]
    grad_middle_norm, grad_gain_mlp, grad_shift_mlp, grad_scale_mlp = mlp_pull(grad_normed_mlp)
    grad_middle = grad_out + grad_middle_norm
    mlp_shards = (
        lax.psum_scatter(grad_w_up, ("fsdp", "dp"), scatter_dimension=1, tiled=True),
        lax.psum_scatter(grad_b_up, ("fsdp", "dp"), scatter_dimension=0, tiled=True),
        lax.psum_scatter(grad_w_down, ("fsdp", "dp"), scatter_dimension=1, tiled=True),
        lax.psum_scatter(grad_b_down, ("fsdp", "dp"), scatter_dimension=0, tiled=True),
        lax.psum_scatter(grad_gain_mlp, ("fsdp", "dp"), scatter_dimension=0, tiled=True),
    )
    grad_gate_attn = jnp.sum(grad_middle * branch_attn, axis=1)
    grad_branch_attn = (grad_middle * groups[2][:, None, :]).astype(jnp.bfloat16)
    grad_w_out = jnp.einsum(
        "sqd,sqe->de", attended, grad_branch_attn, preferred_element_type=jnp.float32
    )
    grad_attended = jnp.einsum(
        "sqe,de->sqd", grad_branch_attn, w_out_full, preferred_element_type=jnp.float32
    ).astype(jnp.bfloat16)
    grad_queries, grad_keys_all, grad_values_all = attend_backward(
        queries, keys_all, values_all, grad_attended, log_totals, same_doc
    )
    grad_keys, grad_values = (
        lax.psum_scatter(
            grad_keys_all.astype(jnp.bfloat16), "dp", scatter_dimension=1, tiled=True
        ).astype(jnp.float32),
        lax.psum_scatter(
            grad_values_all.astype(jnp.bfloat16), "dp", scatter_dimension=1, tiled=True
        ).astype(jnp.float32),
    )
    head_shape = (slot_count, quarter, model_width // HEAD, HEAD)
    query_back = rotate(grad_queries.reshape(head_shape), cosine, -sine_table).reshape(tokens.shape)
    key_back = rotate(grad_keys.reshape(head_shape), cosine, -sine_table).reshape(tokens.shape)
    grad_projected = jnp.concatenate([query_back, key_back, grad_values], axis=-1).astype(
        jnp.bfloat16
    )
    grad_w_qkv = jnp.einsum(
        "sqd,sqe->de", normed, grad_projected, preferred_element_type=jnp.float32
    )
    grad_normed = jnp.einsum(
        "sqe,de->sqd", grad_projected, w_qkv_full, preferred_element_type=jnp.float32
    )
    attn_pull = jax.vjp(
        norm_mod,
        tokens.astype(jnp.float32),
        gain_attn_full.astype(jnp.float32),
        groups[0],
        groups[1],
    )[1]
    grad_tokens_norm, grad_gain_attn, grad_shift_attn, grad_scale_attn = attn_pull(grad_normed)
    grad_tokens = (grad_middle + grad_tokens_norm).astype(jnp.bfloat16)
    grad_mod_part = jnp.concatenate(
        [
            grad_shift_attn,
            grad_scale_attn,
            grad_gate_attn,
            grad_shift_mlp,
            grad_scale_mlp,
            grad_gate_mlp,
        ],
        axis=-1,
    )
    grad_modulation = lax.psum(grad_mod_part.astype(jnp.bfloat16), "dp")
    grad_condition = jnp.einsum(
        "se,ce->sc", grad_modulation, w_ada_full, preferred_element_type=jnp.float32
    ).astype(jnp.bfloat16)
    owner_weight = (lax.axis_index("dp") == 0).astype(jnp.float32)
    grad_w_ada = (
        jnp.einsum("sc,se->ce", condition, grad_modulation, preferred_element_type=jnp.float32)
        * owner_weight
    )
    grad_b_ada = jnp.sum(grad_modulation.astype(jnp.float32), axis=0) * owner_weight
    attn_shards = (
        lax.psum_scatter(grad_w_ada, ("fsdp", "dp"), scatter_dimension=1, tiled=True),
        lax.psum_scatter(grad_b_ada, ("fsdp", "dp"), scatter_dimension=0, tiled=True),
        lax.psum_scatter(grad_gain_attn, ("fsdp", "dp"), scatter_dimension=0, tiled=True),
        lax.psum_scatter(grad_w_qkv, ("fsdp", "dp"), scatter_dimension=1, tiled=True),
        lax.psum_scatter(grad_w_out, ("fsdp", "dp"), scatter_dimension=1, tiled=True),
    )
    totals = (
        lax.all_gather(mlp_shards[0].astype(jnp.bfloat16), "dp", axis=1, tiled=True).astype(
            jnp.float32
        ),
        lax.all_gather(mlp_shards[1].astype(jnp.bfloat16), "dp", axis=0, tiled=True).astype(
            jnp.float32
        ),
        lax.all_gather(mlp_shards[2].astype(jnp.bfloat16), "dp", axis=1, tiled=True).astype(
            jnp.float32
        ),
        lax.all_gather(mlp_shards[3].astype(jnp.bfloat16), "dp", axis=0, tiled=True).astype(
            jnp.float32
        ),
        lax.all_gather(mlp_shards[4].astype(jnp.bfloat16), "dp", axis=0, tiled=True).astype(
            jnp.float32
        ),
        lax.all_gather(attn_shards[0].astype(jnp.bfloat16), "dp", axis=1, tiled=True).astype(
            jnp.float32
        ),
        lax.all_gather(attn_shards[1].astype(jnp.bfloat16), "dp", axis=0, tiled=True).astype(
            jnp.float32
        ),
        lax.all_gather(attn_shards[2].astype(jnp.bfloat16), "dp", axis=0, tiled=True).astype(
            jnp.float32
        ),
        lax.all_gather(attn_shards[3].astype(jnp.bfloat16), "dp", axis=1, tiled=True).astype(
            jnp.float32
        ),
        lax.all_gather(attn_shards[4].astype(jnp.bfloat16), "dp", axis=1, tiled=True).astype(
            jnp.float32
        ),
    )
    return (
        outputs,
        grad_tokens,
        grad_condition,
        totals[5],
        totals[6],
        totals[7],
        totals[8],
        totals[9],
        totals[4],
        totals[0],
        totals[1],
        totals[2],
        totals[3],
    )


def solution(mesh):
    return jax.shard_map(
        shards,
        mesh=mesh,
        in_specs=(
            P("fsdp", "dp", None),
            P("fsdp", None),
            P("fsdp", None),
            P(None, "fsdp"),
            P("fsdp"),
            P("fsdp"),
            P(None, "fsdp"),
            P(None, "fsdp"),
            P("fsdp"),
            P(None, "fsdp"),
            P("fsdp"),
            P(None, "fsdp"),
            P("fsdp"),
            P("fsdp", "dp", None),
        ),
        out_specs=(
            P("fsdp", "dp", None),
            P("fsdp", "dp", None),
            P("fsdp", None),
            P(None, "fsdp"),
            P("fsdp"),
            P("fsdp"),
            P(None, "fsdp"),
            P(None, "fsdp"),
            P("fsdp"),
            P(None, "fsdp"),
            P("fsdp"),
            P(None, "fsdp"),
            P("fsdp"),
        ),
        check_vma=False,
    )
```

profile of v0, /device:TPU:1, one launch (start us, length us, event | category | flops | bytes accessed | tf_op | source)
XLA Modules:
  0.0 1243.4 jit_solution(4368432708855261143)
XLA Ops:
  14.7 32.1 %all-reduce.16 = (bf16[4608]{0:T(1024)(128)(2,1)S(1)}, bf16[768]{0:T(1024)(128)(2,1)S(1)}, bf16[768]{0:T(1024)(128)(2,1)}, bf16[768]{0:T(1024)(128)(2,1)}) all-reduce(bf16[4608]{0:T(1024)(128)(2,1)S(1)} %dynamic-update-slice, bf16[768]{0:T(1024)(128)(2,1)S(1)} %dynamic-update-slice.1, ...), channel_id=1, replica_groups=mesh['fsdp'=8,'dp'=4] {'fsdp'}, use_global_device_ids=true, to_apply=%add.1 | all-reduce | flops 6912 | bytes 27648
  54.8 64.1 %all-gather.11.cloned.1.call-done = bf16[768,2304]{0,1:T(8,128)(2,1)} async-done(((bf16[768,288]{0,1:T(8,128)(2,1)}), bf16[768,2304]{0,1:T(8,128)(2,1)}) %all-gather.11.cloned.1.call-update) | async-done | bytes 3538960 | tf_op jit(solution)/shard_map/all_gather | solution.py:232
  144.2 21.3 %all-gather = bf16[8,1,384]{2,1,0:T(2,128)(2,1)S(1)} all-gather(bf16[1,1,384]{2,1,0:T(2,128)(2,1)S(1)} %reshape.237), channel_id=1, replica_groups=mesh['fsdp'=8,'dp'=4] {'fsdp'}, dimensions={0}, use_global_device_ids=true | all-gather | bytes 6912 | tf_op jit(solution)/shard_map/all_gather | solution.py:237
  167.3 5.2 copy.82
  172.4 13.4 %all-gather.13.cloned.1.call-done = bf16[2,1024,768]{1,2,0:T(8,128)(2,1)} async-done(((bf16[2,256,768]{1,2,0:T(8,128)(2,1)}), bf16[2,1024,768]{1,2,0:T(8,128)(2,1)}) %all-gather.13.cloned.1.call-update) | async-done | bytes 3145744 | tf_op jit(solution)/shard_map/all_gather | solution.py:244
  185.8 49.9 %while.49 = (s32[]{:T(128)}, bf16[2,256,768]{1,2,0:T(8,128)(2,1)S(1)}, f32[2,256,12]{1,0,2:T(2,128)}, bf16[2,256,768]{1,2,0:T(8,128)(2,1)S(1)}, bf16[2,1024,768]...) while((s32[]{:T(128)}, ...), condition=%wide.region_13.14_spmd.clone, body=%wide.region_10.13_spmd.clone.sunk | while | flops 138935808 | bytes 7041199 | solution.py:118
  240.4 69.4 %all-gather.19.cloned.1.call-done = bf16[768,3072]{1,0:T(8,128)(2,1)} async-done(((bf16[768,384]{1,0:T(8,128)(2,1)}), bf16[768,3072]{1,0:T(8,128)(2,1)}) %all-gather.19.cloned.1.call-update) | async-done | bytes 4718608 | tf_op jit(solution)/shard_map/all_gather | solution.py:236
  309.8 7.0 fusion.93
  316.8 72.7 %all-gather.21.cloned.1.call-done = bf16[3072,768]{0,1:T(8,128)(2,1)} async-done(((bf16[3072,96]{0,1:T(8,128)(2,1)}), bf16[3072,768]{0,1:T(8,128)(2,1)}) %all-gather.21.cloned.1.call-update) | async-done | bytes 4718608 | tf_op jit(solution)/shard_map/all_gather | solution.py:238
  389.5 9.2 convert_reduce_fusion
  414.4 120.9 %while.50 = (s32[]{:T(128)}, f32[2,256,768]{1,2,0:T(8,128)}, bf16[2,1024,768]{1,2,0:T(8,128)(2,1)}, bf16[2,1024,768]{1,2,0:T(8,128)(2,1)}, bf16[2,256,768]{1,2,0...) while((s32[]{:T(128)}, f32[2,256,768]{1,2,0:T(8,128)}, ...), condition=%wide.region_20.21_spmd.clone, body=%wide.region_18.20_spmd.clone.sunk | while | flops 340950528 | bytes 17982664 | solution.py:168
  545.3 8.2 fusion.118
  553.6 18.9 %reduce-scatter.8.cloned.1.call-done = bf16[2,256,768]{1,2,0:T(8,128)(2,1)} async-done(((bf16[2,1024,768]{1,2,0:T(8,128)(2,1)}), bf16[2,256,768]{1,2,0:T(8,128)(2,1)}) %reduce-scatter.8.cloned.1.call-update) | async-done | bytes 786448 | tf_op jit(solution)/shard_map/reduce_scatter | solution.py:318
  579.2 34.0 %reduce-scatter.10.cloned.1.call-done = bf16[2,256,768]{2,1,0:T(8,128)(2,1)} async-done(((bf16[2,1024,768]{2,1,0:T(8,128)(2,1)}), bf16[2,256,768]{2,1,0:T(8,128)(2,1)}) %reduce-scatter.10.cloned.1.call-update) | async-done | bytes 786448 | tf_op jit(solution)/shard_map/reduce_scatter | solution.py:321
  613.2 5.0 fusion.120
  621.7 10.8 psum.7
  634.6 9.6 convolution_bitcast_fusion.1
  644.3 8.4 convolution_bitcast_fusion.2
  654.3 5.2 convolution_bitcast_fusion
  662.7 53.5 %while.48 = (s32[]{:T(128)}, bf16[2,256,768]{1,2,0:T(8,128)(2,1)S(1)}, bf16[2,256,768]{1,2,0:T(8,128)(2,1)}, bf16[2,1024,768]{1,2,0:T(8,128)(2,1)}, bf16[2,1024,...) while((s32[]{:T(128)}, ...), condition=%wide.region_7.8_spmd.clone, body=%wide.region_4.0_spmd.clone.sunk | while | flops 207096320 | bytes 1076379 | solution.py:118
  718.7 10.4 add_convert_fusion.2
  729.9 5.7 all_gather.94
  736.5 40.9 %all-reduce.15 = (bf16[4608]{0:T(1024)(128)(2,1)S(1)}, bf16[768]{0:T(1024)(128)(2,1)S(1)}, bf16[768]{0:T(1024)(128)(2,1)S(1)}, bf16[3072]{0:T(1024)(128)(2,1)S(1)}, bf16[768]{0:T(1024)(128)(2,1)S(1)}) all-reduce(f32[4608]{0:T(1024)S(1)} %broadcast_multiply_fusion, ...), channel_id=5, replica_groups=mesh['fsdp'=8,'dp'=4] {'fsdp','dp'}, use_global_device_ids=true, to_apply=%region_34.35.clone | all-reduce | flops 9984 | bytes 59904
  778.8 6.2 all-reduce.17
  788.5 31.8 %reduce-scatter.12.cloned.1.call-done = f32[128,144]{0,1:T(8,128)} async-done(((f32[128,4608]{0,1:T(8,128)}), f32[128,144]{0,1:T(8,128)}) %reduce-scatter.12.cloned.1.call-update) | async-done | bytes 73744 | tf_op jit(solution)/shard_map/reduce_scatter | solution.py:368
  821.2 7.6 all_gather.90
  829.5 130.8 %reduce-scatter.20.cloned.1.call-done = f32[3072,24]{0,1:T(8,128)} async-done(((f32[3072,768]{0,1:T(8,128)}), f32[3072,24]{0,1:T(8,128)}) %reduce-scatter.20.cloned.1.call-update) | async-done | bytes 294928 | tf_op jit(solution)/shard_map/reduce_scatter | solution.py:302
  961.3 10.0 all_gather.98
  972.4 129.6 %reduce-scatter.18.cloned.1.call-done = f32[768,96]{0,1:T(8,128)} async-done(((f32[768,3072]{0,1:T(8,128)}), f32[768,96]{0,1:T(8,128)}) %reduce-scatter.18.cloned.1.call-update) | async-done | bytes 294928 | tf_op jit(solution)/shard_map/reduce_scatter | solution.py:300
  1102.9 9.6 all_gather.96
  1113.8 112.0 %reduce-scatter.14.cloned.1.call-done = f32[768,72]{0,1:T(8,128)} async-done(((f32[768,2304]{0,1:T(8,128)}), f32[768,72]{0,1:T(8,128)}) %reduce-scatter.14.cloned.1.call-update) | async-done | bytes 221200 | tf_op jit(solution)/shard_map/reduce_scatter | solution.py:371
  1226.7 8.7 all_gather.93
  (394 shorter events, 326.4 us)
Async XLA Ops:
  7.2 45.3 %copy-start = (bf16[2,128]{1,0:T(2,128)(2,1)S(1)}, bf16[2,128]{1,0:T(2,128)(2,1)}, u32[]{:S(2)}) copy-start(bf16[2,128]{1,0:T(2,128)(2,1)} %param.21) | copy-start | bytes 1540
  7.2 111.7 %copy-start.1 = (bf16[2,256,768]{2,1,0:T(8,128)(2,1)S(1)}, bf16[2,256,768]{2,1,0:T(8,128)(2,1)}, u32[]{:S(2)}) copy-start(bf16[2,256,768]{2,1,0:T(8,128)(2,1)} %param.20) | copy-start | bytes 2359300
  7.2 45.3 %all-gather.9.cloned.1.call-start = ((), (), s32[]{:S(2)}) async-start(), calls=%async_computation.7 | async-start | bytes 1327104 | tf_op jit(solution)/shard_map/all_gather | solution.py:229
  7.9 110.9 %all-gather.11.cloned.1.call-start = ((), (), s32[]{:S(2)}) async-start(), calls=%async_computation.8 | async-start | bytes 3981312 | tf_op jit(solution)/shard_map/all_gather | solution.py:232
  8.7 158.6 %all-gather.15.cloned.1.call-start = ((), (), s32[]{:S(2)}) async-start(), calls=%async_computation.10 | async-start | bytes 3932160 | tf_op jit(solution)/shard_map/all_gather | solution.py:245
  46.7 76.3 %copy-start.24 = (f32[768]{0:T(1024)}, f32[768]{0:T(1024)S(1)}, u32[]{:S(2)}) copy-start(f32[768]{0:T(1024)S(1)} %convert_element_type.204) | copy-start | bytes 9220
  48.1 75.0 %copy-start.26 = (f32[2,256]{1,0:T(2,128)}, f32[2,256]{1,0:T(2,128)S(1)}, u32[]{:S(2)}) copy-start(f32[2,256]{1,0:T(2,128)S(1)} %broadcast_multiply_fusion.3) | copy-start | bytes 6148
  50.2 72.9 %copy-start.32 = (f32[2,256]{1,0:T(2,128)}, f32[2,256]{1,0:T(2,128)S(1)}, u32[]{:S(2)}) copy-start(f32[2,256]{1,0:T(2,128)S(1)} %fusion.152) | copy-start | bytes 6148
  54.8 68.4 %copy-start.22 = (f32[2,768]{1,0:T(2,128)}, f32[2,768]{1,0:T(2,128)S(1)}, u32[]{:S(2)}) copy-start(f32[2,768]{1,0:T(2,128)S(1)} %get-tuple-element.749) | copy-start | bytes 18436
  54.8 68.4 %copy-start.37 = (f32[2,768]{1,0:T(2,128)}, f32[2,768]{1,0:T(2,128)S(1)}, u32[]{:S(2)}) copy-start(f32[2,768]{1,0:T(2,128)S(1)} %get-tuple-element.748) | copy-start | bytes 18436
  126.2 59.6 %all-gather.13.cloned.1.call-start = ((), (), s32[]{:S(2)}) async-start(), calls=%async_computation.9 | async-start | bytes 3932160 | tf_op jit(solution)/shard_map/all_gather | solution.py:244
  141.4 94.3 %all-gather.17.cloned.1.call-start = ((), (), s32[]{:S(2)}) async-start(), calls=%async_computation.11 | async-start | bytes 1327104 | tf_op jit(solution)/shard_map/all_gather | solution.py:233
  142.0 167.8 %all-gather.19.cloned.1.call-start = ((), (), s32[]{:S(2)}) async-start(), calls=%async_computation.12 | async-start | bytes 5308416 | tf_op jit(solution)/shard_map/all_gather | solution.py:236
  142.6 246.9 %all-gather.21.cloned.1.call-start = ((), (), s32[]{:S(2)}) async-start(), calls=%async_computation.13 | async-start | bytes 5308416 | tf_op jit(solution)/shard_map/all_gather | solution.py:238
  143.3 429.2 %reduce-scatter.8.cloned.1.call-start = ((), (), s32[]{:S(2)}) async-start(), calls=%async_computation.14 | async-start | bytes 3932160 | tf_op jit(solution)/shard_map/reduce_scatter | solution.py:318
  185.8 50.8 %copy-start.21 = (f32[2,768]{1,0:T(2,128)S(1)}, f32[2,768]{1,0:T(2,128)}, u32[]{:S(2)}) copy-start(f32[2,768]{1,0:T(2,128)} %get-tuple-element.750) | copy-start | bytes 18436
  236.6 73.2 %copy-start.28 = (f32[2,768]{1,0:T(2,128)S(1)}, f32[2,768]{1,0:T(2,128)}, u32[]{:S(2)}) copy-start(f32[2,768]{1,0:T(2,128)} %get-tuple-element.747) | copy-start | bytes 18436
  236.6 73.2 %copy-start.34 = (f32[768]{0:T(1024)S(1)}, f32[768]{0:T(1024)}, u32[]{:S(2)}) copy-start(f32[768]{0:T(1024)} %convert_element_type.210) | copy-start | bytes 9220
  236.6 73.2 %copy-start.36 = (f32[2,768]{1,0:T(2,128)S(1)}, f32[2,768]{1,0:T(2,128)}, u32[]{:S(2)}) copy-start(f32[2,768]{1,0:T(2,128)} %get-tuple-element.746) | copy-start | bytes 18436
  309.8 79.7 %copy-start.29 = (f32[2,768]{1,0:T(2,128)S(1)}, f32[2,768]{1,0:T(2,128)}, u32[]{:S(2)}) copy-start(f32[2,768]{1,0:T(2,128)} %get-tuple-element.745) | copy-start | bytes 18436
  309.8 79.7 %copy-start.35 = (f32[8,1,384]{2,1,0:T(1,128)S(1)}, f32[8,1,384]{2,1,0:T(1,128)}, u32[]{:S(2)}) copy-start(f32[8,1,384]{2,1,0:T(1,128)} %convert_element_type.252) | copy-start | bytes 36868
  535.3 77.9 %reduce-scatter.10.cloned.1.call-start = ((), (), s32[]{:S(2)}) async-start(), calls=%async_computation.15 | async-start | bytes 3932160 | tf_op jit(solution)/shard_map/reduce_scatter | solution.py:321
  540.1 189.0 %reduce-scatter.16.cloned.1.call-start = ((), (), s32[]{:S(2)}) async-start(), calls=%async_computation.18 | async-start | bytes 2433024 | tf_op jit(solution)/shard_map/reduce_scatter | solution.py:372
  544.2 276.2 %reduce-scatter.12.cloned.1.call-start = ((), (), s32[]{:S(2)}) async-start(), calls=%async_computation.16 | async-start | bytes 2433024 | tf_op jit(solution)/shard_map/reduce_scatter | solution.py:368
  575.7 37.5 %copy-start.25 = (f32[768]{0:T(1024)S(1)}, f32[768]{0:T(1024)}, u32[]{:S(2)}) copy-start(f32[768]{0:T(1024)} %copy-done.24) | copy-start | bytes 9220
  575.7 37.5 %copy-start.27 = (f32[2,256]{1,0:T(2,128)S(1)}, f32[2,256]{1,0:T(2,128)}, u32[]{:S(2)}) copy-start(f32[2,256]{1,0:T(2,128)} %copy-done.26) | copy-start | bytes 6148
  579.2 39.0 %copy-start.31 = (f32[2,256]{1,0:T(2,128)S(1)}, f32[2,256]{1,0:T(2,128)}, u32[]{:S(2)}) copy-start(f32[2,256]{1,0:T(2,128)} %copy-done.30) | copy-start | bytes 6148
  579.2 39.1 %copy-start.33 = (f32[2,256]{1,0:T(2,128)S(1)}, f32[2,256]{1,0:T(2,128)}, u32[]{:S(2)}) copy-start(f32[2,256]{1,0:T(2,128)} %copy-done.32) | copy-start | bytes 6148
  634.5 325.7 %reduce-scatter.20.cloned.1.call-start = ((), (), s32[]{:S(2)}) async-start(), calls=%async_computation.20 | async-start | bytes 9732096 | tf_op jit(solution)/shard_map/reduce_scatter | solution.py:302
  644.2 457.7 %reduce-scatter.18.cloned.1.call-start = ((), (), s32[]{:S(2)}) async-start(), calls=%async_computation.19 | async-start | bytes 9732096 | tf_op jit(solution)/shard_map/reduce_scatter | solution.py:300
  652.7 573.0 %reduce-scatter.14.cloned.1.call-start = ((), (), s32[]{:S(2)}) async-start(), calls=%async_computation.17 | async-start | bytes 7299072 | tf_op jit(solution)/shard_map/reduce_scatter | solution.py:371
  718.7 69.1 %copy-start.6 = (bf16[128,4608]{0,1:T(8,128)(2,1)S(1)}, bf16[128,4608]{0,1:T(8,128)(2,1)}, u32[]{:S(2)}) copy-start(bf16[128,4608]{0,1:T(8,128)(2,1)} %all-gather.9.cloned.1.call-done) | copy-start | bytes 3538948
  (28 other events, 158.7 us)
Sparse Core Ops, SparseCore 0:
  10.2 42.1 all-gather.8
  54.6 64.1 all-gather.10
  126.4 28.4 all-gather.14
  156.8 28.9 all-gather.12
  187.8 39.4 all-gather.16
  229.3 80.4 all-gather.18
  312.0 77.5 all-gather.20
  535.4 37.0 reduce-scatter.7
  575.2 37.9 reduce-scatter.9
  618.3 97.4 reduce-scatter.15
  722.0 98.2 reduce-scatter.11
  826.1 134.1 reduce-scatter.19
  967.2 134.6 reduce-scatter.17
  1107.4 118.2 reduce-scatter.13
where the time goes:
time: 1250 us; the launch traced here: 1240 us
  waiting for transfers between devices  682 us (55%)
  matrix products  285 us (23%)
  blocking collectives  153 us (12%)
  local copies, waits for them, and re-layouts  57.6 us (5%)
  other arithmetic  46.2 us (4%)
  between operations  18.2 us (1%)
    reduce_scatter x1, waiting for transfers between devices, shards(): lax.psum_scatter(grad_w_down, ('fsdp', 'dp'), scatter_dimension=1, tiled=...  131 us
    reduce_scatter x1, waiting for transfers between devices, shards(): lax.psum_scatter(grad_w_up, ('fsdp', 'dp'), scatter_dimension=1, tiled=True)  130 us
    reduce_scatter x1, waiting for transfers between devices, shards(): lax.psum_scatter(grad_w_qkv, ('fsdp', 'dp'), scatter_dimension=1, tiled=T...  112 us
    unnamed x3, blocking collectives  79.2 us
    all_gather x1, waiting for transfers between devices, shards(): lax.all_gather(w_down, 'fsdp', axis=1, tiled=True)  72.7 us
    all_gather x1, waiting for transfers between devices, shards(): lax.all_gather(w_up, 'fsdp', axis=1, tiled=True)  69.4 us
    all_gather x1, waiting for transfers between devices, shards(): lax.all_gather(w_qkv, 'fsdp', axis=1, tiled=True)  64.1 us
    dot_general x24, matrix products, one_head(): jnp.einsum('sqk,skd->sqd', weights_low, value_head, preferred_element_typ...  48.4 us
  transfers between devices with their start and end apart: 14, of which 11 were waited for; matrix products, arithmetic and copies ran while one was open for 18% of the time, Pallas kernels for 0%

commit v1 on v0

v1 whole, which is shorter than its diff:
```python
import functools
import math

import jax
import jax.numpy as jnp
import numpy as np
from jax import lax
from jax.experimental import pallas as pl
from jax.experimental.pallas import tpu as pltpu
from jax.sharding import PartitionSpec as P

HEAD = 64
EPS = 1e-05
ROPE_BASE = 10000.0
MASKED = -1e30
F32 = jnp.float32
BF16 = jnp.bfloat16

NN = (((1,), (0,)), ((), ()))
NT = (((1,), (1,)), ((), ()))
TN = (((0,), (0,)), ((), ()))


def mm(a, b, dims):
    return lax.dot_general(a, b, dims, preferred_element_type=F32)


def rope_table(length):
    inverse = ROPE_BASE ** (-2.0 * np.arange(HEAD // 2) / HEAD)
    angles = np.arange(length)[:, None] * inverse[None, :]
    cosine = np.concatenate([np.cos(angles)] * 2, axis=1)
    sine = np.concatenate([-np.sin(angles), np.sin(angles)], axis=1)
    return cosine.astype(np.float32), sine.astype(np.float32)


def swap_halves(v):
    half = HEAD // 2
    return jnp.concatenate([v[..., half:], v[..., :half]], axis=-1)


def key_window(segments_row, own_row, tile):
    first = jnp.min(own_row)
    last = jnp.max(own_row)
    low = jnp.sum((segments_row < first).astype(jnp.int32))
    high = jnp.sum((segments_row <= last).astype(jnp.int32)) - 1
    start = low // tile
    return start, high // tile - start + 1


def as_column(row):
    size = row.shape[1]
    return jnp.transpose(jnp.broadcast_to(row, (128, size)))[:, :1]


def attend_kernel(tile, seg_ref, qkv_ref, out_ref, log_ref):
    length = seg_ref.shape[2]
    part = qkv_ref.shape[2] // 3
    heads = part // HEAD
    rows = pl.ds(pl.multiple_of(pl.program_id(1) * tile, tile), tile)
    own_row = seg_ref[0, :, rows]
    start, width = key_window(seg_ref[0], own_row, tile)
    own_col = as_column(own_row)
    keys = pl.multiple_of(start * tile, tile)
    for w in range(1, length // tile + 1):

        @pl.when(width == w)
        def _(w=w):
            cols = pl.ds(keys, w * tile)
            same = own_col == seg_ref[0, :, cols]
            for h in range(heads):
                at = h * HEAD
                q = qkv_ref[0, rows, at : at + HEAD]
                k = qkv_ref[0, cols, part + at : part + at + HEAD]
                v = qkv_ref[0, cols, 2 * part + at : 2 * part + at + HEAD]
                scores = jnp.where(same, mm(q, k, NT), MASKED)
                largest = jnp.max(scores, axis=1, keepdims=True)
                weights = jnp.exp(scores - largest)
                total = jnp.sum(weights, axis=1, keepdims=True)
                result = mm(weights.astype(BF16), v, NN) / total
                out_ref[0, :, at : at + HEAD] = result.astype(BF16)
                log_ref[0, :, h : h + 1] = largest + jnp.log(total)


def attend(segments, qkv, tile):
    slots, length, wide = qkv.shape
    part = wide // 3
    return pl.pallas_call(
        functools.partial(attend_kernel, tile),
        grid=(slots, length // tile),
        out_shape=(
            jax.ShapeDtypeStruct((slots, length, part), BF16),
            jax.ShapeDtypeStruct((slots, length, 128), F32),
        ),
        in_specs=[
            pl.BlockSpec((1, 1, length), lambda s, b: (s, 0, 0)),
            pl.BlockSpec((1, length, wide), lambda s, b: (s, 0, 0)),
        ],
        out_specs=(
            pl.BlockSpec((1, tile, part), lambda s, b: (s, b, 0)),
            pl.BlockSpec((1, tile, 128), lambda s, b: (s, b, 0)),
        ),
        compiler_params=pltpu.CompilerParams(vmem_limit_bytes=48 << 20),
        name="attend",
    )(segments[:, None, :], qkv)


def attend_back_kernel(
    tile, seg_ref, qkv_ref, grad_ref, out_ref, log_ref, cos_ref, sin_ref, back_ref, dk_ref, dv_ref
):
    length = seg_ref.shape[2]
    part = qkv_ref.shape[2] // 3
    heads = part // HEAD
    step = pl.program_id(1)
    rows = pl.ds(pl.multiple_of(step * tile, tile), tile)
    own_row = seg_ref[0, :, rows]
    start, width = key_window(seg_ref[0], own_row, tile)
    own_col = as_column(own_row)
    keys = pl.multiple_of(start * tile, tile)
    scale = 1.0 / math.sqrt(HEAD)

    @pl.when(step == 0)
    def _():
        dk_ref[...] = jnp.zeros_like(dk_ref)
        dv_ref[...] = jnp.zeros_like(dv_ref)

    for w in range(1, length // tile + 1):

        @pl.when(width == w)
        def _(w=w):
            cols = pl.ds(keys, w * tile)
            same = own_col == seg_ref[0, :, cols]
            cosine = cos_ref[rows, :]
            sine = sin_ref[rows, :]
            for h in range(heads):
                at = h * HEAD
                q = qkv_ref[0, rows, at : at + HEAD]
                k = qkv_ref[0, cols, part + at : part + at + HEAD]
                v = qkv_ref[0, cols, 2 * part + at : 2 * part + at + HEAD]
                g = grad_ref[0, :, at : at + HEAD]
                o = out_ref[0, :, at : at + HEAD]
                inner = jnp.sum(g.astype(F32) * o.astype(F32), axis=1, keepdims=True)
                scores = jnp.where(same, mm(q, k, NT), MASKED)
                weights = jnp.exp(scores - log_ref[0, :, h : h + 1])
                dots = mm(g, v, NT)
                dscores = (weights * (dots - inner)).astype(BF16)
                dq = mm(dscores, k, NN) * scale
                back_ref[0, rows, at : at + HEAD] = (dq * cosine - swap_halves(dq) * sine).astype(BF16)
                dk_ref[cols, at : at + HEAD] += mm(dscores, q, TN)
                dv_ref[cols, at : at + HEAD] += mm(weights.astype(BF16), g, TN)

    @pl.when(step == pl.num_programs(1) - 1)
    def _():
        cosine = cos_ref[...]
        sine = sin_ref[...]
        for h in range(heads):
            at = h * HEAD
            dk = dk_ref[:, at : at + HEAD]
            back_ref[0, :, part + at : part + at + HEAD] = (
                dk * cosine - swap_halves(dk) * sine
            ).astype(BF16)
        back_ref[0, :, 2 * part :] = dv_ref[...].astype(BF16)


def attend_back(segments, qkv, grad, out, log, cosine, sine, tile):
    slots, length, wide = qkv.shape
    part = wide // 3
    whole = lambda s, b: (s, 0, 0)
    step = lambda s, b: (s, b, 0)
    table = lambda s, b: (0, 0)
    return pl.pallas_call(
        functools.partial(attend_back_kernel, tile),
        grid=(slots, length // tile),
        out_shape=jax.ShapeDtypeStruct((slots, length, wide), BF16),
        in_specs=[
            pl.BlockSpec((1, 1, length), whole),
            pl.BlockSpec((1, length, wide), whole),
            pl.BlockSpec((1, tile, part), step),
            pl.BlockSpec((1, tile, part), step),
            pl.BlockSpec((1, tile, 128), step),
            pl.BlockSpec((length, HEAD), table),
            pl.BlockSpec((length, HEAD), table),
        ],
        out_specs=pl.BlockSpec((1, length, wide), whole),
        scratch_shapes=[pltpu.VMEM((length, part), F32)] * 2,
        compiler_params=pltpu.CompilerParams(vmem_limit_bytes=48 << 20),
        name="attend_back",
    )(segments[:, None, :], qkv, grad, out, log, cosine, sine)


def norm_parts(stream):
    average = jnp.mean(stream, axis=-1, keepdims=True)
    centered = stream - average
    variance = jnp.mean(centered * centered, axis=-1, keepdims=True)
    inverse = lax.rsqrt(variance + EPS)
    return centered * inverse, inverse


def norm_back(grad, normal, inverse, factor):
    e = grad * factor
    mean_e = jnp.mean(e, axis=-1, keepdims=True)
    mean_en = jnp.mean(e * normal, axis=-1, keepdims=True)
    return inverse * (e - mean_e - normal * mean_en)


def column_plan(shards_n, ranks, columns):
    per = columns // shards_n
    rank_of = (np.arange(columns) // HEAD) % ranks
    lists = [
        [[c for c in range(per) if rank_of[f * per + c] == r] for r in range(ranks)]
        for f in range(shards_n)
    ]
    most = max(len(l) for row in lists for l in row)
    most = -(-most // 16) * 16
    take = np.full((shards_n, ranks, most), -1, np.int32)
    place = np.full((ranks, shards_n * most), -1, np.int32)
    home = np.full((shards_n, ranks * most), -1, np.int32)
    for r in range(ranks):
        order = {c: i for i, c in enumerate(np.flatnonzero(rank_of == r))}
        for f in range(shards_n):
            for i, c in enumerate(lists[f][r]):
                take[f, r, i] = c
                place[r, f * most + i] = order[f * per + c]
                home[f, r * most + i] = c
    return most, take, place, home


def pick(indices, size):
    return (indices[:, None] == jnp.arange(size, dtype=jnp.int32)[None, :]).astype(BF16)


def shards(
    tokens,
    condition,
    segments,
    w_ada,
    b_ada,
    gain_attn,
    w_qkv,
    w_out,
    gain_mlp,
    w_up,
    b_up,
    w_down,
    b_down,
    cotangent,
):
    slots, quarter, width = tokens.shape
    length = segments.shape[1]
    n = lax.axis_size("fsdp")
    m = lax.axis_size("dp")
    f = lax.axis_index("fsdp")
    d = lax.axis_index("dp")
    heads = width // HEAD
    part = width // m
    hidden_part = w_up.shape[1] * n // m
    tile = 256
    cos_np, sin_np = rope_table(length)
    cosine, sine = jnp.asarray(cos_np), jnp.asarray(sin_np)

    cond_all = lax.all_gather(condition, "fsdp", axis=0, tiled=True)
    mod_cols = mm(cond_all, w_ada, NN) + b_ada.astype(F32)
    modulation = lax.all_to_all(mod_cols, "fsdp", 0, 1, tiled=True)
    shift_attn, scale_attn, gate_attn, shift_mlp, scale_mlp, gate_mlp = [
        g[:, None, :] for g in jnp.split(modulation, 6, axis=-1)
    ]
    own_vec = jnp.concatenate([b_up, gain_attn, gain_mlp, b_down])[None]
    vecs = lax.all_gather(own_vec, "fsdp", axis=0, tiled=True).astype(F32)
    ups = b_up.shape[0]
    small = gain_attn.shape[0]
    b_up_all = vecs[:, :ups].reshape(n, m, ups // m)
    b_up_rank = lax.dynamic_index_in_dim(b_up_all, d, 1, False).reshape(-1)
    gain_attn_all = vecs[:, ups : ups + small].reshape(-1)
    gain_mlp_all = vecs[:, ups + small : ups + 2 * small].reshape(-1)
    b_down_all = vecs[:, ups + 2 * small :].reshape(-1)

    most, take, place, home = column_plan(n, m, w_qkv.shape[1] * n)
    picked = pick(jnp.asarray(take)[f, d], w_qkv.shape[1])
    qkv_rows = mm(picked, w_qkv, NT).astype(BF16)
    up_rows = lax.dynamic_slice_in_dim(w_up, d * (ups // m), ups // m, 1).T
    down_rows = lax.dynamic_index_in_dim(
        w_down.reshape(n, m, ups // m, small), d, 1, False
    ).reshape(-1, small).T
    out_rows = w_out.reshape(heads // m, m, HEAD, small).transpose(1, 0, 2, 3).reshape(-1, small).T
    qkv_packed = lax.all_gather(qkv_rows, "fsdp", axis=0, tiled=True)
    placing = pick(jnp.asarray(place)[d], 3 * part)
    w_qkv_t = mm(placing, qkv_packed, TN).astype(BF16)
    w_out_t = lax.all_gather(out_rows, "fsdp", axis=0, tiled=True)
    w_up_t = lax.all_gather(up_rows, "fsdp", axis=0, tiled=True)
    w_down_t = lax.all_gather(down_rows, "fsdp", axis=0, tiled=True)

    group_tokens = lax.all_gather(tokens, "dp", axis=1, tiled=True)
    normal, _ = norm_parts(group_tokens.astype(F32))
    normed = (normal * (gain_attn_all * (1.0 + scale_attn)) + shift_attn).astype(BF16)
    projected = mm(normed.reshape(-1, width), w_qkv_t, NT).reshape(slots, length, 3 * heads // m, HEAD)
    rot = projected * cosine[:, None, :] + swap_halves(projected) * sine[:, None, :]
    hr = heads // m
    qkv = jnp.concatenate(
        [rot[:, :, :hr] * (1.0 / math.sqrt(HEAD)), rot[:, :, hr : 2 * hr], projected[:, :, 2 * hr :]],
        axis=2,
    ).astype(BF16).reshape(slots, length, 3 * part)

    attended, logs = attend(segments, qkv, tile)

    own = lax.all_to_all(attended, "dp", 1, 2, tiled=True)
    own_tokens = tokens.astype(F32)
    flat = lambda v: v.reshape(-1, v.shape[-1])
    back = lambda v: v.reshape(slots, -1, v.shape[-1])
    branch_attn = back(mm(flat(own), w_out_t, NT))
    middle = own_tokens + gate_attn * branch_attn
    normal_mlp, inverse_mlp = norm_parts(middle)
    normed_mlp = (normal_mlp * (gain_mlp_all * (1.0 + scale_mlp)) + shift_mlp).astype(BF16)
    normed_mlp_all = flat(lax.all_gather(normed_mlp, "dp", axis=1, tiled=True))
    cot_all = lax.all_gather(cotangent, "dp", axis=1, tiled=True)
    gbm = flat((cot_all.astype(F32) * gate_mlp).astype(BF16))
    hidden = mm(normed_mlp_all, w_up_t, NT) + b_up_rank
    activated, gelu_pull = jax.vjp(lambda h: jax.nn.gelu(h, approximate=True), hidden)
    activated = activated.astype(BF16)
    branch_part = back(mm(activated, w_down_t, NT).astype(BF16))
    branch_mlp = lax.psum_scatter(branch_part, "dp", scatter_dimension=1, tiled=True).astype(F32) + b_down_all
    outputs = (middle + gate_mlp * branch_mlp).astype(BF16)
    grad_act = mm(gbm, w_down_t, NN)
    grad_hidden = gelu_pull(grad_act)[0].astype(BF16)
    grad_normed_part = back(mm(grad_hidden, w_up_t, NN).astype(BF16))
    grad_normed_mlp = lax.psum_scatter(
        grad_normed_part, "dp", scatter_dimension=1, tiled=True
    ).astype(F32)
    cot = cotangent.astype(F32)
    own_gbm = (cot * gate_mlp).astype(BF16).astype(F32)
    grad_middle = cot + norm_back(
        grad_normed_mlp, normal_mlp, inverse_mlp, gain_mlp_all * (1.0 + scale_mlp)
    )
    grad_branch_attn = (grad_middle * gate_attn).astype(BF16)
    grad_att_own = back(mm(flat(grad_branch_attn), w_out_t, NN).astype(BF16))
    grad_attended = lax.all_to_all(grad_att_own, "dp", 2, 1, tiled=True)

    dw_down_t = mm(gbm, activated, TN).astype(BF16)
    dw_up_t = mm(grad_hidden, normed_mlp_all, TN).astype(BF16)
    dw_out_t = mm(flat(grad_branch_attn), flat(own), TN).astype(BF16)
    db_up = jnp.sum(grad_hidden.astype(F32), axis=0)

    gqkv = attend_back(segments, qkv, grad_attended, attended, logs, cosine, sine, tile)
    gqkv_flat = flat(gqkv)
    dw_qkv_t = mm(gqkv_flat, flat(normed), TN).astype(BF16)
    grad_normed = lax.psum_scatter(
        back(mm(gqkv_flat, w_qkv_t, NN).astype(BF16)), "dp", scatter_dimension=1, tiled=True
    ).astype(F32)
    normal_attn, inverse_attn = norm_parts(own_tokens)
    d_tokens = (
        grad_middle
        + norm_back(grad_normed, normal_attn, inverse_attn, gain_attn_all * (1.0 + scale_attn))
    ).astype(BF16)

    sum_attn = jnp.sum(grad_normed * normal_attn, axis=1)
    sum_mlp = jnp.sum(grad_normed_mlp * normal_mlp, axis=1)
    sums = jnp.concatenate(
        [
            jnp.sum(grad_normed, axis=1),
            sum_attn,
            jnp.sum(grad_middle * branch_attn, axis=1),
            jnp.sum(grad_normed_mlp, axis=1),
            sum_mlp,
            jnp.sum(cot * branch_mlp, axis=1),
            jnp.sum(own_gbm, axis=1),
        ],
        axis=-1,
    )
    sums = lax.psum(sums, "dp")
    sh_a, sc_a, ga_a, sh_m, sc_m, ga_m, gb = jnp.split(sums, 7, axis=-1)
    d_gain_attn = jnp.sum(sc_a * (1.0 + scale_attn[:, 0]), axis=0)
    d_gain_mlp = jnp.sum(sc_m * (1.0 + scale_mlp[:, 0]), axis=0)
    d_b_down = jnp.sum(gb, axis=0)
    gmod = jnp.concatenate(
        [sh_a, sc_a * gain_attn_all, ga_a, sh_m, sc_m * gain_mlp_all, ga_m], axis=-1
    ).astype(BF16)
    gmod_cols = lax.all_to_all(gmod, "fsdp", 1, 0, tiled=True)
    d_w_ada = mm(cond_all, gmod_cols, TN)
    d_b_ada = jnp.sum(gmod_cols.astype(F32), axis=0)
    d_condition = lax.psum_scatter(
        mm(gmod_cols, w_ada, NT), "fsdp", scatter_dimension=0, tiled=True
    ).astype(BF16)
    vec_sums = lax.psum_scatter(
        jnp.stack([d_gain_attn, d_gain_mlp, d_b_down]), "fsdp", scatter_dimension=1, tiled=True
    )

    def scatter(v):
        return lax.psum_scatter(v, "fsdp", scatter_dimension=0, tiled=True)

    def spread(v):
        return lax.all_gather(v, "dp", axis=0)

    up_all = spread(scatter(dw_up_t))
    d_w_up = up_all.reshape(-1, width).astype(F32).T
    down_all = spread(scatter(dw_down_t))
    d_w_down = (
        down_all.reshape(m, small, n, ups // m).transpose(2, 0, 3, 1).reshape(-1, small).astype(F32)
    )
    out_all = lax.psum(scatter(dw_out_t).astype(F32), "dp")
    d_w_out = (
        out_all.reshape(small, m, heads // m, HEAD).transpose(2, 1, 3, 0).reshape(-1, small)
    )
    d_b_up = spread(scatter(db_up)).reshape(-1)
    qkv_all = spread(scatter(mm(placing, dw_qkv_t, NN).astype(BF16)))
    homing = pick(jnp.asarray(home)[f], w_qkv.shape[1])
    d_w_qkv = mm(qkv_all.reshape(-1, width), homing, TN)
    return (
        outputs,
        d_tokens,
        d_condition,
        d_w_ada,
        d_b_ada,
        vec_sums[0],
        d_w_qkv,
        d_w_out,
        vec_sums[1],
        d_w_up,
        d_b_up,
        d_w_down,
        vec_sums[2],
    )


def solution(mesh):
    return jax.shard_map(
        shards,
        mesh=mesh,
        in_specs=(
            P("fsdp", "dp", None),
            P("fsdp", None),
            P("fsdp", None),
            P(None, "fsdp"),
            P("fsdp"),
            P("fsdp"),
            P(None, "fsdp"),
            P(None, "fsdp"),
            P("fsdp"),
            P(None, "fsdp"),
            P("fsdp"),
            P(None, "fsdp"),
            P("fsdp"),
            P("fsdp", "dp", None),
        ),
        out_specs=(
            P("fsdp", "dp", None),
            P("fsdp", "dp", None),
            P("fsdp", None),
            P(None, "fsdp"),
            P("fsdp"),
            P("fsdp"),
            P(None, "fsdp"),
            P(None, "fsdp"),
            P("fsdp"),
            P(None, "fsdp"),
            P("fsdp"),
            P(None, "fsdp"),
            P("fsdp"),
        ),
        check_vma=False,
    )
```

time: 1250 us -> 860 us (0.69)
  matrix products: 285 us -> 74.1 us
  waiting for transfers between devices: 682 us -> 474 us
  Pallas kernels: 0 us -> 46.5 us
  other arithmetic: 46.2 us -> 25.9 us
  starting transfers between devices: 0.56 us -> 15.3 us
    reduce_scatter x7, waiting for transfers between devices: 457 us -> 261 us  [the longest x4 166 us: scatter(): return lax.psum_scatter(v, 'fsdp', scatter_dimension=0, tiled=True)]
    dot_general x113 -> x18, matrix products: 262 us -> 74.1 us  [mm(): return lax.dot_general(a, b, dims, preferred_element_type=F32)]
    all_gather x7, waiting for transfers between devices: 222 us -> 118 us  [the longest x1 37.3 us: shards(): w_up_t = lax.all_gather(up_rows, 'fsdp', axis=0, tiled=True)]
    unnamed x14 -> x17, waiting for transfers between devices: 3.28 us -> 62.5 us
    pallas_call x0 -> x2, Pallas kernels: none -> 46.5 us  [the longest x1 30.2 us: attend_back(): pl.pallas_call(functools.partial(attend_back_kernel, tile), grid=(slots,...]
    sub x12 -> x0, matrix products: 22.9 us -> none  [one_head(): weights = jnp.exp(masked - largest)]
    psum x0 -> x1, waiting for transfers between devices: none -> 20.2 us  [shards(): out_all = lax.psum(scatter(dw_out_t).astype(F32), 'dp')]
    all_gather x6 -> x4, blocking collectives: 62.9 us -> 47.3 us  [the longest x3 29.5 us: spread(): return lax.all_gather(v, 'dp', axis=0)]
  transfers between devices with their start and end apart: 14 -> 19, of which waited for: 11 -> 14; matrix products, arithmetic and copies ran while one was open for 18% -> 14% of each run, Pallas kernels for 0% -> 5%
where the time goes in v1:
time: 860 us; the launch traced here: 849 us
  waiting for transfers between devices  474 us (55%)
  blocking collectives  145 us (17%)
  matrix products  74.1 us (9%)
  local copies, waits for them, and re-layouts  49.6 us (6%)
  Pallas kernels  46.5 us (5%)
  other arithmetic  25.9 us (3%)
  between operations  18 us (2%)
  starting transfers between devices  15.3 us (2%)
    reduce_scatter x4, waiting for transfers between devices, scatter(): return lax.psum_scatter(v, 'fsdp', scatter_dimension=0, tiled=True)  166 us
    dot_general x18, matrix products, mm(): return lax.dot_general(a, b, dims, preferred_element_type=F32)  74.1 us
    unnamed x3, blocking collectives  73.5 us
    unnamed x17, waiting for transfers between devices  62.5 us
    reduce_scatter x1, waiting for transfers between devices, shards(): lax.psum_scatter(branch_part, 'dp', scatter_dimension=1, tiled=True)  38.8 us
    all_gather x1, waiting for transfers between devices, shards(): w_up_t = lax.all_gather(up_rows, 'fsdp', axis=0, tiled=True)  37.3 us
    all_gather x1, waiting for transfers between devices, shards(): w_down_t = lax.all_gather(down_rows, 'fsdp', axis=0, tiled=True)  34.7 us
    all_gather x1, waiting for transfers between devices, shards(): normed_mlp_all = flat(lax.all_gather(normed_mlp, 'dp', axis=1, tiled=True))  31 us
  transfers between devices with their start and end apart: 19, of which 14 were waited for; matrix products, arithmetic and copies ran while one was open for 14% of the time, Pallas kernels for 5%

profile of v1, /device:TPU:1, one launch (start us, length us, event | category | flops | bytes accessed | tf_op | source)
XLA Modules:
  0.0 848.7 jit_solution(14058906675529753911)
XLA Ops:
  13.5 17.8 %all-gather.5 = bf16[8,2,128]{2,1,0:T(2,128)(2,1)S(1)} all-gather(bf16[1,2,128]{2,1,0:T(2,128)(2,1)S(1)} %bitcast.137), channel_id=1, replica_groups=mesh['fsdp'=8,'dp'=4] {'fsdp'}, dimensions={0}, use_global_device_ids=true | all-gather | bytes 4608 | tf_op jit(solution)/shard_map/all_gather | solution.py:260
  38.1 30.2 %all-reduce = bf16[5376]{0:T(1024)(128)(2,1)S(1)} all-reduce(bf16[5376]{0:T(1024)(128)(2,1)S(1)} %dynamic-update-slice), channel_id=2, replica_groups=mesh['fsdp'=8,'dp'=4] {'fsdp'}, use_global_device_ids=true, to_apply=%add | all-reduce | flops 5376 | bytes 21504
  73.0 10.7 %all-gather.14.cloned.1.call-done = bf16[2,1024,768]{2,1,0:T(8,128)(2,1)} async-done(((bf16[2,256,768]{2,1,0:T(8,128)(2,1)}), bf16[2,1024,768]{2,1,0:T(8,128)(2,1)}) %all-gather.14.cloned.1.call-update) | async-done | bytes 3145744 | tf_op jit(solution)/shard_map/all_gather | solution.py:291
  98.4 16.2 %attend.1 = (bf16[2,1024,192]{2,1,0:T(8,128)(2,1)S(1)}, f32[2,1024,128]{2,1,0:T(8,128)S(1)}) custom-call(s32[2,1,1024]{2,1,0:T(1,128)S(1)} %broadcast_in_dim.4.seg_ref, bf16[2,1024,576]{2,1,0:T(8,128)(2,1)S(1)} %copy.109.qkv_ref), custom_call_target="tpu_custom_call" | custom-call | tf_op jit(solution)/shard_map/attend/pallas_call | solution.py:87
  118.7 5.5 all-to-all-start.1
  125.6 12.3 %all-to-all-done.1 = bf16[2,1024,192]{2,0,1:T(2,128)(2,1)} async-done(((bf16[2,1024,192]{2,0,1:T(2,128)(2,1)}), bf16[2,1024,192]{2,0,1:T(2,128)(2,1)}, u32[]{:S(2)}, u32[]{:S(2)}) %all-to-all-start.1) | async-done | bytes 786464 | tf_op jit(solution)/shard_map/all_to_all | solution.py:304
  161.0 37.3 %all-gather.22.cloned.1.call-done = bf16[768,768]{1,0:T(8,128)(2,1)} async-done(((bf16[96,768]{1,0:T(8,128)(2,1)}), bf16[768,768]{1,0:T(8,128)(2,1)}) %all-gather.22.cloned.1.call-update) | async-done | bytes 1179664 | tf_op jit(solution)/shard_map/all_gather | solution.py:288
  198.4 31.0 %all-gather.20.cloned.1.call-done = bf16[2,1024,768]{2,1,0:T(8,128)(2,1)} async-done(((bf16[2,256,768]{2,1,0:T(8,128)(2,1)}), bf16[2,1024,768]{2,1,0:T(8,128)(2,1)}) %all-gather.20.cloned.1.call-update) | async-done | bytes 3145744 | tf_op jit(solution)/shard_map/all_gather | solution.py:312
  229.3 7.5 fusion.67
  236.8 34.7 %all-gather.24.cloned.1.call-done = bf16[768,768]{1,0:T(8,128)(2,1)} async-done(((bf16[96,768]{1,0:T(8,128)(2,1)}), bf16[768,768]{1,0:T(8,128)(2,1)}) %all-gather.24.cloned.1.call-update) | async-done | bytes 1179664 | tf_op jit(solution)/shard_map/all_gather | solution.py:289
  271.5 9.2 %convert_reduce_fusion.1 = (f32[768]{0:T(1024)S(1)}, bf16[2048,768]{1,0:T(8,128)(2,1)S(1)}) fusion(f32[2048,768]{1,0:T(8,128)} %fusion.67, f32[768]{0:T(1024)S(1)} %add.160, bf16[2048,768]{1,0:T(8,128)(2,1)} %bitcast.110, bf16[768,768]{1,0:T(8,128)(2,1)} %all-gather.24.cloned.1.call-done), kind=kOutput, calls=%fused_computation.17 | convolution fusion | flops 2452094208 | bytes 13768704 | tf_op jit(solution)/shard_map/dot_general | solution.py:25
  284.8 8.9 %convolution_convert_fusion.2 = bf16[2048,768]{1,0:T(8,128)(2,1)} fusion(bf16[768,768]{1,0:T(8,128)(2,1)} %all-gather.24.cloned.1.call-done, f32[2048,768]{1,0:T(8,128)} %fusion.67, f32[768]{0:T(1024)S(1)} %add.160), kind=kOutput, calls=%fused_computation.24 | convolution fusion | flops 2433220608 | bytes 10619904 | tf_op jit(solution)/shard_map/dot_general | solution.py:25
  296.3 26.5 %reduce-scatter.13.cloned.1.call-done = bf16[2,256,768]{2,1,0:T(8,128)(2,1)} async-done(((bf16[2,1024,768]{2,1,0:T(8,128)(2,1)}), bf16[2,256,768]{2,1,0:T(8,128)(2,1)}) %reduce-scatter.13.cloned.1.call-update) | async-done | bytes 786448 | tf_op jit(solution)/shard_map/reduce_scatter | solution.py:324
  324.8 38.8 %reduce-scatter.11.cloned.1.call-done = bf16[2,256,768]{2,1,0:T(8,128)(2,1)} async-done(((bf16[2,1024,768]{2,1,0:T(8,128)(2,1)}), bf16[2,256,768]{2,1,0:T(8,128)(2,1)}) %reduce-scatter.11.cloned.1.call-update) | async-done | bytes 786448 | tf_op jit(solution)/shard_map/reduce_scatter | solution.py:319
  370.3 6.7 convolution_convert_fusion.4
  377.1 6.8 convolution_convert_fusion.3
  386.9 13.8 %all_to_all.68 = bf16[2,256,768]{1,0,2:T(2,128)(2,1)S(1)} all-to-all(bf16[2,256,768]{1,0,2:T(2,128)(2,1)S(1)} %copy.119), channel_id=1, replica_groups=mesh['fsdp'=8,'dp'=4] {'dp'}, dimensions={2} | all-to-all | bytes 1572864 | tf_op jit(solution)/shard_map/all_to_all | solution.py:334
  405.3 30.2 %attend_back.1 = bf16[2,1024,576]{2,1,0:T(8,128)(2,1)} custom-call(s32[2,1,1024]{2,1,0:T(1,128)S(1)} %broadcast_in_dim.4.seg_ref, bf16[2,1024,576]{2,1,0:T(8,128)(2,1)} %copy-done.2, bf16[2,1024,192]{2,1,0:T(8,128)(2,1)S(1)} %bitcast.103, bf16[2,1024,192]{2,1,0:T(8,128)(2,1)S(1)} %copy-done.4, f32[2,1024,128]{2,1,0:T(8,128)S(1)} %copy-done.6, ...), custom_call_target="tpu_custom_call" | custom-call | tf_op jit(solution)/shard_map/attend_back/pallas_call | solution.py:170
  437.7 7.9 fusion.44
  454.7 45.1 %reduce-scatter.21.cloned.1.call-done = bf16[96,768]{1,0:T(8,128)(2,1)} async-done(((bf16[768,768]{1,0:T(8,128)(2,1)}), bf16[96,768]{1,0:T(8,128)(2,1)}) %reduce-scatter.21.cloned.1.call-update) | async-done | bytes 147472 | tf_op jit(solution)/shard_map/reduce_scatter | solution.py:386
  499.8 9.8 %all-gather.2 = bf16[384,768]{1,0:T(8,128)(2,1)S(1)} all-gather(bf16[96,768]{1,0:T(8,128)(2,1)} %reduce-scatter.21.cloned.1.call-done), channel_id=4, replica_groups=mesh['fsdp'=8,'dp'=4] {'dp'}, dimensions={0}, use_global_device_ids=true | all-gather | bytes 737280 | tf_op jit(solution)/shard_map/all_gather | solution.py:389
  511.1 55.0 %reduce-scatter.23.cloned.1.call-done = bf16[96,768]{1,0:T(8,128)(2,1)} async-done(((bf16[768,768]{1,0:T(8,128)(2,1)}), bf16[96,768]{1,0:T(8,128)(2,1)}) %reduce-scatter.23.cloned.1.call-update) | async-done | bytes 147472 | tf_op jit(solution)/shard_map/reduce_scatter | solution.py:386
  566.1 9.8 %all-gather.4 = bf16[384,768]{1,0:T(8,128)(2,1)S(1)} all-gather(bf16[96,768]{1,0:T(8,128)(2,1)} %reduce-scatter.23.cloned.1.call-done), channel_id=6, replica_groups=mesh['fsdp'=8,'dp'=4] {'dp'}, dimensions={0}, use_global_device_ids=true | all-gather | bytes 737280 | tf_op jit(solution)/shard_map/all_gather | solution.py:389
  580.4 20.2 %all-reduce.7.cloned.1.call-done = f32[768,96]{1,0:T(8,128)} async-done(((f32[768,96]{1,0:T(8,128)}), f32[768,96]{1,0:T(8,128)}) %all-reduce.7.cloned.1.call-update) | async-done | bytes 294928 | tf_op jit(solution)/shard_map/psum | solution.py:397
  602.5 65.7 %reduce-scatter.17.cloned.1.call-done = bf16[96,768]{1,0:T(8,128)(2,1)} async-done(((bf16[768,768]{1,0:T(8,128)(2,1)}), bf16[96,768]{1,0:T(8,128)(2,1)}) %reduce-scatter.17.cloned.1.call-update) | async-done | bytes 147472 | tf_op jit(solution)/shard_map/reduce_scatter | solution.py:386
  668.2 9.9 %all-gather.1 = bf16[384,768]{1,0:T(8,128)(2,1)S(1)} all-gather(bf16[96,768]{1,0:T(8,128)(2,1)} %reduce-scatter.17.cloned.1.call-done), channel_id=3, replica_groups=mesh['fsdp'=8,'dp'=4] {'dp'}, dimensions={0}, use_global_device_ids=true | all-gather | bytes 737280 | tf_op jit(solution)/shard_map/all_gather | solution.py:389
  679.6 29.8 %reduce-scatter.15.cloned.1.call-done = bf16[2,256,768]{2,1,0:T(8,128)(2,1)} async-done(((bf16[2,1024,768]{2,1,0:T(8,128)(2,1)}), bf16[2,256,768]{2,1,0:T(8,128)(2,1)}) %reduce-scatter.15.cloned.1.call-update) | async-done | bytes 786448 | tf_op jit(solution)/shard_map/reduce_scatter | solution.py:344
  711.4 10.8 %psum.14 = f32[2,5376]{1,0:T(2,128)S(1)} all-reduce(f32[2,5376]{1,0:T(2,128)S(1)} %constant_dynamic-update-slice_fusion), channel_id=1, replica_groups=mesh['fsdp'=8,'dp'=4] {'dp'}, use_global_device_ids=true, to_apply=%region_20.21 | all-reduce | flops 10752 | bytes 86016 | tf_op jit(solution)/shard_map/psum | solution.py:367
  723.2 5.4 all-to-all-start.3
  732.3 61.0 %reduce-scatter.25.cloned.1.call-done = f32[96,3]{1,0:T(8,128)} async-done(((f32[768,3]{1,0:T(8,128)}), f32[96,3]{1,0:T(8,128)}) %reduce-scatter.25.cloned.1.call-update) | async-done | bytes 1168
  797.2 28.2 %all-reduce.4 = (bf16[16,128]{1,0:T(8,128)(2,1)S(1)}, f32[768]{0:T(1024)S(1)}) all-reduce(f32[16,128]{1,0:T(8,128)S(1)} %fusion.68, f32[768]{0:T(1024)S(1)} %get-tuple-element.97), channel_id=10, replica_groups=mesh['fsdp'=8,'dp'=4] {'fsdp'}, use_global_device_ids=true, to_apply=%region_21.22.clone | all-reduce | flops 2816 | bytes 18432
  825.6 15.1 %all-reduce.1 = f32[384]{0:T(512)} all-reduce(f32[384]{0:T(512)S(1)} %dynamic-slice_dynamic-update-slice_fusion), channel_id=5, replica_groups=mesh['fsdp'=8,'dp'=4] {'dp'}, use_global_device_ids=true, to_apply=%add.1 | all-reduce | flops 384 | bytes 3072
  (278 shorter events, 112.8 us)
Async XLA Ops:
  7.3 61.7 %copy-start.43 = (s32[2,1024]{1,0:T(2,128)S(1)}, s32[2,1024]{1,0:T(2,128)}, u32[]{:S(2)}) copy-start(s32[2,1024]{1,0:T(2,128)} %param.21) | copy-start | bytes 24580
  7.3 63.4 %all-gather.16.cloned.1.call-start = ((), (), s32[]{:S(2)}) async-start(), calls=%async_computation.13 | async-start | bytes 1327104 | tf_op jit(solution)/shard_map/all_gather | solution.py:284
  10.1 73.6 %all-gather.14.cloned.1.call-start = ((), (), s32[]{:S(2)}) async-start(), calls=%async_computation.12 | async-start | bytes 3932160 | tf_op jit(solution)/shard_map/all_gather | solution.py:291
  10.9 131.1 %all-gather.18.cloned.1.call-start = ((), (), s32[]{:S(2)}) async-start(), calls=%async_computation.14 | async-start | bytes 1327104 | tf_op jit(solution)/shard_map/all_gather | solution.py:287
  12.9 144.0 %all-gather.26.cloned.1.call-start = ((), (), s32[]{:S(2)}) async-start(), calls=%async_computation.19 | async-start | bytes 3932160 | tf_op jit(solution)/shard_map/all_gather | solution.py:313
  32.1 37.8 %all-to-all-start = ((f32[8,2,576]{2,1,0:T(2,128)}), f32[8,2,576]{2,1,0:T(2,128)S(1)}, u32[]{:S(2)}, u32[]{:S(2)}) async-start(f32[8,2,576]{2,1,0:T(2,128)} %all_to_all.50), calls=%async_computation | async-start | bytes 81920 | tf_op jit(solution)/shard_map/all_to_all | solution.py:262
  35.4 162.9 %all-gather.22.cloned.1.call-start = ((), (), s32[]{:S(2)}) async-start(), calls=%async_computation.16 | async-start | bytes 1327104 | tf_op jit(solution)/shard_map/all_gather | solution.py:288
  70.6 71.3 %copy-start.25 = (f32[2,768]{1,0:T(2,128)}, f32[2,768]{1,0:T(2,128)S(1)}, u32[]{:S(2)}) copy-start(f32[2,768]{1,0:T(2,128)S(1)} %get-tuple-element.117) | copy-start | bytes 18436
  118.7 19.2 %all-to-all-start.1 = ((bf16[2,1024,192]{2,0,1:T(2,128)(2,1)}), bf16[2,1024,192]{2,0,1:T(2,128)(2,1)}, u32[]{:S(2)}, u32[]{:S(2)}) async-start(bf16[2,1024,192]{2,0,1:T(2,128)(2,1)} %copy.110), calls=%async_computation.1 | async-start | bytes 2097152 | tf_op jit(solution)/shard_map/all_to_all | solution.py:304
  124.2 105.1 %all-gather.20.cloned.1.call-start = ((), (), s32[]{:S(2)}) async-start(), calls=%async_computation.15 | async-start | bytes 3932160 | tf_op jit(solution)/shard_map/all_gather | solution.py:312
  147.8 123.8 %all-gather.24.cloned.1.call-start = ((), (), s32[]{:S(2)}) async-start(), calls=%async_computation.17 | async-start | bytes 1327104 | tf_op jit(solution)/shard_map/all_gather | solution.py:289
  152.3 170.6 %reduce-scatter.13.cloned.1.call-start = ((), (), s32[]{:S(2)}) async-start(), calls=%async_computation.20 | async-start | bytes 3932160 | tf_op jit(solution)/shard_map/reduce_scatter | solution.py:324
  284.7 78.8 %reduce-scatter.11.cloned.1.call-start = ((), (), s32[]{:S(2)}) async-start(), calls=%async_computation.18 | async-start | bytes 3932160 | tf_op jit(solution)/shard_map/reduce_scatter | solution.py:319
  293.7 141.8 %reduce-scatter.19.cloned.1.call-start = ((), (), s32[]{:S(2)}) async-start(), calls=%async_computation.23 | async-start | bytes 1327104 | tf_op jit(solution)/shard_map/reduce_scatter | solution.py:386
  294.5 69.1 %copy-start.24 = (f32[2,768]{1,0:T(2,128)S(1)}, f32[2,768]{1,0:T(2,128)}, u32[]{:S(2)}) copy-start(f32[2,768]{1,0:T(2,128)} %get-tuple-element.112) | copy-start | bytes 18436
  370.1 129.7 %reduce-scatter.21.cloned.1.call-start = ((), (), s32[]{:S(2)}) async-start(), calls=%async_computation.25 | async-start | bytes 1327104 | tf_op jit(solution)/shard_map/reduce_scatter | solution.py:386
  377.0 189.1 %reduce-scatter.23.cloned.1.call-start = ((), (), s32[]{:S(2)}) async-start(), calls=%async_computation.26 | async-start | bytes 1327104 | tf_op jit(solution)/shard_map/reduce_scatter | solution.py:386
  383.9 216.8 %all-reduce.7.cloned.1.call-start = ((), (), s32[]{:S(2)}) async-start(), calls=%async_computation.24 | async-start | bytes 786432 | tf_op jit(solution)/shard_map/psum | solution.py:397
  405.3 32.4 %copy-start.45 = (f32[2,1024]{1,0:T(2,128)S(1)}, f32[2,1024]{1,0:T(2,128)}, u32[]{:S(2)}) copy-start(f32[2,1024]{1,0:T(2,128)} %copy-done.44) | copy-start | bytes 24580
  405.3 32.4 %copy-start.47 = (f32[2,768]{1,0:T(2,128)S(1)}, f32[2,768]{1,0:T(2,128)}, u32[]{:S(2)}) copy-start(f32[2,768]{1,0:T(2,128)} %copy-done.46) | copy-start | bytes 18436
  405.3 32.4 %copy-start.49 = (s32[768]{0:T(1024)S(1)}, s32[768]{0:T(1024)}, u32[]{:S(2)}) copy-start(s32[768]{0:T(1024)} %copy-done.48) | copy-start | bytes 9220
  437.4 230.9 %reduce-scatter.17.cloned.1.call-start = ((), (), s32[]{:S(2)}) async-start(), calls=%async_computation.22 | async-start | bytes 1327104 | tf_op jit(solution)/shard_map/reduce_scatter | solution.py:386
  445.6 263.7 %reduce-scatter.15.cloned.1.call-start = ((), (), s32[]{:S(2)}) async-start(), calls=%async_computation.21 | async-start | bytes 3932160 | tf_op jit(solution)/shard_map/reduce_scatter | solution.py:344
  577.7 131.6 %copy-start.10 = (bf16[2,256,768]{2,1,0:T(8,128)(2,1)S(1)}, bf16[2,256,768]{2,1,0:T(8,128)(2,1)}, u32[]{:S(2)}) copy-start(bf16[2,256,768]{2,1,0:T(8,128)(2,1)} %param.19) | copy-start | bytes 2359300
  577.7 131.6 %copy-start.36 = (f32[2,256]{1,0:T(2,128)S(1)}, f32[2,256]{1,0:T(2,128)}, u32[]{:S(2)}) copy-start(f32[2,256]{1,0:T(2,128)} %copy-done.35) | copy-start | bytes 6148
  580.4 142.0 %copy-start.34 = (f32[768]{0:T(1024)S(1)}, f32[768]{0:T(1024)}, u32[]{:S(2)}) copy-start(f32[768]{0:T(1024)} %copy-done.33) | copy-start | bytes 9220
  580.4 142.0 %copy-start.32 = (f32[768]{0:T(1024)S(1)}, f32[768]{0:T(1024)}, u32[]{:S(2)}) copy-start(f32[768]{0:T(1024)} %copy-done.31) | copy-start | bytes 9220
  602.5 127.1 %copy-start.12 = (f32[2,256,768]{2,1,0:T(8,128)S(1)}, f32[2,256,768]{2,1,0:T(8,128)}, u32[]{:S(2)}) copy-start(f32[2,256,768]{2,1,0:T(8,128)} %copy-done.11) | copy-start | bytes 4718596
  723.2 72.9 %all-to-all-start.3 = ((bf16[2,8,576]{2,0,1:T(2,128)(2,1)}), bf16[2,8,576]{2,0,1:T(2,128)(2,1)S(1)}, u32[]{:S(2)}, u32[]{:S(2)}) async-start(bf16[2,8,576]{2,0,1:T(2,128)(2,1)} %copy.125), calls=%async_computation.6 | async-start | bytes 40960 | tf_op jit(solution)/shard_map/all_to_all | solution.py:375
  728.6 64.7 %reduce-scatter.25.cloned.1.call-start = ((), (), s32[]{:S(2)}) async-start(), calls=%async_computation.27 | async-start | bytes 442368
  728.7 67.6 %copy-start.30 = (bf16[8,2,128]{2,1,0:T(2,128)(2,1)S(1)}, bf16[8,2,128]{2,1,0:T(2,128)(2,1)}, u32[]{:S(2)}) copy-start(bf16[8,2,128]{2,1,0:T(2,128)(2,1)} %copy-done.29) | copy-start | bytes 12292
  729.6 112.2 %copy-start.1 = (bf16[768,384]{1,0:T(8,128)(2,1)S(1)}, bf16[768,384]{1,0:T(8,128)(2,1)}, u32[]{:S(2)}) copy-start(bf16[768,384]{1,0:T(8,128)(2,1)} %param.28) | copy-start | bytes 1769476
  (49 other events, 605.8 us)
Sparse Core Ops, SparseCore 0:
  10.9 42.3 all-gather.15
  54.8 28.8 all-gather.13
  86.5 39.6 all-gather.17
  127.6 29.2 all-gather.25
  159.5 38.8 all-gather.21
  200.3 28.9 all-gather.19
  232.1 39.3 all-gather.23
  284.8 37.9 reduce-scatter.12
  325.6 37.9 reduce-scatter.10
  370.2 62.4 reduce-scatter.18
  436.7 63.0 reduce-scatter.20
  503.0 63.0 reduce-scatter.22
  569.0 31.5 all-reduce.6
  604.2 63.9 reduce-scatter.16
  670.8 38.4 reduce-scatter.14
  732.4 60.9 reduce-scatter.24

commit v2 on v1

--- a/solution.py
+++ b/solution.py
@@ -200,6 +200,324 @@
     mean_e = jnp.mean(e, axis=-1, keepdims=True)
     mean_en = jnp.mean(e * normal, axis=-1, keepdims=True)
     return inverse * (e - mean_e - normal * mean_en)
+
+
+MESH = pl.DeviceIdType.MESH
+VM = pl.BlockSpec(memory_space=pltpu.VMEM)
+ANY = pl.BlockSpec(memory_space=pl.ANY)
+
+
+def round16(size):
+    return -(-size // 16) * 16
+
+
+def greet(peers):
+    barrier = pltpu.get_barrier_semaphore()
+    for peer in peers:
+        pl.semaphore_signal(barrier, inc=1, device_id=peer, device_id_type=MESH)
+    pl.semaphore_wait(barrier, len(peers))
+
+
+def push(src, dst, send, recv, peer):
+    return pltpu.make_async_remote_copy(
+        src_ref=src,
+        dst_ref=dst,
+        send_sem=send,
+        recv_sem=recv,
+        device_id=peer,
+        device_id_type=MESH,
+    )
+
+
+class Place:
+    def __init__(self, n, m):
+        self.n, self.m = n, m
+        self.f = lax.axis_index("fsdp")
+        self.d = lax.axis_index("dp")
+        self.lines = n // 2
+        self.a = self.f // 2
+        self.b = self.f % 2
+        self.x = self.d // 2
+        self.c = self.d % 2
+        self.sib_d = self.x * 2 + 1 - self.c
+        self.far_d = (1 - self.x) * 2 + self.c
+        self.diag_d = (1 - self.x) * 2 + 1 - self.c
+        self.sib = (self.f, self.sib_d)
+        self.far = (self.f, self.far_d)
+        self.diag = (self.f, self.diag_d)
+        self.side_f = self.a * 2 + 1 - self.b
+        self.side = (self.side_f, self.d)
+
+    def line_f(self, step):
+        return (self.a + step + self.lines) % self.lines * 2 + self.b
+
+    def ring_f(self, step):
+        return (self.f + step + self.n) % self.n
+
+
+def gather_start(p, src, buf, zs, zr, ys, yr):
+    copies = []
+    for i in range(1, p.lines):
+        copies.append(push(src, buf.at[p.f], zs.at[i], zr.at[i], (p.line_f(i), p.d)))
+    copies.append(push(src, buf.at[p.f], ys.at[0], yr.at[0], p.side))
+    for copy in copies:
+        copy.start()
+
+
+def gather_forward(p, buf, zs, zr, ys, yr):
+    for i in range(1, p.lines):
+        block = buf.at[p.line_f(-i)]
+        push(block, block, zs.at[i], zr.at[i], (p.line_f(i), p.d)).wait_recv()
+        push(block, block, ys.at[i], yr.at[i], p.side).start()
+
+
+def gather_finish(p, src, buf, zs, zr, ys, yr):
+    for i in range(p.lines):
+        theirs = buf.at[(p.a - i + p.lines) % p.lines * 2 + 1 - p.b]
+        push(theirs, theirs, ys.at[i], yr.at[i], p.side).wait_recv()
+
+
+def gather_drain(p, src, buf, zs, zr, ys, yr):
+    for i in range(1, p.lines):
+        push(src, buf.at[p.f], zs.at[i], zr.at[i], (p.line_f(i), p.d)).wait_send()
+    for i in range(p.lines):
+        push(src, buf.at[p.f], ys.at[i], yr.at[i], p.side).wait_send()
+
+
+def norm_rows(stream):
+    average = jnp.mean(stream, axis=-1, keepdims=True)
+    centered = stream - average
+    variance = jnp.mean(centered * centered, axis=-1, keepdims=True)
+    inverse = lax.rsqrt(variance + EPS)
+    return centered * inverse, inverse
+
+
+def turned(v):
+    lanes = lax.broadcasted_iota(jnp.int32, v.shape, 1)
+    half = HEAD // 2
+    return jnp.where(lanes % HEAD < half, pltpu.roll(v, 128 - half, 1), pltpu.roll(v, half, 1))
+
+
+def front_kernel(
+    n,
+    m,
+    per,
+    tok_ref,
+    cond_ref,
+    wada_ref,
+    bada_ref,
+    vec_ref,
+    qrow_ref,
+    orow_ref,
+    place_ref,
+    cos_ref,
+    sin_ref,
+    qkv_out,
+    normed_out,
+    mod_ref,
+    vecs_ref,
+    wqkv_ref,
+    wout_out,
+    cond_out,
+    cond_all_ref,
+    qkv_ref,
+    normed_ref,
+    tall_ref,
+    mod_send,
+    mod_recv,
+    vbuf,
+    qbuf,
+    obuf,
+    cs,
+    cr,
+    ms,
+    mr,
+    gz,
+    ts,
+    tr,
+    local,
+):
+    p = Place(n, m)
+    slots, quarter, width = tok_ref.shape
+    half = quarter // 2
+    part = width // m
+    greet([p.sib, p.far] + [(p.ring_f(i), p.d) for i in range(1, n)])
+
+    cond_all_ref[p.f] = cond_ref[...]
+    for i in range(1, n):
+        push(cond_ref, cond_all_ref.at[p.f], cs.at[i], cr.at[i], (p.ring_f(i), p.d)).start()
+    vec = (p, vec_ref, vbuf) + tuple(gz.at[0, k] for k in range(4))
+    qry = (p, qrow_ref, qbuf) + tuple(gz.at[1, k] for k in range(4))
+    out = (p, orow_ref, obuf) + tuple(gz.at[2, k] for k in range(4))
+    gather_start(*vec)
+
+    def token_copy(kind, k):
+        s, rows = k // 2, pl.ds(k % 2 * half, half)
+        if kind == 2:
+            block = tall_ref.at[p.far_d, s, rows]
+            return push(block, block, ts.at[kind, k], tr.at[kind, k], p.sib)
+        return push(
+            tok_ref.at[s, rows],
+            tall_ref.at[p.d, s, rows],
+            ts.at[kind, k],
+            tr.at[kind, k],
+            p.sib if kind == 0 else p.far,
+        )
+
+    for k in range(2 * slots):
+        token_copy(1, k).start()
+    gather_start(*qry)
+    for k in range(2 * slots):
+        token_copy(0, k).start()
+    gather_start(*out)
+    vbuf[p.f] = vec_ref[...]
+    qbuf[p.f] = qrow_ref[...]
+    obuf[p.f] = orow_ref[...]
+
+    def pass_on(k):
+        token_copy(1, k).wait_recv()
+        token_copy(2, k).start()
+
+    for i in range(1, n):
+        push(cond_ref, cond_all_ref.at[p.f], cs.at[i], cr.at[i], (p.ring_f(i), p.d)).wait_recv()
+    cond_out[...] = cond_all_ref[...]
+    conds = cond_all_ref[...].reshape(n * 16, cond_ref.shape[1])
+    mod_cols = mm(conds, wada_ref[...], NN) + bada_ref[...].astype(F32)
+    mod_send[...] = mod_cols.reshape(n, 16, mod_cols.shape[1])[:, :8]
+    mod_recv[p.f] = mod_send[p.f]
+    for i in range(1, n):
+        peer = p.ring_f(i)
+        push(mod_send.at[peer], mod_recv.at[p.f], ms.at[i], mr.at[i], (peer, p.d)).start()
+    gather_forward(*vec[:1], *vec[2:])
+    pass_on(0)
+    for i in range(1, n):
+        peer = p.ring_f(i)
+        push(mod_send.at[peer], mod_recv.at[p.f], ms.at[i], mr.at[i], (peer, p.d)).wait_recv()
+    cols = mod_cols.shape[1]
+    for g in range(n):
+        mod_ref[:, g * cols : (g + 1) * cols] = mod_recv[g]
+    gather_finish(*vec)
+    for g in range(n):
+        row = vbuf[g].astype(F32)
+        for k in range(4):
+            vecs_ref[k : k + 1, g * per[k] : (g + 1) * per[k]] = row[k : k + 1, : per[k]]
+    vecs_ref[4:8, :] = jnp.zeros((4, vecs_ref.shape[1]), F32)
+    pass_on(1)
+
+    gain = vecs_ref[1:2, :width]
+
+    def normed_of(q, s):
+        stream = tall_ref[q, s].astype(F32)
+        normal, _ = norm_rows(stream)
+        shift = mod_ref[s : s + 1, :width]
+        scale = mod_ref[s : s + 1, width : 2 * width]
+        rows = pl.ds(pl.multiple_of(q * quarter, quarter), quarter)
+        normed_ref[s, rows, :] = (normal * (gain * (1.0 + scale)) + shift).astype(BF16)
+
+    def project(q, s, index):
+        rows = pl.ds(pl.multiple_of(q * quarter, quarter), quarter)
+        got = mm(normed_ref[s, rows, :], wqkv_ref[...], NT)
+        cosine = cos_ref[rows, :]
+        sine = sin_ref[rows, :]
+        lanes = lax.broadcasted_iota(jnp.int32, (quarter, 128), 1)
+        for t in range(0, 2 * part, 128):
+            tile = got[:, t : t + 128]
+            tile = tile * cosine + turned(tile) * sine
+            tile = jnp.where(lanes + t < part, tile * (1.0 / math.sqrt(HEAD)), tile)
+            qkv_ref[s, rows, t : t + 128] = tile.astype(BF16)
+        qkv_ref[s, rows, 2 * part :] = got[:, 2 * part :].astype(BF16)
+        for src, dst, k in ((qkv_ref, qkv_out, 0), (normed_ref, normed_out, 1)):
+            pltpu.make_async_copy(src.at[s, rows], dst.at[s, rows], local.at[k, index]).start()
+
+    tall_ref[p.d] = tok_ref[...]
+    for s in range(slots):
+        normed_of(p.d, s)
+    gather_forward(p, *qry[2:])
+    for k in range(slots):
+        token_copy(0, 2 * k).wait_recv()
+        token_copy(0, 2 * k + 1).wait_recv()
+        normed_of(p.sib_d, k)
+    pass_on(2)
+    gather_finish(*qry)
+    sel = lax.broadcasted_iota(jnp.int32, (3 * part, qbuf.shape[0] * qbuf.shape[1]), 0)
+    placing = (sel == place_ref[...]).astype(BF16)
+    wqkv_ref[...] = mm(placing, qbuf[...].reshape(-1, width), NN).astype(BF16)
+    for s in range(slots):
+        project(p.d, s, s)
+        project(p.sib_d, s, slots + s)
+    gather_forward(p, *out[2:])
+    pass_on(3)
+    for s in range(slots):
+        normed_of(p.far_d, s)
+        project(p.far_d, s, 2 * slots + s)
+        token_copy(2, 2 * s).wait_recv()
+        token_copy(2, 2 * s + 1).wait_recv()
+        normed_of(p.diag_d, s)
+        project(p.diag_d, s, 3 * slots + s)
+    gather_finish(*out)
+    keep = pltpu.make_async_copy(obuf, wout_out, local.at[2, 0])
+    keep.start()
+
+    for i in range(1, n):
+        peer = p.ring_f(i)
+        push(cond_ref, cond_all_ref.at[p.f], cs.at[i], cr.at[i], (peer, p.d)).wait_send()
+        push(mod_send.at[peer], mod_recv.at[p.f], ms.at[i], mr.at[i], (peer, p.d)).wait_send()
+    for item in (vec, qry, out):
+        gather_drain(*item)
+    for k in range(2 * slots):
+        for kind in range(3):
+            token_copy(kind, k).wait_send()
+    for s in range(slots):
+        for j, q in enumerate((p.d, p.sib_d, p.far_d, p.diag_d)):
+            rows = pl.ds(pl.multiple_of(q * quarter, quarter), quarter)
+            for src, dst, k in ((qkv_ref, qkv_out, 0), (normed_ref, normed_out, 1)):
+                pltpu.make_async_copy(src.at[s, rows], dst.at[s, rows], local.at[k, j * slots + s]).wait()
+    keep.wait()
+
+
+def front(n, m, per, length, tokens, cond, w_ada, b_ada, vec, qkv_rows, out_rows, place, cosine, sine):
+    slots, quarter, width = tokens.shape
+    part = width // m
+    lines = n // 2
+    dma = pltpu.SemaphoreType.DMA
+    shape = jax.ShapeDtypeStruct
+    return pl.pallas_call(
+        functools.partial(front_kernel, n, m, per),
+        out_shape=(
+            shape((slots, length, 3 * part), BF16),
+            shape((slots, length, width), BF16),
+            shape((8, 6 * width), F32),
+            shape((8, max(width, n * per[0])), F32),
+            shape((3 * part, width), BF16),
+            shape((n,) + out_rows.shape, BF16),
+            shape((n,) + cond.shape, BF16),
+        ),
+        in_specs=[VM] * 10,
+        out_specs=(ANY, ANY, VM, VM, VM, ANY, VM),
+        scratch_shapes=[
+            pltpu.VMEM((n,) + cond.shape, BF16),
+            pltpu.VMEM((slots, length, 3 * part), BF16),
+            pltpu.VMEM((slots, length, width), BF16),
+            pltpu.VMEM((m, slots, quarter, width), BF16),
+            pltpu.VMEM((n, 8, w_ada.shape[1]), F32),
+            pltpu.VMEM((n, 8, w_ada.shape[1]), F32),
+            pltpu.VMEM((n,) + vec.shape, BF16),
+            pltpu.VMEM((n,) + qkv_rows.shape, BF16),
+            pltpu.VMEM((n,) + out_rows.shape, BF16),
+            dma((n,)),
+            dma((n,)),
+            dma((n,)),
+            dma((n,)),
+            dma((3, 4, lines)),
+            dma((3, 2 * slots)),
+            dma((3, 2 * slots)),
+            dma((3, m * slots)),
+        ],
+        compiler_params=pltpu.CompilerParams(
+            collective_id=1, has_side_effects=True, vmem_limit_bytes=48 << 20
+        ),
+        name="front",
+    )(tokens, cond, w_ada, b_ada, vec, qkv_rows, out_rows, place, cosine, sine)
 
 
 def column_plan(shards_n, ranks, columns):
@@ -257,22 +575,8 @@
     cos_np, sin_np = rope_table(length)
     cosine, sine = jnp.asarray(cos_np), jnp.asarray(sin_np)
 
-    cond_all = lax.all_gather(condition, "fsdp", axis=0, tiled=True)
-    mod_cols = mm(cond_all, w_ada, NN) + b_ada.astype(F32)
-    modulation = lax.all_to_all(mod_cols, "fsdp", 0, 1, tiled=True)
-    shift_attn, scale_attn, gate_attn, shift_mlp, scale_mlp, gate_mlp = [
-        g[:, None, :] for g in jnp.split(modulation, 6, axis=-1)
-    ]
-    own_vec = jnp.concatenate([b_up, gain_attn, gain_mlp, b_down])[None]
-    vecs = lax.all_gather(own_vec, "fsdp", axis=0, tiled=True).astype(F32)
     ups = b_up.shape[0]
     small = gain_attn.shape[0]
-    b_up_all = vecs[:, :ups].reshape(n, m, ups // m)
-    b_up_rank = lax.dynamic_index_in_dim(b_up_all, d, 1, False).reshape(-1)
-    gain_attn_all = vecs[:, ups : ups + small].reshape(-1)
-    gain_mlp_all = vecs[:, ups + small : ups + 2 * small].reshape(-1)
-    b_down_all = vecs[:, ups + 2 * small :].reshape(-1)
-
     most, take, place, home = column_plan(n, m, w_qkv.shape[1] * n)
     picked = pick(jnp.asarray(take)[f, d], w_qkv.shape[1])
     qkv_rows = mm(picked, w_qkv, NT).astype(BF16)
@@ -281,28 +585,54 @@
         w_down.reshape(n, m, ups // m, small), d, 1, False
     ).reshape(-1, small).T
     out_rows = w_out.reshape(heads // m, m, HEAD, small).transpose(1, 0, 2, 3).reshape(-1, small).T
-    qkv_packed = lax.all_gather(qkv_rows, "fsdp", axis=0, tiled=True)
-    placing = pick(jnp.asarray(place)[d], 3 * part)
-    w_qkv_t = mm(placing, qkv_packed, TN).astype(BF16)
-    w_out_t = lax.all_gather(out_rows, "fsdp", axis=0, tiled=True)
+    place_row = jnp.asarray(place)[d]
+    placing = pick(place_row, 3 * part)
+
+    pad_rows = lambda v, size: jnp.pad(v, ((0, size - v.shape[0]), (0, 0)))
+    wide = max(width, n * (ups // m))
+    vec = jnp.stack(
+        [
+            jnp.pad(v, (0, width - v.shape[0]))
+            for v in (
+                lax.dynamic_slice_in_dim(b_up, d * (ups // m), ups // m, 0),
+                gain_attn,
+                gain_mlp,
+                b_down,
+            )
+        ]
+    )
+    qkv, normed, mod_rows, vec_rows, w_qkv_t, out_blocks, cond_blocks = front(
+        n,
+        m,
+        (ups // m, small, small, small),
+        length,
+        tokens,
+        pad_rows(condition, 16),
+        w_ada,
+        b_ada[None],
+        pad_rows(vec, 16),
+        qkv_rows,
+        pad_rows(out_rows, round16(small)),
+        place_row[None],
+        jnp.concatenate([cosine, cosine], axis=1),
+        jnp.concatenate([sine, sine], axis=1),
+    )
+    cond_all = cond_blocks[:, :slots].reshape(n * slots, -1)
+    modulation = mod_rows[:slots]
+    shift_attn, scale_attn, gate_attn, shift_mlp, scale_mlp, gate_mlp = [
+        g[:, None, :] for g in jnp.split(modulation, 6, axis=-1)
+    ]
+    b_up_rank = vec_rows[0, : hidden_part]
+    gain_attn_all, gain_mlp_all, b_down_all = [vec_rows[i, :width] for i in (1, 2, 3)]
+    w_out_t = out_blocks[:, :small].reshape(width, width)
     w_up_t = lax.all_gather(up_rows, "fsdp", axis=0, tiled=True)
     w_down_t = lax.all_gather(down_rows, "fsdp", axis=0, tiled=True)
 
-    group_tokens = lax.all_gather(tokens, "dp", axis=1, tiled=True)
-    normal, _ = norm_parts(group_tokens.astype(F32))
-    normed = (normal * (gain_attn_all * (1.0 + scale_attn)) + shift_attn).astype(BF16)
-    projected = mm(normed.reshape(-1, width), w_qkv_t, NT).reshape(slots, length, 3 * heads // m, HEAD)
-    rot = projected * cosine[:, None, :] + swap_halves(projected) * sine[:, None, :]
-    hr = heads // m
-    qkv = jnp.concatenate(
-        [rot[:, :, :hr] * (1.0 / math.sqrt(HEAD)), rot[:, :, hr : 2 * hr], projected[:, :, 2 * hr :]],
-        axis=2,
-    ).astype(BF16).reshape(slots, length, 3 * part)
-
     attended, logs = attend(segments, qkv, tile)
 
     own = lax.all_to_all(attended, "dp", 1, 2, tiled=True)
     own_tokens = tokens.astype(F32)
+    hr = heads // m
     flat = lambda v: v.reshape(-1, v.shape[-1])
     back = lambda v: v.reshape(slots, -1, v.shape[-1])
     branch_attn = back(mm(flat(own), w_out_t, NT))

time: 860 us -> 789 us (0.917)
  waiting for transfers between devices: 474 us -> 396 us
  Pallas kernels: 46.5 us -> 108 us
  blocking collectives: 145 us -> 98.1 us
  local copies, waits for them, and re-layouts: 49.6 us -> 60.7 us
    pallas_call x0 -> x1, Pallas kernels: none -> 62.3 us  [front(): pl.pallas_call(functools.partial(front_kernel, n, m, per), out_shape=(sha...]
    all_gather x1, waiting for transfers between devices: 37.3 us -> 0.01 us  [shards(): w_up_t = lax.all_gather(up_rows, 'fsdp', axis=0, tiled=True)]
    unnamed x3 -> x2, blocking collectives: 73.5 us -> 43.3 us
    all_gather x1 -> x0, blocking collectives: 17.8 us -> none  [shards(): cond_all = lax.all_gather(condition, 'fsdp', axis=0, tiled=True)]
    all_gather x1, waiting for transfers between devices: 31 us -> 17.6 us  [shards(): normed_mlp_all = flat(lax.all_gather(normed_mlp, 'dp', axis=1, tiled=True))]
    all_gather x3 -> x0, waiting for transfers between devices: 10.7 us -> none  [the longest x1 10.7 us: shards(): group_tokens = lax.all_gather(tokens, 'dp', axis=1, tiled=True)]
    dot_general x18 -> x15, matrix products: 74.1 us -> 68.2 us  [mm(): return lax.dot_general(a, b, dims, preferred_element_type=F32)]
    unnamed x145 -> x76, local copies, waits for them, and re-layouts: 17.6 us -> 23.2 us
  transfers between devices with their start and end apart: 19 -> 15, of which waited for: 14 -> 11; matrix products, arithmetic and copies ran while one was open for 14% -> 14% of each run, Pallas kernels for 5% -> 14%
where the time goes in v2:
time: 789 us; the launch traced here: 781 us
  waiting for transfers between devices  396 us (50%)
  Pallas kernels  108 us (14%)
  blocking collectives  98.1 us (12%)
  matrix products  68.2 us (9%)
  local copies, waits for them, and re-layouts  60.7 us (8%)
  other arithmetic  19.8 us (3%)
  between operations  16.9 us (2%)
  starting transfers between devices  12.5 us (2%)
    reduce_scatter x4, waiting for transfers between devices, scatter(): return lax.psum_scatter(v, 'fsdp', scatter_dimension=0, tiled=True)  159 us
    dot_general x15, matrix products, mm(): return lax.dot_general(a, b, dims, preferred_element_type=F32)  68.2 us
    pallas_call x1, Pallas kernels, front(): pl.pallas_call(functools.partial(front_kernel, n, m, per), out_shape=(sha...  62.3 us
    unnamed x14, waiting for transfers between devices  61.8 us
    unnamed x2, blocking collectives  43.3 us
    reduce_scatter x1, waiting for transfers between devices, shards(): lax.psum_scatter(branch_part, 'dp', scatter_dimension=1, tiled=True)  38.1 us
    all_gather x1, waiting for transfers between devices, shards(): w_down_t = lax.all_gather(down_rows, 'fsdp', axis=0, tiled=True)  34.5 us
    pallas_call x1, Pallas kernels, attend_back(): pl.pallas_call(functools.partial(attend_back_kernel, tile), grid=(slots,...  30.1 us
  transfers between devices with their start and end apart: 15, of which 11 were waited for; matrix products, arithmetic and copies ran while one was open for 14% of the time, Pallas kernels for 14%

profile of v2, /device:TPU:1, one launch (start us, length us, event | category | flops | bytes accessed | tf_op | source)
XLA Modules:
  0.0 780.9 jit_solution(14351929786950339691)
XLA Ops:
  17.5 62.3 %front.1 = (bf16[2,1024,576]{2,1,0:T(8,128)(2,1)}, bf16[2,1024,768]{2,1,0:T(8,128)(2,1)}, f32[8,4608]{1,0:T(8,128)S(1)}, f32[8,768]{1,0:T(8,128)S(1)}, bf16[576,...) custom-call(bf16[2,256,768]{2,1,0:T(8,128)(2,1)S(1)} %copy-done.2, ...), custom_call_target="tpu_custom_call" | custom-call | tf_op jit(solution)/shard_map/front/pallas_call | solution.py:484
  83.4 16.0 %attend.1 = (bf16[2,1024,192]{2,1,0:T(8,128)(2,1)S(1)}, f32[2,1024,128]{2,1,0:T(8,128)S(1)}) custom-call(s32[2,1,1024]{2,1,0:T(1,128)S(1)} %broadcast_in_dim.5.seg_ref, bf16[2,1024,576]{2,1,0:T(8,128)(2,1)S(1)} %copy-done.3), custom_call_target="tpu_custom_call" | custom-call | tf_op jit(solution)/shard_map/attend/pallas_call | solution.py:87
  102.4 5.6 all-to-all-start
  108.3 13.3 %all-to-all-done = bf16[2,1024,192]{2,0,1:T(2,128)(2,1)S(1)} async-done(((bf16[2,1024,192]{2,0,1:T(2,128)(2,1)}), bf16[2,1024,192]{2,0,1:T(2,128)(2,1)S(1)}, u32[]{:S(2)}, u32[]{:S(2)}) %all-to-all-start) | async-done | bytes 786464 | tf_op jit(solution)/shard_map/all_to_all | solution.py:633
  138.4 4.4 multiply_convert_fusion
  142.7 17.6 %all-gather.9.cloned.1.call-done = bf16[2,1024,768]{2,1,0:T(8,128)(2,1)} async-done(((bf16[2,256,768]{2,1,0:T(8,128)(2,1)}), bf16[2,1024,768]{2,1,0:T(8,128)(2,1)}) %all-gather.9.cloned.1.call-update) | async-done | bytes 3145744 | tf_op jit(solution)/shard_map/all_gather | solution.py:642
  160.3 7.5 fusion.50
  167.9 34.5 %all-gather.13.cloned.1.call-done = bf16[768,768]{1,0:T(8,128)(2,1)} async-done(((bf16[96,768]{1,0:T(8,128)(2,1)}), bf16[768,768]{1,0:T(8,128)(2,1)}) %all-gather.13.cloned.1.call-update) | async-done | bytes 1179664 | tf_op jit(solution)/shard_map/all_gather | solution.py:629
  202.4 8.8 %convert_reduce_fusion = (f32[768]{0:T(1024)S(1)}, bf16[2048,768]{1,0:T(8,128)(2,1)S(1)}) fusion(f32[2048,768]{1,0:T(8,128)} %fusion.50, f32[768]{0:T(1024)S(1)} %get-tuple-element.98, bf16[2048,768]{1,0:T(8,128)(2,1)} %bitcast.98, bf16[768,768]{1,0:T(8,128)(2,1)} %all-gather.13.cloned.1.call-done), kind=kOutput, calls=%fused_computation.9 | convolution fusion | flops 2452094208 | bytes 13768704 | tf_op jit(solution)/shard_map/dot_general | solution.py:25
  211.2 4.0 convolution_convert_fusion.1
  215.3 8.9 %convolution_convert_fusion.2 = bf16[2048,768]{1,0:T(8,128)(2,1)} fusion(bf16[768,768]{1,0:T(8,128)(2,1)} %all-gather.13.cloned.1.call-done, f32[2048,768]{1,0:T(8,128)} %fusion.50, f32[768]{0:T(1024)S(1)} %get-tuple-element.98), kind=kOutput, calls=%fused_computation.14 | convolution fusion | flops 2433220608 | bytes 10619904 | tf_op jit(solution)/shard_map/dot_general | solution.py:25
  226.3 27.1 %reduce-scatter.13.cloned.1.call-done = bf16[2,256,768]{2,1,0:T(8,128)(2,1)} async-done(((bf16[2,1024,768]{2,1,0:T(8,128)(2,1)}), bf16[2,256,768]{2,1,0:T(8,128)(2,1)}) %reduce-scatter.13.cloned.1.call-update) | async-done | bytes 786448 | tf_op jit(solution)/shard_map/reduce_scatter | solution.py:654
  255.8 38.1 %reduce-scatter.11.cloned.1.call-done = bf16[2,256,768]{2,1,0:T(8,128)(2,1)} async-done(((bf16[2,1024,768]{2,1,0:T(8,128)(2,1)}), bf16[2,256,768]{2,1,0:T(8,128)(2,1)}) %reduce-scatter.11.cloned.1.call-update) | async-done | bytes 786448 | tf_op jit(solution)/shard_map/reduce_scatter | solution.py:649
  301.1 6.5 convolution_convert_fusion.4
  307.7 7.8 %convolution_convert_fusion.3 = bf16[768,768]{1,0:T(8,128)(2,1)} fusion(bf16[2048,768]{1,0:T(8,128)(2,1)} %bitcast.99, f32[2048,768]{1,0:T(8,128)} %fusion.50, f32[768]{0:T(1024)S(1)} %get-tuple-element.98), kind=kOutput, calls=%fused_computation.60 | convolution fusion | flops 2432237568 | bytes 10619904 | tf_op jit(solution)/shard_map/dot_general | solution.py:25
  320.9 14.1 %all_to_all.49 = bf16[2,256,768]{1,0,2:T(2,128)(2,1)S(1)} all-to-all(bf16[2,256,768]{1,0,2:T(2,128)(2,1)S(1)} %copy.88), channel_id=1, replica_groups=mesh['fsdp'=8,'dp'=4] {'dp'}, dimensions={2} | all-to-all | bytes 1572864 | tf_op jit(solution)/shard_map/all_to_all | solution.py:664
  339.7 30.1 %attend_back.1 = bf16[2,1024,576]{2,1,0:T(8,128)(2,1)} custom-call(s32[2,1,1024]{2,1,0:T(1,128)S(1)} %broadcast_in_dim.5.seg_ref, bf16[2,1024,576]{2,1,0:T(8,128)(2,1)} %get-tuple-element.23.qkv_ref, bf16[2,1024,192]{2,1,0:T(8,128)(2,1)S(1)} %bitcast.88, bf16[2,1024,192]{2,1,0:T(8,128)(2,1)S(1)} %get-tuple-element.24.out_ref, f32[2,1024,128]{2,1,0:T(8,128)S(1)} %copy-done.6, ...), custom_call_target="tpu_custom_call" | custom-call | tf_op jit(solution)/shard_map/attend_back/pallas_call | solution.py:170
  371.9 7.6 fusion.30
  379.6 6.0 convolution_convert_fusion
  390.2 40.1 %reduce-scatter.21.cloned.1.call-done = bf16[96,768]{1,0:T(8,128)(2,1)} async-done(((bf16[768,768]{1,0:T(8,128)(2,1)}), bf16[96,768]{1,0:T(8,128)(2,1)}) %reduce-scatter.21.cloned.1.call-update) | async-done | bytes 147472 | tf_op jit(solution)/shard_map/reduce_scatter | solution.py:716
  430.3 9.8 %all-gather.1 = bf16[384,768]{1,0:T(8,128)(2,1)S(1)} all-gather(bf16[96,768]{1,0:T(8,128)(2,1)} %reduce-scatter.21.cloned.1.call-done), channel_id=3, replica_groups=mesh['fsdp'=8,'dp'=4] {'dp'}, dimensions={0}, use_global_device_ids=true | all-gather | bytes 737280 | tf_op jit(solution)/shard_map/all_gather | solution.py:719
  443.8 52.8 %reduce-scatter.23.cloned.1.call-done = bf16[96,768]{1,0:T(8,128)(2,1)} async-done(((bf16[768,768]{1,0:T(8,128)(2,1)}), bf16[96,768]{1,0:T(8,128)(2,1)}) %reduce-scatter.23.cloned.1.call-update) | async-done | bytes 147472 | tf_op jit(solution)/shard_map/reduce_scatter | solution.py:716
  496.6 9.8 %all-gather.3 = bf16[384,768]{1,0:T(8,128)(2,1)S(1)} all-gather(bf16[96,768]{1,0:T(8,128)(2,1)} %reduce-scatter.23.cloned.1.call-done), channel_id=5, replica_groups=mesh['fsdp'=8,'dp'=4] {'dp'}, dimensions={0}, use_global_device_ids=true | all-gather | bytes 737280 | tf_op jit(solution)/shard_map/all_gather | solution.py:719
  515.6 15.4 %all-reduce.12.cloned.1.call-done = f32[768,96]{1,0:T(8,128)} async-done(((f32[768,96]{1,0:T(8,128)}), f32[768,96]{1,0:T(8,128)}) %all-reduce.12.cloned.1.call-update) | async-done | bytes 294928 | tf_op jit(solution)/shard_map/psum | solution.py:727
  532.9 66.0 %reduce-scatter.17.cloned.1.call-done = bf16[96,768]{1,0:T(8,128)(2,1)} async-done(((bf16[768,768]{1,0:T(8,128)(2,1)}), bf16[96,768]{1,0:T(8,128)(2,1)}) %reduce-scatter.17.cloned.1.call-update) | async-done | bytes 147472 | tf_op jit(solution)/shard_map/reduce_scatter | solution.py:716
  598.9 9.9 %all-gather = bf16[384,768]{1,0:T(8,128)(2,1)S(1)} all-gather(bf16[96,768]{1,0:T(8,128)(2,1)} %reduce-scatter.17.cloned.1.call-done), channel_id=2, replica_groups=mesh['fsdp'=8,'dp'=4] {'dp'}, dimensions={0}, use_global_device_ids=true | all-gather | bytes 737280 | tf_op jit(solution)/shard_map/all_gather | solution.py:719
  610.2 29.8 %reduce-scatter.15.cloned.1.call-done = bf16[2,256,768]{2,1,0:T(8,128)(2,1)} async-done(((bf16[2,1024,768]{2,1,0:T(8,128)(2,1)}), bf16[2,256,768]{2,1,0:T(8,128)(2,1)}) %reduce-scatter.15.cloned.1.call-update) | async-done | bytes 786448 | tf_op jit(solution)/shard_map/reduce_scatter | solution.py:674
  642.1 11.1 %psum.14 = f32[2,5376]{1,0:T(2,128)S(1)} all-reduce(f32[2,5376]{1,0:T(2,128)S(1)} %constant_dynamic-update-slice_fusion), channel_id=1, replica_groups=mesh['fsdp'=8,'dp'=4] {'dp'}, use_global_device_ids=true, to_apply=%region_18.19 | all-reduce | flops 10752 | bytes 86016 | tf_op jit(solution)/shard_map/psum | solution.py:697
  654.9 5.5 all-to-all-start.2
  664.4 60.9 %reduce-scatter.25.cloned.1.call-done = f32[96,3]{1,0:T(8,128)} async-done(((f32[768,3]{1,0:T(8,128)}), f32[96,3]{1,0:T(8,128)}) %reduce-scatter.25.cloned.1.call-update) | async-done | bytes 1168
  728.3 28.2 %all-reduce.9 = (bf16[16,128]{1,0:T(8,128)(2,1)S(1)}, f32[768]{0:T(1024)S(1)}) all-reduce(f32[16,128]{1,0:T(8,128)S(1)} %fusion.51, f32[768]{0:T(1024)S(1)} %get-tuple-element.102), channel_id=9, replica_groups=mesh['fsdp'=8,'dp'=4] {'fsdp'}, use_global_device_ids=true, to_apply=%region_19.20.clone | all-reduce | flops 2816 | bytes 18432
  756.7 15.1 %all-reduce.6 = f32[384]{0:T(512)} all-reduce(f32[384]{0:T(512)S(1)} %dynamic-slice_dynamic-update-slice_fusion), channel_id=4, replica_groups=mesh['fsdp'=8,'dp'=4] {'dp'}, use_global_device_ids=true, to_apply=%add.6 | all-reduce | flops 384 | bytes 3072
  (184 shorter events, 89.3 us)
Async XLA Ops:
  7.2 10.2 %copy-start.7 = (f32[1024,128]{1,0:T(8,128)S(1)}, f32[1024,128]{1,0:T(8,128)}, u32[]{:S(2)}) copy-start(f32[1024,128]{1,0:T(8,128)} %constant.85.sin_ref) | copy-start | bytes 1572868
  7.2 8.1 %copy-start.22 = (bf16[768,96]{0,1:T(8,128)(2,1)S(1)}, bf16[768,96]{0,1:T(8,128)(2,1)}, u32[]{:S(2)}) copy-start(bf16[768,96]{0,1:T(8,128)(2,1)} %param.26) | copy-start | bytes 442372
  7.2 9.1 %copy-start.21 = (bf16[768,288]{0,1:T(8,128)(2,1)S(1)}, bf16[768,288]{0,1:T(8,128)(2,1)}, u32[]{:S(2)}) copy-start(bf16[768,288]{0,1:T(8,128)(2,1)} %param.25) | copy-start | bytes 1327108
  7.2 10.2 %copy-start.2 = (bf16[2,256,768]{2,1,0:T(8,128)(2,1)S(1)}, bf16[2,256,768]{2,1,0:T(8,128)(2,1)}, u32[]{:S(2)}) copy-start(bf16[2,256,768]{2,1,0:T(8,128)(2,1)} %tok_ref.1) | copy-start | bytes 2359300
  7.2 131.1 %all-gather.15.cloned.1.call-start = ((), (), s32[]{:S(2)}) async-start(), calls=%async_computation.15 | async-start | bytes 3932160 | tf_op jit(solution)/shard_map/all_gather | solution.py:643
  8.0 134.8 %all-gather.11.cloned.1.call-start = ((), (), s32[]{:S(2)}) async-start(), calls=%async_computation.12 | async-start | bytes 1327104 | tf_op jit(solution)/shard_map/all_gather | solution.py:628
  8.6 8.9 %copy-start.8 = (f32[1024,128]{1,0:T(8,128)S(1)}, f32[1024,128]{1,0:T(8,128)}, u32[]{:S(2)}) copy-start(f32[1024,128]{1,0:T(8,128)} %constant.84.cos_ref) | copy-start | bytes 1572868
  81.6 26.7 %copy-start.11 = (f32[8,4608]{1,0:T(8,128)}, f32[8,4608]{1,0:T(8,128)S(1)}, u32[]{:S(2)}) copy-start(f32[8,4608]{1,0:T(8,128)S(1)} %get-tuple-element.22) | copy-start | bytes 442372
  81.6 1.8 copy-start.3
  102.4 19.2 %all-to-all-start = ((bf16[2,1024,192]{2,0,1:T(2,128)(2,1)}), bf16[2,1024,192]{2,0,1:T(2,128)(2,1)S(1)}, u32[]{:S(2)}, u32[]{:S(2)}) async-start(bf16[2,1024,192]{2,0,1:T(2,128)(2,1)} %copy.82), calls=%async_computation | async-start | bytes 2097152 | tf_op jit(solution)/shard_map/all_to_all | solution.py:633
  108.1 52.3 %all-gather.9.cloned.1.call-start = ((), (), s32[]{:S(2)}) async-start(), calls=%async_computation.11 | async-start | bytes 3932160 | tf_op jit(solution)/shard_map/all_gather | solution.py:642
  131.6 70.8 %all-gather.13.cloned.1.call-start = ((), (), s32[]{:S(2)}) async-start(), calls=%async_computation.13 | async-start | bytes 1327104 | tf_op jit(solution)/shard_map/all_gather | solution.py:629
  137.9 115.5 %reduce-scatter.13.cloned.1.call-start = ((), (), s32[]{:S(2)}) async-start(), calls=%async_computation.16 | async-start | bytes 3932160 | tf_op jit(solution)/shard_map/reduce_scatter | solution.py:654
  202.4 8.8 %copy-start.23 = (bf16[768,768]{1,0:T(8,128)(2,1)S(1)}, bf16[768,768]{1,0:T(8,128)(2,1)}, u32[]{:S(2)}) copy-start(bf16[768,768]{1,0:T(8,128)(2,1)} %all-gather.11.cloned.1.call-done) | copy-start | bytes 3538948
  211.2 4.0 copy-start.26
  215.3 78.6 %reduce-scatter.11.cloned.1.call-start = ((), (), s32[]{:S(2)}) async-start(), calls=%async_computation.14 | async-start | bytes 3932160 | tf_op jit(solution)/shard_map/reduce_scatter | solution.py:649
  224.2 145.6 %reduce-scatter.19.cloned.1.call-start = ((), (), s32[]{:S(2)}) async-start(), calls=%async_computation.19 | async-start | bytes 1327104 | tf_op jit(solution)/shard_map/reduce_scatter | solution.py:716
  225.3 68.6 %copy-start.17 = (bf16[2,256,768]{2,1,0:T(8,128)(2,1)S(1)}, bf16[2,256,768]{2,1,0:T(8,128)(2,1)}, u32[]{:S(2)}) copy-start(bf16[2,256,768]{2,1,0:T(8,128)(2,1)} %param.32) | copy-start | bytes 2359300
  297.5 1.7 copy-start.19
  301.1 129.2 %reduce-scatter.21.cloned.1.call-start = ((), (), s32[]{:S(2)}) async-start(), calls=%async_computation.21 | async-start | bytes 1327104 | tf_op jit(solution)/shard_map/reduce_scatter | solution.py:716
  307.7 188.9 %reduce-scatter.23.cloned.1.call-start = ((), (), s32[]{:S(2)}) async-start(), calls=%async_computation.22 | async-start | bytes 1327104 | tf_op jit(solution)/shard_map/reduce_scatter | solution.py:716
  315.6 215.4 %all-reduce.12.cloned.1.call-start = ((), (), s32[]{:S(2)}) async-start(), calls=%async_computation.20 | async-start | bytes 786432 | tf_op jit(solution)/shard_map/psum | solution.py:727
  335.0 2.4 copy-start.10
  371.6 227.3 %reduce-scatter.17.cloned.1.call-start = ((), (), s32[]{:S(2)}) async-start(), calls=%async_computation.18 | async-start | bytes 1327104 | tf_op jit(solution)/shard_map/reduce_scatter | solution.py:716
  371.9 7.7 copy-start.13
  379.5 260.5 %reduce-scatter.15.cloned.1.call-start = ((), (), s32[]{:S(2)}) async-start(), calls=%async_computation.17 | async-start | bytes 3932160 | tf_op jit(solution)/shard_map/reduce_scatter | solution.py:674
  385.6 2.6 copy-start.24
  640.0 21.5 %copy-start.18 = (bf16[2,256,768]{2,1,0:T(8,128)(2,1)S(1)}, bf16[2,256,768]{2,1,0:T(8,128)(2,1)}, u32[]{:S(2)}) copy-start(bf16[2,256,768]{2,1,0:T(8,128)(2,1)} %reduce-scatter.15.cloned.1.call-done) | copy-start | bytes 2359300
  654.9 73.2 %all-to-all-start.2 = ((bf16[2,8,576]{2,0,1:T(2,128)(2,1)}), bf16[2,8,576]{2,0,1:T(2,128)(2,1)S(1)}, u32[]{:S(2)}, u32[]{:S(2)}) async-start(bf16[2,8,576]{2,0,1:T(2,128)(2,1)} %copy.91), calls=%async_computation.5 | async-start | bytes 40960 | tf_op jit(solution)/shard_map/all_to_all | solution.py:705
  660.4 64.9 %reduce-scatter.25.cloned.1.call-start = ((), (), s32[]{:S(2)}) async-start(), calls=%async_computation.23 | async-start | bytes 442368
  661.5 66.7 %copy-start.20 = (bf16[128,576]{0,1:T(8,128)(2,1)S(1)}, bf16[128,576]{0,1:T(8,128)(2,1)}, u32[]{:S(2)}) copy-start(bf16[128,576]{0,1:T(8,128)(2,1)} %param.22) | copy-start | bytes 442372
  661.5 112.4 %copy-start.1 = (bf16[768,384]{1,0:T(8,128)(2,1)S(1)}, bf16[768,384]{1,0:T(8,128)(2,1)}, u32[]{:S(2)}) copy-start(bf16[768,384]{1,0:T(8,128)(2,1)} %param.28) | copy-start | bytes 1769476
  (10 other events, 10.4 us)
Sparse Core Ops, SparseCore 0:
  9.6 44.7 all-gather.14
  57.2 43.6 all-gather.10
  131.7 28.5 all-gather.8
  163.0 39.3 all-gather.12
  215.4 37.9 reduce-scatter.12
  255.9 37.9 reduce-scatter.10
  301.2 62.4 reduce-scatter.18
  367.1 63.1 reduce-scatter.20
  433.6 62.9 reduce-scatter.22
  499.4 31.5 all-reduce.11
  534.8 64.0 reduce-scatter.16
  601.5 38.4 reduce-scatter.14
  664.5 60.7 reduce-scatter.24

commit v3 on v1

v3 whole, which is shorter than its diff:
```python
import functools
import math

import jax
import jax.numpy as jnp
import numpy as np
from jax import lax
from jax.experimental import pallas as pl
from jax.experimental.pallas import tpu as pltpu
from jax.sharding import PartitionSpec as P

HEAD = 64
EPS = 1e-05
ROPE_BASE = 10000.0
MASKED = -1e30
F32 = jnp.float32
BF16 = jnp.bfloat16

NN = (((1,), (0,)), ((), ()))
NT = (((1,), (1,)), ((), ()))
TN = (((0,), (0,)), ((), ()))


def mm(a, b, dims):
    return lax.dot_general(a, b, dims, preferred_element_type=F32)


def rope_table(length):
    inverse = ROPE_BASE ** (-2.0 * np.arange(HEAD // 2) / HEAD)
    angles = np.arange(length)[:, None] * inverse[None, :]
    cosine = np.concatenate([np.cos(angles)] * 2, axis=1)
    sine = np.concatenate([-np.sin(angles), np.sin(angles)], axis=1)
    return cosine.astype(np.float32), sine.astype(np.float32)


def swap_halves(v):
    half = HEAD // 2
    return jnp.concatenate([v[..., half:], v[..., :half]], axis=-1)


MESH = pl.DeviceIdType.MESH
VM = pl.BlockSpec(memory_space=pltpu.VMEM)
ANY = pl.BlockSpec(memory_space=pl.ANY)
LIMIT = 63 << 20


def round16(size):
    return -(-size // 16) * 16


def iota(shape, dim):
    return lax.broadcasted_iota(jnp.int32, shape, dim)


def greet(peers, meanwhile=None):
    barrier = pltpu.get_barrier_semaphore()
    for peer in peers:
        pl.semaphore_signal(barrier, inc=1, device_id=peer, device_id_type=MESH)
    if meanwhile is not None:
        meanwhile()
    pl.semaphore_wait(barrier, len(peers))


def push(src, dst, send, recv, peer):
    return pltpu.make_async_remote_copy(
        src_ref=src,
        dst_ref=dst,
        send_sem=send,
        recv_sem=recv,
        device_id=peer,
        device_id_type=MESH,
    )


class Place:
    def __init__(self, n, m):
        self.n, self.m = n, m
        self.f = lax.axis_index("fsdp")
        self.d = lax.axis_index("dp")
        self.lines = n // 2
        self.a = self.f // 2
        self.b = self.f % 2
        self.x = self.d // 2
        self.c = self.d % 2
        self.sib_d = self.x * 2 + 1 - self.c
        self.far_d = (1 - self.x) * 2 + self.c
        self.diag_d = (1 - self.x) * 2 + 1 - self.c
        self.sib = (self.f, self.sib_d)
        self.far = (self.f, self.far_d)
        self.diag = (self.f, self.diag_d)
        self.side = (self.a * 2 + 1 - self.b, self.d)
        last = self.lines - 1
        self.right = (jnp.minimum(self.a + 1, last) * 2 + self.b, self.d)
        self.left = (jnp.maximum(self.a - 1, 0) * 2 + self.b, self.d)
        self.has_right = self.a < last
        self.has_left = self.a > 0

    def ring_f(self, step):
        return (self.f + step + self.n) % self.n

    def ring(self):
        return [(self.ring_f(i), self.d) for i in range(1, self.n)]

    def line_peers(self):
        return [((self.a + i) % self.lines * 2 + self.b, self.d) for i in range(1, self.lines)] + [
            self.side
        ]


class Gather:
    def __init__(self, p, src, slot, sems):
        self.p, self.src, self.slot = p, src, slot
        self.zs, self.zr, self.ys, self.yr = [sems.at[k] for k in range(4)]

    def line_copy(self, way, t):
        p = self.p
        block = self.slot(jnp.clip(p.a + (t if way else -t), 0, p.lines - 1) * 2 + p.b)
        return push(
            self.src if t == 0 else block,
            block,
            self.zs.at[way, t],
            self.zr.at[way, t + 1],
            p.left if way else p.right,
        )

    def line_wait(self, way, t):
        p = self.p
        block = self.slot(jnp.clip(p.a + (t if way else -t), 0, p.lines - 1) * 2 + p.b)
        push(block, block, self.zs.at[way, t], self.zr.at[way, t], p.left if way else p.right).wait_recv()

    def side_copy(self, way, t, theirs=False):
        p = self.p
        b = 1 - p.b if theirs else p.b
        block = self.slot(jnp.clip(p.a + (t if way else -t), 0, p.lines - 1) * 2 + b)
        return push(
            self.src if t == 0 else block, block, self.ys.at[way, t], self.yr.at[way, t], p.side
        )

    def held(self, way, t):
        p = self.p
        return p.a + t < p.lines if way else p.a - t >= 0

    def onward(self, way):
        return self.p.has_left if way else self.p.has_right

    def start(self):
        for way in range(2):
            pl.when(self.onward(way))(lambda way=way: self.line_copy(way, 0).start())
        self.side_copy(0, 0).start()

    def step(self, t):
        for way in range(2):

            @pl.when(self.held(way, t))
            def _(way=way):
                self.line_wait(way, t)
                if t < self.p.lines - 1:
                    pl.when(self.onward(way))(lambda: self.line_copy(way, t).start())
                self.side_copy(way, t).start()

    def finish(self):
        self.side_copy(0, 0, True).wait_recv()
        for t in range(1, self.p.lines):
            for way in range(2):
                pl.when(self.held(way, t))(
                    lambda way=way, t=t: self.side_copy(way, t, True).wait_recv()
                )

    def drain(self):
        self.side_copy(0, 0).wait_send()
        for way in range(2):
            pl.when(self.onward(way))(lambda way=way: self.line_copy(way, 0).wait_send())
        for t in range(1, self.p.lines):
            for way in range(2):

                @pl.when(self.held(way, t))
                def _(way=way, t=t):
                    if t < self.p.lines - 1:
                        pl.when(self.onward(way))(lambda: self.line_copy(way, t).wait_send())
                    self.side_copy(way, t).wait_send()


class Both:
    def __init__(self, *gathers):
        self.gathers = gathers

    def start(self):
        for g in self.gathers:
            g.start()

    def step(self, t):
        for g in self.gathers:
            g.step(t)

    def finish(self):
        for g in self.gathers:
            g.finish()

    def drain(self):
        for g in self.gathers:
            g.drain()


def gather_halves(p, src, buf, sems):
    rows = src.shape[0]
    if rows % 32:
        return Gather(p, src, lambda f: buf.at[f], sems.at[0])
    cut = [pl.ds(h * rows // 2, rows // 2) for h in range(2)]
    return Both(
        *[Gather(p, src.at[cut[h]], lambda f, h=h: buf.at[f, cut[h]], sems.at[h]) for h in range(2)]
    )


class Reduce:
    def __init__(self, p, src, side, total, zrecv, sems, summed=False):
        self.p, self.src, self.side, self.total = p, src, side, total
        self.zrecv, self.summed = zrecv, summed
        self.ys, self.yr, self.zs, self.zr = [sems.at[k] for k in range(4)]

    def order(self):
        lines = self.p.lines
        return [j for k in range(lines // 2) for j in (lines - 1 - k, k)]

    def side_copy(self, j):
        p = self.p
        return push(self.src(2 * j + 1 - p.b), self.side.at[j], self.ys.at[0, j], self.yr.at[0, j], p.side)

    def line_copy(self, way, j):
        p = self.p
        at = jnp.where(j == p.a - 1, p.lines, j) if way else j
        return push(
            self.total.at[j],
            self.zrecv.at[at],
            self.zs.at[way, j],
            self.zr.at[way, j],
            p.left if way else p.right,
        )

    def line_wait(self, way, j):
        p = self.p
        at = jnp.where(j == p.a, p.lines, j) if way else j
        block = self.zrecv.at[at]
        push(block, block, self.zs.at[way, j], self.zr.at[way, j], p.left if way else p.right).wait_recv()
        return block[...].astype(F32)

    def start(self):
        for j in self.order():
            self.side_copy(j).start()

    def side_sum(self, j):
        p = self.p
        self.side_copy(j).wait_recv()
        mine = self.src(2 * j + p.b)[...].astype(F32)
        self.total[j] = (mine + self.side[j].astype(F32)).astype(BF16)

    def step(self, t):
        p = self.p
        if 2 * t < p.lines and not self.summed:
            for j in self.order()[2 * t : 2 * t + 2]:
                self.side_sum(j)
        for way in range(2):
            j = t - (p.lines - 1 - p.a) if way else p.lines - 1 - (t - p.a)
            ahead = (j >= 0) & (j < p.a) if way else (j < p.lines) & (j > p.a)
            behind = p.has_right if way else p.has_left

            @pl.when(ahead)
            def _(way=way, j=j, behind=behind):
                @pl.when(behind)
                def _():
                    arrived = self.line_wait(way, j)
                    self.total[j] = (self.total[j].astype(F32) + arrived).astype(BF16)

                self.line_copy(way, j).start()

    def own(self, out):
        p = self.p
        for way in range(2):

            @pl.when(p.has_right if way else p.has_left)
            def _(way=way):
                arrived = self.line_wait(way, p.a)
                self.total[p.a] = (self.total[p.a].astype(F32) + arrived).astype(BF16)

        out[...] = self.total[p.a]

    def drain(self):
        p = self.p
        for j in range(p.lines):
            if not self.summed:
                self.side_copy(j).wait_send()
            for way in range(2):
                ahead = p.a > j if way else p.a < j
                pl.when(ahead)(lambda way=way, j=j: self.line_copy(way, j).wait_send())


class Spread:
    def __init__(self, p, buf, send, recv):
        self.p, self.buf, self.send, self.recv = p, buf, send, recv

    def copy(self, kind):
        p = self.p
        block = self.buf.at[p.far_d if kind == 2 else p.d]
        return push(block, block, self.send.at[kind], self.recv.at[kind], p.far if kind == 1 else p.sib)

    def start(self):
        self.copy(1).start()
        self.copy(0).start()

    def forward(self):
        self.copy(1).wait_recv()
        self.copy(2).start()

    def finish(self):
        self.copy(0).wait_recv()
        self.copy(2).wait_recv()

    def drain(self):
        for kind in range(3):
            self.copy(kind).wait_send()


def norm_rows(stream):
    average = jnp.mean(stream, axis=-1, keepdims=True)
    centered = stream - average
    variance = jnp.mean(centered * centered, axis=-1, keepdims=True)
    inverse = lax.rsqrt(variance + EPS)
    return centered * inverse, inverse


def norm_back(grad, normal, inverse, factor):
    e = grad * factor
    mean_e = jnp.mean(e, axis=-1, keepdims=True)
    mean_en = jnp.mean(e * normal, axis=-1, keepdims=True)
    return inverse * (e - mean_e - normal * mean_en)


def turned(v):
    lanes = iota(v.shape, 1)
    half = HEAD // 2
    return jnp.where(lanes % HEAD < half, pltpu.roll(v, 128 - half, 1), pltpu.roll(v, half, 1))


def gelu_parts(h):
    root = math.sqrt(2.0 / math.pi)
    square = h * h
    t = jnp.tanh(root * h * (1.0 + 0.044715 * square))
    half = 0.5 * (1.0 + t)
    slope = half + 0.5 * h * (1.0 - t * t) * (root * (1.0 + 3.0 * 0.044715 * square))
    return h * half, slope


def compact(blocks, per):
    count, rows, lanes = blocks.shape
    flat = blocks.reshape(count * rows, lanes)
    if rows == per:
        return flat
    want = iota((count * per, count * rows), 0)
    have = iota((count * per, count * rows), 1)
    chosen = (have == want // per * rows + want % per).astype(BF16)
    return mm(chosen, flat, NN).astype(BF16)


def as_column(row):
    size = row.shape[1]
    return jnp.transpose(jnp.broadcast_to(row, (128, size)))[:, :1]


def front_kernel(
    n,
    m,
    per,
    tile,
    tok_ref,
    cot_ref,
    cond_ref,
    seg_ref,
    wada_ref,
    bada_ref,
    bup_ref,
    ga_ref,
    gm_ref,
    bdown_ref,
    wqkv_ref,
    wout_ref,
    wup_ref,
    take_ref,
    place_ref,
    cos_ref,
    sin_ref,
    qkv_out,
    normed_out,
    att_out,
    own_out,
    log_out,
    cotfar_out,
    wout_out,
    up_out,
    mod_ref,
    vecs_ref,
    wqkvt_ref,
    vec_out,
    qkv_ref,
    normed_ref,
    tall_ref,
    att_v,
    arecv,
    log_v,
    cotfar_v,
    mod_send,
    mod_recv,
    vsrc,
    vbuf,
    qsrc,
    qbuf,
    osrc,
    obuf,
    usrc,
    ubuf,
    vs,
    vr,
    ms,
    mr,
    gz,
    ts,
    tr,
    os_,
    or_,
    as_,
    ar,
    cs,
    cr,
    local,
):
    p = Place(n, m)
    slots, quarter, width = tok_ref.shape
    half = quarter // 2
    part = width // m
    heads = part // HEAD
    hidden_per, small = per
    pad = round16(hidden_per)
    halves = obuf.shape[1]
    length = m * quarter
    peers = (p.sib, p.far, p.diag)
    ranks = (p.sib_d, p.far_d, p.diag_d)
    own_tokens = pltpu.make_async_copy(tok_ref, tall_ref.at[p.d], local.at[2, 0])
    own_tokens.start()
    log_v[...] = jnp.zeros_like(log_v)

    def prepare():
        vsrc[...] = jnp.zeros_like(vsrc)
        for row, ref in enumerate((bup_ref, ga_ref, gm_ref, bdown_ref)):
            vsrc[row : row + 1, : ref.shape[1]] = ref[...]
        vsrc[4 : 4 + slots, : cond_ref.shape[1]] = cond_ref[...]
        columns = wqkv_ref.shape[0]
        most = qsrc.shape[0]
        taking = take_ref[pl.ds(p.f * m + p.d, 1), :]
        chosen = (iota((columns, most), 0) == taking).astype(BF16)
        qsrc[...] = mm(chosen, wqkv_ref[...], TN).astype(BF16)

    greet(list(peers) + p.ring(), prepare)

    def vec_copy(i):
        return push(vsrc, vbuf.at[p.f], vs.at[i], vr.at[i], (p.ring_f(i), p.d))

    for i in range(1, n):
        vec_copy(i).start()

    def token_copy(kind, k):
        s, rows = k // 2, pl.ds(k % 2 * half, half)
        if kind == 2:
            block = tall_ref.at[p.far_d, s, rows]
            return push(block, block, ts.at[kind, k], tr.at[kind, k], p.sib)
        return push(
            tok_ref.at[s, rows],
            tall_ref.at[p.d, s, rows],
            ts.at[kind, k],
            tr.at[kind, k],
            p.sib if kind == 0 else p.far,
        )

    qry = gather_halves(p, qsrc, qbuf, gz.at[0])
    qry.start()
    for k in range(2 * slots):
        token_copy(1, k).start()
    for k in range(2 * slots):
        token_copy(0, k).start()
    vbuf[p.f] = vsrc[...]
    qbuf[p.f] = qsrc[...]

    lane = iota((1, width), 1)
    rank, inner = lane // part, lane % part
    want = (inner // HEAD * m + rank) * HEAD + inner % HEAD
    chosen = (iota((width, width), 0) == want).astype(BF16)
    got = mm(wout_ref[...], chosen, NN).astype(BF16)
    if small < osrc.shape[0]:
        got = jnp.concatenate([got, jnp.zeros((osrc.shape[0] - small, width), BF16)])
    osrc[...] = got
    split = osrc.shape[0] // halves
    mine = p.c if halves == 2 else 0
    out = Gather(
        p,
        osrc.at[pl.ds(pl.multiple_of(mine * split, 16), split)],
        lambda f: obuf.at[f, mine],
        gz.at[1, 0],
    )
    for h in range(halves):
        obuf[p.f, h] = osrc[h * split : (h + 1) * split]

    ups = wup_ref.shape[1]
    at, lane = iota((pad, ups), 0), iota((pad, ups), 1)
    chosen = ((lane == at + p.d * hidden_per) & (at < hidden_per)).astype(BF16)
    usrc[...] = mm(chosen, wup_ref[...], NT).astype(BF16)
    ubuf[p.f] = usrc[...]
    up = gather_halves(p, usrc, ubuf, gz.at[2])

    def pass_on(k):
        token_copy(1, k).wait_recv()
        token_copy(2, k).start()

    for i in range(1, n):
        vec_copy(i).wait_recv()
    vecs = vbuf[...].reshape(n * 16, width)
    mod_cols = mm(vecs[:, : cond_ref.shape[1]], wada_ref[...], NT) + bada_ref[...].astype(F32)
    mod_send[...] = mod_cols.reshape(n, 16, mod_cols.shape[1])[:, :8]
    mod_recv[p.f] = mod_send[p.f]

    def mod_copy(i):
        peer = p.ring_f(i)
        return push(mod_send.at[peer], mod_recv.at[p.f], ms.at[i], mr.at[i], (peer, p.d))

    for i in range(1, n):
        mod_copy(i).start()
    vec_out[...] = vbuf[...]
    vecs_ref[...] = jnp.zeros_like(vecs_ref)
    mine_up = (iota((ups, pad), 0) == iota((ups, pad), 1) + p.d * hidden_per) & (
        iota((ups, pad), 1) < hidden_per
    )
    b_up = mm(vecs[:, :ups], mine_up.astype(BF16), NN)
    for g in range(n):
        vecs_ref[0:1, g * pad : (g + 1) * pad] = b_up[16 * g : 16 * g + 1]
        rest = vecs[16 * g : 16 * g + 8].astype(F32)
        for k in range(1, 4):
            vecs_ref[k : k + 1, g * small : (g + 1) * small] = rest[k : k + 1, :small]
    qry.step(1)
    pass_on(0)
    for i in range(1, n):
        mod_copy(i).wait_recv()
    cols = mod_cols.shape[1]
    for g in range(n):
        for s in range(slots):
            mod_ref[s, :, g * cols : (g + 1) * cols] = mod_recv[g, 4 + s : 5 + s]
    gain = vecs_ref[1:2, :width]

    for k in range(2, p.lines - 1):
        qry.step(k)
    out.start()
    pass_on(1)
    qry.step(p.lines - 1)
    pass_on(2)
    def cot_copy(s):
        return push(cot_ref.at[s], cotfar_v.at[s], cs.at[s], cr.at[s], p.far)

    for s in range(slots):
        cot_copy(s).start()

    qry.finish()
    up.start()
    count = n * qsrc.shape[0]
    placing = (iota((3 * part, count), 0) == place_ref[pl.ds(p.d, 1), :]).astype(BF16)
    wqkvt_ref[...] = mm(placing, qbuf[...].reshape(count, width), NN).astype(BF16)
    own_tokens.wait()

    def chunk(i):
        q = jnp.where(
            i < 2, p.d, jnp.where(i < 4, p.sib_d, jnp.where(i % 2 == 0, p.far_d, p.diag_d))
        )
        s = jnp.where(i < 4, i % 2, (i - 4) // 2)
        return q, s, pl.ds(pl.multiple_of(q * quarter, quarter), quarter)

    def keeps(i):
        _, s, rows = chunk(i)
        return [
            pltpu.make_async_copy(src.at[s, rows], dst.at[s, rows], local.at[k, i])
            for k, (src, dst) in enumerate(((qkv_ref, qkv_out), (normed_ref, normed_out)))
        ]

    @pl.loop(0, m * slots)
    def _(i):
        for k in range(2):

            @pl.when(i == 2 + k)
            def _(k=k):
                token_copy(0, 2 * k).wait_recv()
                token_copy(0, 2 * k + 1).wait_recv()

            @pl.when(i == 5 + 2 * k)
            def _(k=k):
                token_copy(2, 2 * k).wait_recv()
                token_copy(2, 2 * k + 1).wait_recv()

        pl.when(i == 2)(lambda: out.step(1))
        pl.when(i == 4)(lambda: pass_on(3))

        q, s, rows = chunk(i)
        normal, _ = norm_rows(tall_ref[q, s].astype(F32))
        shift = mod_ref[s, :, :width]
        scale = mod_ref[s, :, width : 2 * width]
        normed = (normal * (gain * (1.0 + scale)) + shift).astype(BF16)
        normed_ref[s, rows, :] = normed
        got = mm(normed, wqkvt_ref[...], NT)
        cosine = cos_ref[rows, :]
        sine = sin_ref[rows, :]
        lanes = iota((quarter, 128), 1)
        for t in range(0, 2 * part, 128):
            piece = got[:, t : t + 128]
            piece = piece * cosine + turned(piece) * sine
            piece = jnp.where(lanes + t < part, piece * (1.0 / math.sqrt(HEAD)), piece)
            qkv_ref[s, rows, t : t + 128] = piece.astype(BF16)
        qkv_ref[s, rows, 2 * part :] = got[:, 2 * part :].astype(BF16)
        for keep in keeps(i):
            keep.start()

    def att_copy(kind, s):
        return push(
            att_v.at[s, ranks[kind]], arecv.at[s, p.d], as_.at[kind, s], ar.at[kind, s], peers[kind]
        )

    for k in range(2, p.lines):
        out.step(k)
    up.step(1)
    tiles = length // tile

    @pl.loop(0, slots * tiles)
    def _(i):
        s = i // tiles
        rows = pl.ds(pl.multiple_of(i % tiles * tile, tile), tile)
        same = as_column(seg_ref[pl.ds(s, 1), :]) == seg_ref[pl.ds(s, 1), rows]
        ones = jnp.ones((length, HEAD), BF16)
        for h in range(heads):
            at = h * HEAD
            q = qkv_ref[s, rows, at : at + HEAD]
            k = qkv_ref[s, :, part + at : part + at + HEAD]
            v = qkv_ref[s, :, 2 * part + at : 2 * part + at + HEAD]
            scores = jnp.where(same, mm(k, q, NT), MASKED)
            largest = jnp.max(scores, axis=0, keepdims=True)
            weights = jnp.exp(scores - largest)
            log_v[s, h : h + 1, rows] = largest + jnp.log(jnp.sum(weights, axis=0, keepdims=True))
            result = mm(weights.astype(BF16), jnp.concatenate([v, ones], axis=1), TN)
            result = (result[:, :HEAD] / result[:, HEAD : HEAD + 1]).astype(BF16)
            for j in range(tile // half):
                att_v[s, i % tiles * (tile // quarter) + j // 2, :, j % 2 * part + at : j % 2 * part + at + HEAD] = (
                    result[j * half : (j + 1) * half]
                )
        for k in range(2, p.lines):
            pl.when(i == k - 2)(lambda k=k: up.step(k))
        for k in range(slots):

            @pl.when(i == (k + 1) * tiles - 1)
            def _(k=k):
                for kind in (2, 1, 0):
                    att_copy(kind, k).start()

    for k in range(slots * tiles + 2, p.lines):
        up.step(k)
    stores = [
        pltpu.make_async_copy(src, dst, local.at[2, 1 + k])
        for k, (src, dst) in enumerate(
            (
                (att_v, att_out),
                (log_v, log_out),
                (obuf, wout_out),
                (ubuf, up_out),
                (cotfar_v, cotfar_out),
                (arecv, own_out),
            )
        )
    ]
    for k in range(2):
        stores[k].start()
    for s in range(slots):
        arecv[s, p.d] = att_v[s, p.d]
    out.finish()
    if halves == 2:

        def swap(h):
            return push(obuf.at[:, h], obuf.at[:, h], os_.at[0], or_.at[0], p.sib)

        swap(p.c).start()
        swap(1 - p.c).wait_recv()
    stores[2].start()
    up.finish()
    stores[3].start()
    for s in range(slots):
        cot_copy(s).wait_recv()
    stores[4].start()
    for s in range(slots):
        for kind in range(3):
            att_copy(kind, s).wait_recv()
    stores[5].start()

    for i in range(1, n):
        vec_copy(i).wait_send()
        mod_copy(i).wait_send()
    for item in (qry, out, up):
        item.drain()
    if halves == 2:
        swap(p.c).wait_send()
    for k in range(2 * slots):
        for kind in range(3):
            token_copy(kind, k).wait_send()
    for s in range(slots):
        cot_copy(s).wait_send()
        for kind in range(3):
            att_copy(kind, s).wait_send()

    @pl.loop(0, m * slots)
    def _(i):
        for keep in keeps(i):
            keep.wait()

    for copy in stores:
        copy.wait()


def front(n, m, length, tile, most, args):
    tokens, cond = args[0], args[2]
    w_ada, b_up, w_up = args[4], args[6], args[12]
    slots, quarter, width = tokens.shape
    part = width // m
    lines = n // 2
    dma = pltpu.SemaphoreType.DMA
    shape = jax.ShapeDtypeStruct
    vmem = pltpu.VMEM
    hidden_per = b_up.shape[1] // m
    small = width // n
    block = round16(small)
    pad = round16(hidden_per)
    halves = 2 if block % 32 == 0 else 1
    rows = (slots, quarter, width)
    att = (slots, m, quarter // 2, 2 * part)
    return pl.pallas_call(
        functools.partial(front_kernel, n, m, (hidden_per, small), tile),
        out_shape=(
            shape((slots, length, 3 * part), BF16),
            shape((slots, length, width), BF16),
            shape(att, BF16),
            shape(att, BF16),
            shape((slots, 8, length), F32),
            shape(rows, BF16),
            shape((n, halves, block // halves, width), BF16),
            shape((n, pad, width), BF16),
            shape((slots, 1, 6 * width), F32),
            shape((8, max(width, n * pad)), F32),
            shape((3 * part, width), BF16),
            shape((n, 16, width), BF16),
        ),
        in_specs=[ANY] * 2 + [VM] * (len(args) - 2),
        out_specs=(ANY,) * 8 + (VM,) * 4,
        scratch_shapes=[
            vmem((slots, length, 3 * part), BF16),
            vmem((slots, length, width), BF16),
            vmem((m,) + rows, BF16),
            vmem(att, BF16),
            vmem(att, BF16),
            vmem((slots, 8, length), F32),
            vmem(rows, BF16),
            vmem((n, 8, w_ada.shape[0]), F32),
            vmem((n, 8, w_ada.shape[0]), F32),
            vmem((16, width), BF16),
            vmem((n, 16, width), BF16),
            vmem((most, width), BF16),
            vmem((n, most, width), BF16),
            vmem((block, width), BF16),
            vmem((n, halves, block // halves, width), BF16),
            vmem((pad, width), BF16),
            vmem((n, pad, width), BF16),
            dma((n,)),
            dma((n,)),
            dma((n,)),
            dma((n,)),
            dma((3, 2, 4, 2, lines)),
            dma((3, 2 * slots)),
            dma((3, 2 * slots)),
            dma((1,)),
            dma((1,)),
            dma((3, slots)),
            dma((3, slots)),
            dma((slots,)),
            dma((slots,)),
            dma((3, m * slots)),
        ],
        compiler_params=pltpu.CompilerParams(
            collective_id=1, has_side_effects=True, vmem_limit_bytes=LIMIT
        ),
        name="front",
    )(*args)


def middle_kernel(
    n,
    m,
    tok_ref,
    cot_ref,
    cotfar_ref,
    att_ref,
    wout_ref,
    up_ref,
    mod_ref,
    vec_ref,
    wdown_ref,
    gm_out,
    base_out,
    xsend_out,
    gatt_out,
    dwu_out,
    downtotal_out,
    outsum_out,
    dbup_ref,
    sums_ref,
    tok_v,
    cot_v,
    wout_v,
    arecv,
    own_ref,
    br_ref,
    mid_ref,
    nrm_ref,
    inv_ref,
    nm_ref,
    ct_ref,
    act_ref,
    gp_ref,
    drow,
    ubuf,
    dbuf,
    down_v,
    gsc,
    psend,
    precv,
    xs_ref,
    xr_ref,
    gn_ref,
    bo_ref,
    gba_ref,
    gm_ref,
    xsend_ref,
    gsend,
    grecv,
    dwd_ref,
    dwu_ref,
    dwo_ref,
    oswap,
    side_d,
    total_d,
    n_s,
    n_r,
    c_s,
    c_r,
    gz,
    p_s,
    p_r,
    g_s,
    g_r,
    rz,
    o_s,
    o_r,
    local,
):
    p = Place(n, m)
    slots, quarter, width = tok_ref.shape
    half = quarter // 2
    part = width // m
    small = wdown_ref.shape[0]
    block, inner = drow.shape
    pad = ubuf.shape[1]
    hidden_per = wdown_ref.shape[1] // (n * m)
    peers = (p.sib, p.far, p.diag)
    ranks = (p.sib_d, p.far_d, p.diag_d)

    loads = [
        pltpu.make_async_copy(src, dst, local.at[k])
        for k, (src, dst) in enumerate(
            (
                (att_ref, arecv),
                (wout_ref, wout_v),
                (tok_ref, tok_v),
                (up_ref, ubuf),
                (cot_ref, ct_ref.at[p.d]),
                (cotfar_ref, ct_ref.at[p.far_d]),
                (cot_ref, cot_v),
            )
        )
    ]
    for load in loads:
        load.start()

    def prepare():
        row, lane = iota((wdown_ref.shape[1], inner), 0), iota((1, inner), 1)
        want = jnp.where(
            lane % pad < hidden_per, (lane // pad * m + p.d) * hidden_per + lane % pad, -1
        )
        got = mm(wdown_ref[...], (row == want).astype(BF16), NN).astype(BF16)
        if small < block:
            got = jnp.concatenate([got, jnp.zeros((block - small, inner), BF16)])
        drow[...] = got

    greet(list(peers) + p.line_peers(), prepare)
    down = gather_halves(p, drow, dbuf, gz)
    down.start()

    def cot_copy(kind, s):
        src = cot_ref if kind == 0 else cotfar_ref
        at = p.d if kind == 0 else p.far_d
        return push(src.at[s], ct_ref.at[at, s], c_s.at[kind, s], c_r.at[kind, s], p.sib)

    dbuf[p.f] = drow[...]

    def group(s, k):
        return mod_ref[s, :, k * width : (k + 1) * width]

    gain = vec_ref[2:3, :width]
    b_down = vec_ref[3:4, :width]
    b_up = vec_ref[0:1, :inner]

    def nm_copy(kind, s, h):
        k = s * 2 + h
        at = p.far_d if kind == 2 else p.d
        block = nm_ref.at[at, s, pl.ds(h * half, half)]
        return push(block, block, n_s.at[kind, k], n_r.at[kind, k], p.far if kind == 1 else p.sib)

    for k in range(3):
        loads[k].wait()

    @pl.loop(0, slots)
    def _(s):
        for r in range(m):
            for h in range(2):
                own_ref[s, h * half : (h + 1) * half, r * part : (r + 1) * part] = arecv[
                    s, r, :, h * part : (h + 1) * part
                ]
        branch = mm(own_ref[s], wout_v[...], NT)
        br_ref[s] = branch
        middle = tok_v[s].astype(F32) + group(s, 2) * branch
        mid_ref[s] = middle
        normal, inverse = norm_rows(middle)
        nrm_ref[s] = normal
        inv_ref[s] = inverse
        nm_ref[p.d, s] = (normal * (gain * (1.0 + group(s, 4))) + group(s, 3)).astype(BF16)
        for kind in (1, 0):
            for h in range(2):
                nm_copy(kind, s, h).start()

    def pass_on(s):
        for h in range(2):
            nm_copy(1, s, h).wait_recv()
            nm_copy(2, s, h).start()

    def arrived(kind, s):
        for h in range(2):
            nm_copy(kind, s, h).wait_recv()

    w_up = lambda: ubuf[...].reshape(-1, width)

    def expand(q, s):
        hidden = mm(nm_ref[q, s], w_up(), NT) + b_up
        value, slope = gelu_parts(hidden)
        act_ref[q, s] = value.astype(BF16)
        gp_ref[q, s] = slope.astype(BF16)

    dbup_ref[...] = jnp.zeros_like(dbup_ref)

    def pull(q, s):
        g = (ct_ref[q, s].astype(F32) * group(s, 5)).astype(BF16)
        ct_ref[q, s] = g
        grad = (mm(g, down_v[...], NN) * gp_ref[q, s].astype(F32)).astype(BF16)
        gp_ref[q, s] = grad
        dbup_ref[0:1, :] += jnp.sum(grad.astype(F32), axis=0, keepdims=True)
        gsc[...] = mm(grad, w_up(), NN)

    def part_copy(kind, s):
        if kind == 4:
            return push(xs_ref.at[s], xr_ref.at[s], p_s.at[4, s], p_r.at[4, s], p.far)
        return push(psend.at[kind, s], precv.at[kind, s], p_s.at[kind, s], p_r.at[kind, s], p.sib)

    for k in range(3, 7):
        loads[k].wait()
    for s in range(slots):
        for kind in range(2):
            cot_copy(kind, s).start()

    @pl.loop(0, 2 * slots)
    def _(i):
        s = i % slots
        pl.when(i >= slots)(lambda: arrived(0, s))
        expand(jnp.where(i < slots, p.d, p.sib_d), s)

    down.step(1)
    for s in range(slots):
        for kind in range(2):
            cot_copy(kind, s).wait_recv()
    pass_on(0)
    for t in range(2, p.lines):
        down.step(t)
    down.finish()
    down_v[...] = compact(dbuf[...], small)

    @pl.loop(0, 2 * slots)
    def _(i):
        s = i // 2
        first = i % 2 == 0
        pl.when(first & (s > 0))(lambda: pass_on(s))
        pl.when(first)(lambda: arrived(2, s))
        q = jnp.where(first, p.diag_d, p.far_d)
        expand(q, s)
        pull(q, s)

        @pl.when(first)
        def _():
            psend[0, s] = gsc[...].astype(BF16)
            part_copy(0, s).start()

        @pl.when(jnp.logical_not(first))
        def _():
            part_copy(0, s).wait_recv()
            xs_ref[s] = (gsc[...] + precv[0, s].astype(F32)).astype(BF16)
            part_copy(4, s).start()


    @pl.loop(0, 2 * slots)
    def _(i):
        s = i // 2
        first = i % 2 == 0
        pull(jnp.where(first, p.sib_d, p.d), s)

        @pl.when(first)
        def _():
            psend[1, s] = gsc[...].astype(BF16)
            part_copy(1, s).start()

        @pl.when(jnp.logical_not(first))
        def _():
            gn_ref[s] = gsc[...]

    def weight_grad(left, right, out_ref):
        step = 256

        @pl.loop(0, left.shape[1] // step)
        def _(i):
            at = pl.ds(pl.multiple_of(i * step, step), step)
            out_ref[at, :] = mm(left[:, at], right[...], TN).astype(BF16)

    every = lambda ref: ref.reshape(m * slots * quarter, ref.shape[3])
    weight_grad(every(ct_ref), every(act_ref), dwd_ref.at[:width])
    if small < block:
        dwd_ref[...] = padded(dwd_ref[:width], n, block)
    dwd = dwd_ref.reshape(n, block, inner)
    red_down = Reduce(p, lambda f: dwd.at[f], side_d, total_d, None, rz)
    red_down.start()
    def grad_copy(kind, s):
        return push(
            gsend.at[s, ranks[kind]], grecv.at[s, p.d], g_s.at[kind, s], g_r.at[kind, s], peers[kind]
        )

    def leave(s):
        part_copy(1, s).wait_recv()
        part_copy(4, s).wait_recv()
        cot = cot_v[s].astype(F32)
        gn = gn_ref[s] + precv[1, s].astype(F32) + xr_ref[s].astype(F32)
        normal = nrm_ref[s]
        grad_middle = cot + norm_back(gn, normal, inv_ref[s], gain * (1.0 + group(s, 4)))
        gm_ref[s] = grad_middle
        gba = (grad_middle * group(s, 2)).astype(BF16)
        gba_ref[s] = gba
        gatt = mm(gba, wout_v[...], NN).astype(BF16)
        for r in range(m):
            for h in range(2):
                gsend[s, r, :, h * part : (h + 1) * part] = gatt[
                    h * half : (h + 1) * half, r * part : (r + 1) * part
                ]
        for kind in (2, 1, 0):
            grad_copy(kind, s).start()
        grecv[s, p.d] = gsend[s, p.d]
        total = lambda v: jnp.sum(v, axis=0, keepdims=True)
        sums_ref[s, 0:1, :] = total(gn)
        sums_ref[s, 1:2, :] = total(gn * normal)
        sums_ref[s, 3:4, :] = total(grad_middle * br_ref[s])
        sums_ref[s, 4:5, :] = total((cot * group(s, 5)).astype(BF16).astype(F32))
        sums_ref[s, 5:8, :] = jnp.zeros((3, width), F32)

    leave(0)
    weight_grad(every(gp_ref), every(nm_ref), dwu_ref)

    stores = []

    def store(src, dst):
        stores.append(pltpu.make_async_copy(src, dst, local.at[7 + len(stores)]))
        stores[-1].start()

    store(dwu_ref.reshape(n, pad, width), dwu_out)


    @pl.loop(0, 4 * slots)
    def _(i):
        s = i // 4
        j = i % 4
        q = jnp.where(
            j < 2, jnp.where(j == 0, p.diag_d, p.sib_d), jnp.where(j == 2, p.d, p.far_d)
        )
        gsc[...] = mm(act_ref[q, s], down_v[...], NT)

        @pl.when(j == 0)
        def _():
            psend[2, s] = gsc[...].astype(BF16)
            part_copy(2, s).start()

        @pl.when(j == 1)
        def _():
            psend[3, s] = gsc[...].astype(BF16)
            part_copy(3, s).start()

        @pl.when(j == 2)
        def _():
            bo_ref[s] = gsc[...]

        @pl.when(j == 3)
        def _():
            part_copy(2, s).wait_recv()
            xsend_ref[s] = (gsc[...] + precv[2, s].astype(F32)).astype(BF16)

    store(xsend_ref, xsend_out)
    for s in range(1, slots):
        leave(s)
    store(gm_ref, gm_out)
    flat = lambda ref: ref.reshape(slots * quarter, width)
    weight_grad(flat(gba_ref), flat(own_ref), dwo_ref.at[:width])
    if small < block:
        dwo_ref[...] = padded(dwo_ref[:width], n, block)
    rows = oswap.shape[1]
    dwo = dwo_ref.reshape(n, block // rows, rows, width)
    mine = p.c if rows < block else 0
    theirs = 1 - p.c if rows < block else 0
    swap = push(dwo.at[:, theirs], oswap, o_s.at[0], o_r.at[0], p.sib)
    swap.start()

    @pl.loop(0, slots)
    def _(s):
        part_copy(3, s).wait_recv()
        branch = bo_ref[s] + precv[3, s].astype(F32) + b_down
        mid_ref[s] = mid_ref[s] + group(s, 5) * branch
        sums_ref[s, 2:3, :] = jnp.sum(cot_v[s].astype(F32) * branch, axis=0, keepdims=True)

    store(mid_ref, base_out)
    for j in red_down.order():
        red_down.side_sum(j)
    store(total_d, downtotal_out)
    swap.wait_recv()
    oswap[...] = (dwo[:, mine].astype(F32) + oswap[...].astype(F32)).astype(BF16)
    store(oswap, outsum_out)
    for s in range(slots):
        for kind in range(3):
            grad_copy(kind, s).wait_recv()
    store(grecv, gatt_out)

    down.drain()
    for j in range(p.lines):
        red_down.side_copy(j).wait_send()
    swap.wait_send()
    for s in range(slots):
        for kind in range(3):
            grad_copy(kind, s).wait_send()
            for h in range(2):
                nm_copy(kind, s, h).wait_send()
        for kind in range(2):
            cot_copy(kind, s).wait_send()
        for kind in range(5):
            part_copy(kind, s).wait_send()
    for copy in stores:
        copy.wait()


def padded(rows, count, block):
    per = rows.shape[0] // count
    want = iota((count * block, rows.shape[0]), 0)
    have = iota((count * block, rows.shape[0]), 1)
    chosen = (have == want // block * per + want % block) & (want % block < per)
    return mm(chosen.astype(BF16), rows, NN).astype(BF16)


def middle(n, m, args):
    tokens, att, up_t, w_down = args[0], args[3], args[5], args[8]
    slots, quarter, width = tokens.shape
    dma = pltpu.SemaphoreType.DMA
    shape = jax.ShapeDtypeStruct
    rows = (slots, quarter, width)
    lines = n // 2
    pad = up_t.shape[1]
    block = round16(w_down.shape[0])
    inner = n * pad
    swapped = block // 2 if block % 32 == 0 else block
    vmem = pltpu.VMEM
    return pl.pallas_call(
        functools.partial(middle_kernel, n, m),
        out_shape=(
            shape(rows, F32),
            shape(rows, F32),
            shape(rows, BF16),
            shape(att.shape, BF16),
            shape((n, pad, width), BF16),
            shape((lines, block, inner), BF16),
            shape((n, swapped, width), BF16),
            shape((8, inner), F32),
            shape((slots, 8, width), F32),
        ),
        in_specs=[ANY] * 6 + [VM] * 3,
        out_specs=(ANY,) * 7 + (VM,) * 2,
        scratch_shapes=[
            vmem(rows, BF16),
            vmem(rows, BF16),
            vmem((width, width), BF16),
            vmem(att.shape, BF16),
            vmem(rows, BF16),
            vmem(rows, F32),
            vmem(rows, F32),
            vmem(rows, F32),
            vmem((slots, quarter, 1), F32),
            vmem((m,) + rows, BF16),
            vmem((m,) + rows, BF16),
            vmem((m, slots, quarter, inner), BF16),
            vmem((m, slots, quarter, inner), BF16),
            vmem((block, inner), BF16),
            vmem((n, pad, width), BF16),
            vmem((n, block, inner), BF16),
            vmem((width, inner), BF16),
            vmem((quarter, width), F32),
            vmem((4,) + rows, BF16),
            vmem((4,) + rows, BF16),
            vmem(rows, BF16),
            vmem(rows, BF16),
            vmem(rows, F32),
            vmem(rows, F32),
            vmem(rows, BF16),
            vmem(rows, F32),
            vmem(rows, BF16),
            vmem(att.shape, BF16),
            vmem(att.shape, BF16),
            vmem((n * block, inner), BF16),
            vmem((inner, width), BF16),
            vmem((n * block, width), BF16),
            vmem((n, swapped, width), BF16),
            vmem((lines, block, inner), BF16),
            vmem((lines, block, inner), BF16),
            dma((3, 2 * slots)),
            dma((3, 2 * slots)),
            dma((2, slots)),
            dma((2, slots)),
            dma((2, 4, 2, lines)),
            dma((5, slots)),
            dma((5, slots)),
            dma((3, slots)),
            dma((3, slots)),
            dma((4, 2, lines)),
            dma((1,)),
            dma((1,)),
            dma((16,)),
        ],
        compiler_params=pltpu.CompilerParams(
            collective_id=2, has_side_effects=True, vmem_limit_bytes=LIMIT
        ),
        name="middle",
    )(*args)


def back_kernel(
    n,
    m,
    per,
    tile,
    qkv_ref,
    grad_ref,
    att_ref,
    normed_ref,
    tok_ref,
    gm_ref,
    xsend_ref,
    cot_ref,
    dwu_ref,
    downtotal_ref,
    outsum_ref,
    log_ref,
    seg_ref,
    cos_ref,
    sin_ref,
    wqkvt_ref,
    mod_ref,
    vec_ref,
    sums_ref,
    vblk_ref,
    wada_ref,
    dbup_ref,
    place_ref,
    dtok_out,
    other_out,
    down_out,
    up_out,
    wo_out,
    q_out,
    dcond_ref,
    dwada_ref,
    dbada_ref,
    dvec_ref,
    qkv_v,
    grad_v,
    att_v,
    gq_v,
    dk_ref,
    dv_ref,
    normed_v,
    tok_v,
    gm_v,
    other_v,
    cot_v,
    dtok_v,
    gsc,
    psend,
    precv,
    xs_ref,
    xr_ref,
    gn_ref,
    dwq_ref,
    qblk,
    dwu_v,
    outsum_v,
    total_d,
    zrecv_d,
    side_u,
    total_u,
    zrecv_u,
    side_o,
    total_o,
    zrecv_o,
    side_q,
    total_q,
    zrecv_q,
    spr_d,
    spr_u,
    spr_q,
    opiece,
    ofar,
    ofin,
    ssend,
    srecv,
    gsend,
    grecv,
    vsend,
    vrecv,
    dsend,
    drecv,
    p_s,
    p_r,
    rz,
    d_s,
    d_r,
    s_s,
    s_r,
    g_s,
    g_r,
    v_s,
    v_r,
    c_s,
    c_r,
    x_s,
    x_r,
    local,
):
    p = Place(n, m)
    hidden_per, small = per
    slots, quarter, width = tok_ref.shape
    length = m * quarter
    half = quarter // 2
    part = width // m
    heads = part // HEAD
    lines = p.lines
    peers = (p.sib, p.far, p.diag)
    loads = [
        pltpu.make_async_copy(src, dst, local.at[k])
        for k, (src, dst) in enumerate(
            (
                (qkv_ref, qkv_v),
                (grad_ref, grad_v),
                (att_ref, att_v),
                (downtotal_ref, total_d),
                (dwu_ref, dwu_v),
                (outsum_ref, outsum_v),
                (normed_ref, normed_v),
                (tok_ref, tok_v),
                (gm_ref, gm_v),
                (cot_ref, cot_v),
            )
        )
    ]
    for load in loads:
        load.start()
    greet(list(peers) + p.ring())

    def other_copy(s):
        return push(xsend_ref.at[s], other_v.at[s], x_s.at[s], x_r.at[s], p.far)

    def part_copy(kind, s):
        if kind == 2:
            return push(xs_ref.at[s], xr_ref.at[s], p_s.at[2, s], p_r.at[2, s], p.far)
        return push(psend.at[kind, s], precv.at[kind, s], p_s.at[kind, s], p_r.at[kind, s], p.sib)

    for s in range(slots):
        other_copy(s).start()
    red_d = Reduce(p, None, None, total_d, zrecv_d, rz.at[0], summed=True)
    red_u = Reduce(p, lambda f: dwu_v.at[f], side_u, total_u, zrecv_u, rz.at[1])
    red_o = Reduce(p, lambda f: outsum_v.at[f], side_o, total_o, zrecv_o, rz.at[2])
    red_q = Reduce(p, lambda f: qblk.at[f], side_q, total_q, zrecv_q, rz.at[3])
    down = Spread(p, spr_d, d_s.at[0], d_r.at[0])
    up = Spread(p, spr_u, d_s.at[1], d_r.at[1])
    qry = Spread(p, spr_q, d_s.at[2], d_r.at[2])
    loads[4].wait()
    red_u.start()
    loads[3].wait()
    red_d.step(0)
    for k in (0, 1, 2):
        loads[k].wait()
    tiles = length // tile

    @pl.loop(0, slots)
    def _(s):
        dk_ref[...] = jnp.zeros_like(dk_ref)
        dv_ref[...] = jnp.zeros_like(dv_ref)
        column = as_column(seg_ref[pl.ds(s, 1), :])

        @pl.loop(0, tiles)
        def _(i):
            rows = pl.ds(pl.multiple_of(i * tile, tile), tile)
            same = column == seg_ref[pl.ds(s, 1), rows]
            cosine = cos_ref[rows, :HEAD]
            sine = sin_ref[rows, :HEAD]
            ones = jnp.ones((8, HEAD), BF16)
            for h in range(heads):
                at = h * HEAD
                q = qkv_v[s, rows, at : at + HEAD]
                k = qkv_v[s, :, part + at : part + at + HEAD]
                v = qkv_v[s, :, 2 * part + at : 2 * part + at + HEAD]
                g, o = [
                    jnp.concatenate(
                        [
                            ref[s, i * (tile // quarter) + j // 2, :, j % 2 * part + at : j % 2 * part + at + HEAD]
                            for j in range(tile // half)
                        ]
                    )
                    for ref in (grad_v, att_v)
                ]
                both = g.astype(F32) * o.astype(F32)
                high = both.astype(BF16)
                low = (both - high.astype(F32)).astype(BF16)
                inner = (mm(ones, high, NT) + mm(ones, low, NT))[:1]
                scores = jnp.where(same, mm(k, q, NT), MASKED)
                weights = jnp.exp(scores - log_ref[s, h : h + 1, rows])
                dots = mm(v, g, NT)
                dscores = (weights * (dots - inner)).astype(BF16)
                dq = mm(dscores, k, TN) * (1.0 / math.sqrt(HEAD))
                gq_v[s, rows, at : at + HEAD] = (dq * cosine - swap_halves(dq) * sine).astype(BF16)
                dk_ref[:, at : at + HEAD] += mm(dscores, q, NN)
                dv_ref[:, at : at + HEAD] += mm(weights.astype(BF16), g, NN)

            def reductions(first, red, steps):
                spread = -(-len(steps) // tiles)
                for k, t in enumerate(steps):
                    pl.when((s == first) & (i == k // spread))(lambda t=t: red.step(t))

            reductions(0, red_d, range(1, lines - 1))
            reductions(1, red_u, range(1, lines - 1))

        for h in range(heads):
            at = h * HEAD
            dk = dk_ref[:, at : at + HEAD]
            dk = dk * cos_ref[:, :HEAD] - swap_halves(dk) * sin_ref[:, :HEAD]
            gq_v[s, :, part + at : part + at + HEAD] = dk.astype(BF16)
        gq_v[s, :, 2 * part :] = dv_ref[...].astype(BF16)

        @pl.loop(0, 4)
        def _(j):
            q = jnp.where(
                j < 2, jnp.where(j == 0, p.diag_d, p.far_d), jnp.where(j == 2, p.sib_d, p.d)
            )
            rows = pl.ds(pl.multiple_of(q * quarter, quarter), quarter)
            gsc[...] = mm(gq_v[s, rows, :], wqkvt_ref[...], NN)

            @pl.when(j == 0)
            def _():
                psend[0, s] = gsc[...].astype(BF16)
                part_copy(0, s).start()

            @pl.when(j == 1)
            def _():
                part_copy(0, s).wait_recv()
                xs_ref[s] = (gsc[...] + precv[0, s].astype(F32)).astype(BF16)
                part_copy(2, s).start()

            @pl.when(j == 2)
            def _():
                psend[1, s] = gsc[...].astype(BF16)
                part_copy(1, s).start()

            @pl.when(j == 3)
            def _():
                gn_ref[s] = gsc[...]

        @pl.when(s == 0)
        def _():
            loads[5].wait()
            red_o.start()
            red_d.own(spr_d.at[p.d])
            red_u.step(0)

    loads[6].wait()
    every = slots * length
    gq_all = gq_v.reshape(every, gq_v.shape[2])
    normed_all = normed_v.reshape(every, width)
    whole = gq_v.shape[2] // 128 * 128

    @pl.loop(0, whole // 128)
    def _(i):
        at = pl.ds(pl.multiple_of(i * 128, 128), 128)
        dwq_ref[at, :] = mm(gq_all[:, at], normed_all[...], TN).astype(BF16)

    if whole < gq_v.shape[2]:
        dwq_ref[whole:, :] = mm(gq_all[:, whole:], normed_all[...], TN).astype(BF16)
    count = n * qblk.shape[1]
    placing = (iota((dwq_ref.shape[0], count), 0) == place_ref[pl.ds(p.d, 1), :]).astype(BF16)
    qblk[...] = mm(placing, dwq_ref[...], TN).astype(BF16).reshape(qblk.shape)
    red_q.start()
    down.start()
    red_u.own(spr_u.at[p.d])
    up.start()
    for k in range(lines - 1):
        red_o.step(k)
    red_o.own(opiece)
    halved = ofin.shape[0] == 2
    mine = p.c if halved else 0
    o_far = push(opiece, ofar, d_s.at[3, 0], d_r.at[3, 0], p.far)
    o_far.start()

    def group(s, k):
        return mod_ref[s, :, k * width : (k + 1) * width]

    gain_attn = vec_ref[1:2, :width]
    gain_mlp = vec_ref[2:3, :width]
    wide = dbup_ref.shape[1]
    total_rows = lambda v: jnp.sum(v, axis=0, keepdims=True)
    for k in range(7, 10):
        loads[k].wait()
    ssend[...] = jnp.zeros_like(ssend)

    @pl.loop(0, slots)
    def _(s):
        other_copy(s).wait_recv()
        part_copy(1, s).wait_recv()
        part_copy(2, s).wait_recv()
        gn = gn_ref[s] + precv[1, s].astype(F32) + xr_ref[s].astype(F32)
        normal, inverse = norm_rows(tok_v[s].astype(F32))
        dtok_v[s] = (
            gm_v[s] + norm_back(gn, normal, inverse, gain_attn * (1.0 + group(s, 1)))
        ).astype(BF16)
        extra = total_rows(cot_v[s].astype(F32) * other_v[s].astype(F32))
        ssend[s, 0:1, :width] = total_rows(gn)
        ssend[s, 1:2, :width] = total_rows(gn * normal)
        ssend[s, 2:3, :width] = sums_ref[s, 3:4, :]
        ssend[s, 3:5, :width] = sums_ref[s, 0:2, :]
        ssend[s, 5:6, :width] = sums_ref[s, 2:3, :] + extra
        ssend[s, 6:7, :width] = sums_ref[s, 4:5, :]

    ssend[0, 7:8, :wide] = dbup_ref[0:1, :]

    def sums_copy(kind):
        return push(ssend, srecv.at[p.d], s_s.at[kind], s_r.at[kind], peers[kind])

    for kind in range(3):
        sums_copy(kind).start()
    srecv[p.d] = ssend[...]
    stores = []

    def store(src, dst):
        stores.append(pltpu.make_async_copy(src, dst, local.at[10 + len(stores)]))
        stores[-1].start()

    store(dtok_v, dtok_out)
    store(other_v, other_out)
    red_q.step(0)
    for kind in range(3):
        sums_copy(kind).wait_recv()
    total = srecv[0]
    for r in range(1, m):
        total = total + srecv[r]
    cols = wada_ref.shape[0]
    gmod = []
    vecs = [jnp.zeros((1, width), F32)] * 3
    for s in range(slots):
        at = lambda k, s=s: total[s, k : k + 1, :width]
        gmod.append(
            jnp.concatenate(
                [at(0), at(1) * gain_attn, at(2), at(3), at(4) * gain_mlp, at(5)], axis=1
            )
        )
        vecs = [
            vecs[0] + at(1) * (1.0 + group(s, 1)),
            vecs[1] + at(4) * (1.0 + group(s, 4)),
            vecs[2] + at(6),
        ]
    blank = jnp.zeros((4, 6 * width), F32)
    tail = jnp.zeros((12 - slots, 6 * width), F32)
    gmod = jnp.concatenate([blank] + gmod + [tail], axis=0).astype(BF16)
    vsend[...] = jnp.zeros_like(vsend)
    pad = round16(hidden_per)
    for g in range(n):
        gsend[g] = gmod[:, g * cols : (g + 1) * cols]
        for k, v in enumerate(vecs):
            vsend[g, k : k + 1, :small] = v[:, g * small : (g + 1) * small]
        for r in range(m):
            vsend[g, 3 + r : 4 + r, :hidden_per] = srecv[r, 0, 7:8, g * pad : g * pad + hidden_per]

    def g_copy(i):
        peer = p.ring_f(i)
        return push(gsend.at[peer], grecv.at[p.f], g_s.at[i], g_r.at[i], (peer, p.d))

    def v_copy(i):
        peer = p.ring_f(i)
        return push(vsend.at[peer], vrecv.at[p.f], v_s.at[i], v_r.at[i], (peer, p.d))

    for i in range(1, n):
        g_copy(i).start()
        v_copy(i).start()
    grecv[p.f] = gsend[p.f]
    vrecv[p.f] = vsend[p.f]
    for k in range(1, lines - 1):
        red_q.step(k)
    down.forward()
    up.forward()
    for i in range(1, n):
        g_copy(i).wait_recv()
    got = grecv[...].reshape(n * 16, cols)
    conds = vblk_ref[...].reshape(n * 16, width)[:, : wada_ref.shape[1]]
    dsend[...] = mm(got, wada_ref[...], NN).reshape(n, 16, conds.shape[1])[:, :8]

    def c_copy(i):
        peer = p.ring_f(i)
        return push(dsend.at[peer], drecv.at[p.f], c_s.at[i], c_r.at[i], (peer, p.d))

    for i in range(1, n):
        c_copy(i).start()
    drecv[p.f] = dsend[p.f]
    red_q.own(spr_q.at[p.d])
    qry.start()
    o_far.wait_recv()
    ofin[mine] = (opiece[...].astype(F32) + ofar[...].astype(F32)).astype(BF16)
    if halved:
        o_sib = push(ofin.at[mine], ofin.at[mine], d_s.at[3, 1], d_r.at[3, 1], p.sib)
        o_sib.start()
    dwada_ref[...] = mm(got, conds, TN)
    dbada_ref[...] = jnp.sum(got.astype(F32), axis=0, keepdims=True)
    for i in range(1, n):
        v_copy(i).wait_recv()
    total = vrecv[0]
    for g in range(1, n):
        total = total + vrecv[g]
    dvec_ref[...] = total
    down.finish()
    store(spr_d, down_out)
    up.finish()
    store(spr_u, up_out)
    if halved:
        push(ofin.at[1 - mine], ofin.at[1 - mine], d_s.at[3, 1], d_r.at[3, 1], p.sib).wait_recv()
    store(ofin, wo_out)
    for i in range(1, n):
        c_copy(i).wait_recv()
    total = drecv[0]
    for g in range(1, n):
        total = total + drecv[g]
    dcond_ref[...] = total[4 : 4 + slots]
    qry.forward()
    qry.finish()
    store(spr_q, q_out)

    for s in range(slots):
        other_copy(s).wait_send()
        for kind in range(3):
            part_copy(kind, s).wait_send()
    for red in (red_d, red_u, red_o, red_q):
        red.drain()
    for spread in (down, up, qry):
        spread.drain()
    o_far.wait_send()
    if halved:
        o_sib.wait_send()
    for kind in range(3):
        sums_copy(kind).wait_send()
    for i in range(1, n):
        g_copy(i).wait_send()
        v_copy(i).wait_send()
        c_copy(i).wait_send()
    for copy in stores:
        copy.wait()


def back(n, m, per, tile, args):
    qkv, grad, att, normed, tokens = args[:5]
    dwu, downtotal, outsum = args[8:11]
    vblk, w_ada, dbup, place = args[19:23]
    slots, quarter, width = tokens.shape
    dma = pltpu.SemaphoreType.DMA
    shape = jax.ShapeDtypeStruct
    vmem = pltpu.VMEM
    rows = (slots, quarter, width)
    length = m * quarter
    part = width // m
    lines = n // 2
    wide = max(width, dbup.shape[1])
    _, block, inner = downtotal.shape
    pad = dwu.shape[1]
    orows = outsum.shape[1]
    halves = 2 if orows < block else 1
    most = place.shape[1] // n
    cols, cond = w_ada.shape
    lanes = max(per)

    def reduced(rows, wide):
        return [vmem((lines, rows, wide), BF16)] * 2 + [vmem((lines + 1, rows, wide), BF16)]

    return pl.pallas_call(
        functools.partial(back_kernel, n, m, per, tile),
        out_shape=(
            shape(rows, BF16),
            shape(rows, BF16),
            shape((m, block, inner), BF16),
            shape((m, pad, width), BF16),
            shape((halves, orows, width), BF16),
            shape((m, most, width), BF16),
            shape((slots, cond), F32),
            shape((cols, cond), F32),
            shape((1, cols), F32),
            shape((8, lanes), F32),
        ),
        in_specs=[ANY] * 11 + [VM] * (len(args) - 11),
        out_specs=(ANY,) * 6 + (VM,) * 4,
        scratch_shapes=[
            vmem(qkv.shape, BF16),
            vmem(grad.shape, BF16),
            vmem(att.shape, BF16),
            vmem(qkv.shape, BF16),
            vmem((length, part), F32),
            vmem((length, part), F32),
            vmem(normed.shape, BF16),
            vmem(rows, BF16),
            vmem(rows, F32),
            vmem(rows, BF16),
            vmem(rows, BF16),
            vmem(rows, BF16),
            vmem((quarter, width), F32),
            vmem((2,) + rows, BF16),
            vmem((2,) + rows, BF16),
            vmem(rows, BF16),
            vmem(rows, BF16),
            vmem(rows, F32),
            vmem((qkv.shape[2], width), BF16),
            vmem((n, most, width), BF16),
            vmem(dwu.shape, BF16),
            vmem(outsum.shape, BF16),
        ]
        + reduced(block, inner)[1:]
        + reduced(pad, width)
        + reduced(orows, width)
        + reduced(most, width)
        + [
            vmem((m, block, inner), BF16),
            vmem((m, pad, width), BF16),
            vmem((m, most, width), BF16),
            vmem((orows, width), BF16),
            vmem((orows, width), BF16),
            vmem((halves, orows, width), BF16),
            vmem((slots, 8, wide), F32),
            vmem((m, slots, 8, wide), F32),
            vmem((n, 16, cols), BF16),
            vmem((n, 16, cols), BF16),
            vmem((n, 8, lanes), F32),
            vmem((n, 8, lanes), F32),
            vmem((n, 8, cond), F32),
            vmem((n, 8, cond), F32),
            dma((3, slots)),
            dma((3, slots)),
            dma((4, 4, 2, lines)),
            dma((4, 3)),
            dma((4, 3)),
            dma((3,)),
            dma((3,)),
            dma((n,)),
            dma((n,)),
            dma((n,)),
            dma((n,)),
            dma((n,)),
            dma((n,)),
            dma((slots,)),
            dma((slots,)),
            dma((24,)),
        ],
        compiler_params=pltpu.CompilerParams(
            collective_id=3, has_side_effects=True, vmem_limit_bytes=LIMIT
        ),
        name="back",
    )(*args)


def finish_kernel(
    n,
    m,
    per,
    base_ref,
    other_ref,
    mod_ref,
    dtok_ref,
    dcond_ref,
    dwada_ref,
    dbada_ref,
    dvec_ref,
    down_ref,
    up_ref,
    wo_ref,
    q_ref,
    home_ref,
    out_ref,
    dtok_out,
    dcond_out,
    dwada_out,
    dbada_out,
    dga_out,
    dwqkv_out,
    dwout_out,
    dgm_out,
    dwup_out,
    dbup_out,
    dwdown_out,
    dbdown_out,
):
    hidden_per, small = per
    slots, _, width = base_ref.shape
    pad = round16(hidden_per)
    part = width // m
    for s in range(slots):
        gate = mod_ref[s, :, 5 * width :]
        out_ref[s] = (base_ref[s] + gate * other_ref[s].astype(F32)).astype(BF16)
    dtok_out[...] = dtok_ref[...]
    dcond_out[...] = dcond_ref[...].astype(BF16)
    dwada_out[...] = dwada_ref[...]
    dbada_out[...] = dbada_ref[...]
    for row, ref in ((0, dga_out), (1, dgm_out), (2, dbdown_out)):
        ref[...] = dvec_ref[row : row + 1, :small]
    for r in range(m):
        dbup_out[:, r * hidden_per : (r + 1) * hidden_per] = dvec_ref[3 + r : 4 + r, :hidden_per]
        piece = down_ref[r, :small].astype(F32)
        for g in range(n):
            at = (g * m + r) * hidden_per
            dwdown_out[:, at : at + hidden_per] = piece[:, g * pad : g * pad + hidden_per]
    dwup_out[...] = jnp.concatenate([up_ref[r][:hidden_per] for r in range(m)]).astype(F32).T
    piece = wo_ref[...].reshape(-1, width)[:small].astype(F32)
    heads = part // HEAD
    for r in range(m):
        for h in range(heads):
            at = r * part + h * HEAD
            dwout_out[:, (h * m + r) * HEAD : (h * m + r + 1) * HEAD] = piece[:, at : at + HEAD]
    count = q_ref.shape[0] * q_ref.shape[1]
    f = lax.axis_index("fsdp")
    homing = (iota((dwqkv_out.shape[0], count), 0) == home_ref[pl.ds(f, 1), :]).astype(BF16)
    dwqkv_out[...] = mm(homing, q_ref[...].reshape(count, width), NN)


def finish(n, m, per, columns, args):
    base, dcond, dwada, dbada = args[0], args[4], args[5], args[6]
    hidden_per, small = per
    rows = base.shape
    width = rows[2]
    shape = jax.ShapeDtypeStruct
    return pl.pallas_call(
        functools.partial(finish_kernel, n, m, per),
        out_shape=(
            shape(rows, BF16),
            shape(rows, BF16),
            shape(dcond.shape, BF16),
            shape(dwada.shape, F32),
            shape(dbada.shape, F32),
            shape((1, small), F32),
            shape((columns, width), F32),
            shape((small, width), F32),
            shape((1, small), F32),
            shape((width, m * hidden_per), F32),
            shape((1, m * hidden_per), F32),
            shape((small, n * m * hidden_per), F32),
            shape((1, small), F32),
        ),
        in_specs=[VM] * len(args),
        out_specs=(VM,) * 13,
        compiler_params=pltpu.CompilerParams(vmem_limit_bytes=LIMIT),
        name="finish",
    )(*args)


def column_plan(shards_n, ranks, columns):
    per = columns // shards_n
    rank_of = (np.arange(columns) // HEAD) % ranks
    lists = [
        [[c for c in range(per) if rank_of[f * per + c] == r] for r in range(ranks)]
        for f in range(shards_n)
    ]
    most = max(len(l) for row in lists for l in row)
    most = -(-most // 16) * 16
    take = np.full((shards_n, ranks, most), -1, np.int32)
    place = np.full((ranks, shards_n * most), -1, np.int32)
    home = np.full((shards_n, ranks * most), -1, np.int32)
    for r in range(ranks):
        order = {c: i for i, c in enumerate(np.flatnonzero(rank_of == r))}
        for f in range(shards_n):
            for i, c in enumerate(lists[f][r]):
                take[f, r, i] = c
                place[r, f * most + i] = order[f * per + c]
                home[f, r * most + i] = c
    return most, take, place, home


def shards(
    tokens,
    condition,
    segments,
    w_ada,
    b_ada,
    gain_attn,
    w_qkv,
    w_out,
    gain_mlp,
    w_up,
    b_up,
    w_down,
    b_down,
    cotangent,
):
    slots, quarter, width = tokens.shape
    length = segments.shape[1]
    n = lax.axis_size("fsdp")
    m = lax.axis_size("dp")
    tile = 2 * quarter
    hidden_per = b_up.shape[0] // m
    small = gain_attn.shape[0]
    per = (hidden_per, small)
    columns = w_qkv.shape[1]
    most, take, place, home = column_plan(n, m, columns * n)
    place = jnp.asarray(place)
    cosine, sine = [jnp.asarray(np.concatenate([v, v], axis=1)) for v in rope_table(length)]
    row = lambda v: v[None]

    (
        qkv,
        normed,
        attended,
        own_attended,
        logs,
        cot_far,
        out_blocks,
        up_blocks,
        mod,
        vec,
        w_qkv_t,
        vec_blocks,
    ) = front(
        n,
        m,
        length,
        tile,
        most,
        (
            tokens,
            cotangent,
            condition,
            segments,
            w_ada.T,
            row(b_ada),
            row(b_up),
            row(gain_attn),
            row(gain_mlp),
            row(b_down),
            w_qkv.T,
            w_out.T,
            w_up,
            jnp.asarray(take.reshape(n * m, most)),
            place,
            cosine,
            sine,
        ),
    )
    w_out_t = out_blocks.reshape(n, -1, width)[:, :small].reshape(width, width)
    grad_middle, base, far_part, grad_attended, dw_up, down_total, out_sum, db_up, sums = middle(
        n,
        m,
        (tokens, cotangent, cot_far, own_attended, w_out_t, up_blocks, mod, vec, w_down.T),
    )
    d_tokens, other_part, down_all, up_all, out_all, qkv_all, d_cond, d_w_ada, d_b_ada, d_vec = back(
        n,
        m,
        per,
        tile,
        (
            qkv,
            grad_attended,
            attended,
            normed,
            tokens,
            grad_middle,
            far_part,
            cotangent,
            dw_up,
            down_total,
            out_sum,
            logs,
            segments,
            cosine,
            sine,
            w_qkv_t,
            mod,
            vec,
            sums,
            vec_blocks,
            w_ada.T,
            db_up,
            place,
        ),
    )
    done = finish(
        n,
        m,
        per,
        columns,
        (
            base,
            other_part,
            mod,
            d_tokens,
            d_cond,
            d_w_ada,
            d_b_ada,
            d_vec,
            down_all,
            up_all,
            out_all,
            qkv_all,
            jnp.asarray(home),
        ),
    )
    flat, turned_back = (4, 5, 8, 10, 12), (3, 6, 7, 11)
    return tuple(
        v.reshape(-1) if i in flat else v.T if i in turned_back else v for i, v in enumerate(done)
    )


def solution(mesh):
    return jax.shard_map(
        shards,
        mesh=mesh,
        in_specs=(
            P("fsdp", "dp", None),
            P("fsdp", None),
            P("fsdp", None),
            P(None, "fsdp"),
            P("fsdp"),
            P("fsdp"),
            P(None, "fsdp"),
            P(None, "fsdp"),
            P("fsdp"),
            P(None, "fsdp"),
            P("fsdp"),
            P(None, "fsdp"),
            P("fsdp"),
            P("fsdp", "dp", None),
        ),
        out_specs=(
            P("fsdp", "dp", None),
            P("fsdp", "dp", None),
            P("fsdp", None),
            P(None, "fsdp"),
            P("fsdp"),
            P("fsdp"),
            P(None, "fsdp"),
            P(None, "fsdp"),
            P("fsdp"),
            P(None, "fsdp"),
            P("fsdp"),
            P(None, "fsdp"),
            P("fsdp"),
        ),
        check_vma=False,
    )
```

time: 860 us -> 208 us (0.24); the launches traced: 849 us -> 207 us
  waiting for transfers between devices: 474 us -> 0 us
  Pallas kernels: 46.5 us -> 202 us
  blocking collectives: 145 us -> 0 us
  matrix products: 74.1 us -> 0 us
  local copies, waits for them, and re-layouts: 49.6 us -> 2.51 us
  other arithmetic: 25.9 us -> 2.56 us
  between operations: 18 us -> 0.67 us
  starting transfers between devices: 15.3 us -> 0 us
    reduce_scatter x7 -> x0, waiting for transfers between devices: 261 us -> none  [the longest x4 166 us: scatter(): return lax.psum_scatter(v, 'fsdp', scatter_dimension=0, tiled=True)]
    pallas_call x2 -> x4, Pallas kernels: 46.5 us -> 202 us  [the longest x1 78.5 us: back(): pl.pallas_call(functools.partial(back_kernel, n, m, per, tile), out_shape...]
    all_gather x7 -> x0, waiting for transfers between devices: 118 us -> none  [the longest x1 37.3 us: shards(): w_up_t = lax.all_gather(up_rows, 'fsdp', axis=0, tiled=True)]
    dot_general x18 -> x0, matrix products: 74.1 us -> none  [mm(): return lax.dot_general(a, b, dims, preferred_element_type=F32)]
    unnamed x3 -> x0, blocking collectives: 73.5 us -> none
    unnamed x17 -> x0, waiting for transfers between devices: 62.5 us -> none
    all_gather x4 -> x0, blocking collectives: 47.3 us -> none  [the longest x3 29.5 us: spread(): return lax.all_gather(v, 'dp', axis=0)]
    psum x1 -> x0, waiting for transfers between devices: 20.2 us -> none  [shards(): out_all = lax.psum(scatter(dw_out_t).astype(F32), 'dp')]
  transfers between devices with their start and end apart: 19 -> 0, of which waited for: 14 -> 0; matrix products, arithmetic and copies ran while one was open for 14% -> 0% of each run, Pallas kernels for 5% -> 0%
where the time goes in v3:
time: 208 us; the launch traced here: 207 us
  Pallas kernels  202 us (97%)
  other arithmetic  2.56 us (1%)
  local copies, waits for them, and re-layouts  2.51 us (1%)
    pallas_call x1, Pallas kernels, back(): pl.pallas_call(functools.partial(back_kernel, n, m, per, tile), out_shape...  78.5 us
    pallas_call x1, Pallas kernels, front(): pl.pallas_call(functools.partial(front_kernel, n, m, (hidden_per, small),...  59.9 us
    pallas_call x1, Pallas kernels, middle(): pl.pallas_call(functools.partial(middle_kernel, n, m), out_shape=(shape(r...  58 us
    pallas_call x1, Pallas kernels, finish(): pl.pallas_call(functools.partial(finish_kernel, n, m, per), out_shape=(sh...  5.24 us

profile of v3, /device:TPU:1, one launch (start us, length us, event | category | flops | bytes accessed | tf_op | source)
XLA Modules:
  0.0 207.4 jit_solution(583970678632628859)
XLA Ops:
  0.6 1.2 broadcast_in_dim.16.bup_ref
  1.9 1.3 broadcast_in_dim.15.bada_ref
  3.1 59.9 %front.1 = (bf16[2,1024,576]{2,1,0:T(8,128)(2,1)}, bf16[2,1024,768]{2,1,0:T(8,128)(2,1)}, bf16[2,4,128,384]{3,2,1,0:T(8,128)(2,1)}, bf16[2,4,128,384]{3,2,1,0:T(...) custom-call(bf16[2,256,768]{2,1,0:T(8,128)(2,1)} %tok_ref.5, ...), custom_call_target="tpu_custom_call" | custom-call | tf_op jit(solution)/shard_map/front/pallas_call | solution.py:741
  63.0 58.0 %middle.1 = (f32[2,256,768]{2,1,0:T(8,128)}, f32[2,256,768]{2,1,0:T(8,128)}, bf16[2,256,768]{2,1,0:T(8,128)(2,1)}, bf16[2,4,128,384]{3,2,1,0:T(8,128)(2,1)}, bf1...) custom-call(bf16[2,256,768]{2,1,0:T(8,128)(2,1)} %tok_ref.5, ...), custom_call_target="tpu_custom_call" | custom-call | tf_op jit(solution)/shard_map/middle/pallas_call | solution.py:1201
  121.1 78.5 %back.1 = (bf16[2,256,768]{2,1,0:T(8,128)(2,1)}, bf16[2,256,768]{2,1,0:T(8,128)(2,1)}, bf16[4,96,768]{2,1,0:T(8,128)(2,1)}, bf16[4,96,768]{2,1,0:T(8,128)(2,1)},...) custom-call(bf16[2,1024,576]{2,1,0:T(8,128)(2,1)} %get-tuple-element, ...), custom_call_target="tpu_custom_call" | custom-call | tf_op jit(solution)/shard_map/back/pallas_call | solution.py:1733
  199.6 5.2 %finish.1 = (bf16[2,256,768]{2,1,0:T(8,128)(2,1)}, bf16[2,256,768]{2,1,0:T(8,128)(2,1)}, bf16[2,128]{1,0:T(2,128)(2,1)}, f32[576,128]{1,0:T(8,128)}, f32[1,576]{...) custom-call(f32[2,256,768]{2,1,0:T(8,128)} %get-tuple-element.63.bas, ...), custom_call_target="tpu_custom_call" | custom-call | tf_op jit(solution)/shard_map/finish/pallas_call | solution.py:1885
  204.8 1.3 reduce.1
  206.1 1.3 reduce

commit v4 on v3

--- a/solution.py
+++ b/solution.py
@@ -109,31 +109,32 @@
 
 class Gather:
     def __init__(self, p, src, slot, sems):
-        self.p, self.src, self.slot = p, src, slot
-        self.zs, self.zr, self.ys, self.yr = [sems.at[k] for k in range(4)]
+        self.p, self.src, self.slot, self.sems = p, src, slot, sems
+
+    def place(self, way, t):
+        return jnp.clip(self.p.a + (t if way else -t), 0, self.p.lines - 1)
 
     def line_copy(self, way, t):
-        p = self.p
-        block = self.slot(jnp.clip(p.a + (t if way else -t), 0, p.lines - 1) * 2 + p.b)
+        p, j = self.p, self.place(way, t)
+        block = self.slot(j * 2 + p.b)
+        leave = 4 * p.lines if way and t == 0 else p.lines + j
         return push(
             self.src if t == 0 else block,
             block,
-            self.zs.at[way, t],
-            self.zr.at[way, t + 1],
+            self.sems.at[leave],
+            self.sems.at[j],
             p.left if way else p.right,
         )
 
-    def line_wait(self, way, t):
-        p = self.p
-        block = self.slot(jnp.clip(p.a + (t if way else -t), 0, p.lines - 1) * 2 + p.b)
-        push(block, block, self.zs.at[way, t], self.zr.at[way, t], p.left if way else p.right).wait_recv()
-
     def side_copy(self, way, t, theirs=False):
-        p = self.p
-        b = 1 - p.b if theirs else p.b
-        block = self.slot(jnp.clip(p.a + (t if way else -t), 0, p.lines - 1) * 2 + b)
+        p, j = self.p, self.place(way, t)
+        block = self.slot(j * 2 + (1 - p.b if theirs else p.b))
         return push(
-            self.src if t == 0 else block, block, self.ys.at[way, t], self.yr.at[way, t], p.side
+            self.src if t == 0 else block,
+            block,
+            self.sems.at[2 * p.lines + j],
+            self.sems.at[3 * p.lines + j],
+            p.side,
         )
 
     def held(self, way, t):
@@ -153,7 +154,7 @@
 
             @pl.when(self.held(way, t))
             def _(way=way):
-                self.line_wait(way, t)
+                self.line_copy(way, t).wait_recv()
                 if t < self.p.lines - 1:
                     pl.when(self.onward(way))(lambda: self.line_copy(way, t).start())
                 self.side_copy(way, t).start()
@@ -201,21 +202,23 @@
             g.drain()
 
 
-def gather_halves(p, src, buf, sems):
+def gather_halves(p, src, buf, sems, first):
     rows = src.shape[0]
     if rows % 32:
-        return Gather(p, src, lambda f: buf.at[f], sems.at[0])
+        return Gather(p, src, lambda f: buf.at[f], sems.at[first])
     cut = [pl.ds(h * rows // 2, rows // 2) for h in range(2)]
     return Both(
-        *[Gather(p, src.at[cut[h]], lambda f, h=h: buf.at[f, cut[h]], sems.at[h]) for h in range(2)]
+        *[
+            Gather(p, src.at[cut[h]], lambda f, h=h: buf.at[f, cut[h]], sems.at[first + h])
+            for h in range(2)
+        ]
     )
 
 
 class Reduce:
     def __init__(self, p, src, side, total, zrecv, sems, summed=False):
         self.p, self.src, self.side, self.total = p, src, side, total
-        self.zrecv, self.summed = zrecv, summed
-        self.ys, self.yr, self.zs, self.zr = [sems.at[k] for k in range(4)]
+        self.zrecv, self.sems, self.summed = zrecv, sems, summed
 
     def order(self):
         lines = self.p.lines
@@ -223,7 +226,9 @@
 
     def side_copy(self, j):
         p = self.p
-        return push(self.src(2 * j + 1 - p.b), self.side.at[j], self.ys.at[0, j], self.yr.at[0, j], p.side)
+        return push(
+            self.src(2 * j + 1 - p.b), self.side.at[j], self.sems.at[j], self.sems.at[p.lines + j], p.side
+        )
 
     def line_copy(self, way, j):
         p = self.p
@@ -231,8 +236,8 @@
         return push(
             self.total.at[j],
             self.zrecv.at[at],
-            self.zs.at[way, j],
-            self.zr.at[way, j],
+            self.sems.at[2 * p.lines + j],
+            self.sems.at[3 * p.lines + at],
             p.left if way else p.right,
         )
 
@@ -240,7 +245,13 @@
         p = self.p
         at = jnp.where(j == p.a, p.lines, j) if way else j
         block = self.zrecv.at[at]
-        push(block, block, self.zs.at[way, j], self.zr.at[way, j], p.left if way else p.right).wait_recv()
+        push(
+            block,
+            block,
+            self.sems.at[2 * p.lines + j],
+            self.sems.at[3 * p.lines + at],
+            p.left if way else p.right,
+        ).wait_recv()
         return block[...].astype(F32)
 
     def start(self):
@@ -293,13 +304,34 @@
                 pl.when(ahead)(lambda way=way, j=j: self.line_copy(way, j).wait_send())
 
 
+class Exchange:
+    def __init__(self, p, src, buf, send, recv):
+        self.p, self.src, self.buf, self.send, self.recv = p, src, buf, send, recv
+
+    def start(self):
+        p = self.p
+        for i in range(1, p.n):
+            peer = p.ring_f(i)
+            push(self.src(peer), self.buf.at[p.f], self.send, self.recv, (peer, p.d)).start()
+
+    def every(self):
+        some = self.buf.at[pl.ds(0, self.p.n - 1)]
+        return push(some, some, self.send, self.recv, self.p.side)
+
+    def finish(self):
+        self.every().wait_recv()
+
+    def drain(self):
+        self.every().wait_send()
+
+
 class Spread:
-    def __init__(self, p, buf, send, recv):
-        self.p, self.buf, self.send, self.recv = p, buf, send, recv
+    def __init__(self, p, slot, send, recv):
+        self.p, self.slot, self.send, self.recv = p, slot, send, recv
 
     def copy(self, kind):
         p = self.p
-        block = self.buf.at[p.far_d if kind == 2 else p.d]
+        block = self.slot(p.far_d if kind == 2 else p.d)
         return push(block, block, self.send.at[kind], self.recv.at[kind], p.far if kind == 1 else p.sib)
 
     def start(self):
@@ -416,10 +448,7 @@
     obuf,
     usrc,
     ubuf,
-    vs,
-    vr,
-    ms,
-    mr,
+    ex,
     gz,
     ts,
     tr,
@@ -442,15 +471,19 @@
     length = m * quarter
     peers = (p.sib, p.far, p.diag)
     ranks = (p.sib_d, p.far_d, p.diag_d)
-    own_tokens = pltpu.make_async_copy(tok_ref, tall_ref.at[p.d], local.at[2, 0])
+    own_tokens = pltpu.make_async_copy(tok_ref, tall_ref.at[p.d], local.at[2])
     own_tokens.start()
     log_v[...] = jnp.zeros_like(log_v)
 
     def prepare():
         vsrc[...] = jnp.zeros_like(vsrc)
-        for row, ref in enumerate((bup_ref, ga_ref, gm_ref, bdown_ref)):
-            vsrc[row : row + 1, : ref.shape[1]] = ref[...]
-        vsrc[4 : 4 + slots, : cond_ref.shape[1]] = cond_ref[...]
+        for row, ref in enumerate((ga_ref, gm_ref, bdown_ref)):
+            vsrc[row : row + 1, : ref.shape[0]] = ref[...].reshape(1, -1)
+        vsrc[4 : 4 + slots, :] = cond_ref[...]
+        b_up = bup_ref[...].reshape(1, -1)
+        for k in range(0, b_up.shape[1], 128):
+            some = b_up[:, k : k + 128]
+            vsrc[8 + k // 128 : 9 + k // 128, : some.shape[1]] = some
         columns = wqkv_ref.shape[0]
         most = qsrc.shape[0]
         taking = take_ref[pl.ds(p.f * m + p.d, 1), :]
@@ -459,11 +492,8 @@
 
     greet(list(peers) + p.ring(), prepare)
 
-    def vec_copy(i):
-        return push(vsrc, vbuf.at[p.f], vs.at[i], vr.at[i], (p.ring_f(i), p.d))
-
-    for i in range(1, n):
-        vec_copy(i).start()
+    vec = Exchange(p, lambda f: vsrc, vbuf, ex.at[0], ex.at[1])
+    vec.start()
 
     def token_copy(kind, k):
         s, rows = k // 2, pl.ds(k % 2 * half, half)
@@ -478,7 +508,7 @@
             p.sib if kind == 0 else p.far,
         )
 
-    qry = gather_halves(p, qsrc, qbuf, gz.at[0])
+    qry = gather_halves(p, qsrc, qbuf, gz, 0)
     qry.start()
     for k in range(2 * slots):
         token_copy(1, k).start()
@@ -501,7 +531,7 @@
         p,
         osrc.at[pl.ds(pl.multiple_of(mine * split, 16), split)],
         lambda f: obuf.at[f, mine],
-        gz.at[1, 0],
+        gz.at[2],
     )
     for h in range(halves):
         obuf[p.f, h] = osrc[h * split : (h + 1) * split]
@@ -511,51 +541,50 @@
     chosen = ((lane == at + p.d * hidden_per) & (at < hidden_per)).astype(BF16)
     usrc[...] = mm(chosen, wup_ref[...], NT).astype(BF16)
     ubuf[p.f] = usrc[...]
-    up = gather_halves(p, usrc, ubuf, gz.at[2])
+    up = Gather(p, usrc, lambda f: ubuf.at[f], gz.at[3])
 
     def pass_on(k):
         token_copy(1, k).wait_recv()
         token_copy(2, k).start()
 
-    for i in range(1, n):
-        vec_copy(i).wait_recv()
-    vecs = vbuf[...].reshape(n * 16, width)
-    mod_cols = mm(vecs[:, : cond_ref.shape[1]], wada_ref[...], NT) + bada_ref[...].astype(F32)
-    mod_send[...] = mod_cols.reshape(n, 16, mod_cols.shape[1])[:, :8]
+    qry.step(1)
+    vec.finish()
+    vecs = vbuf[...].reshape(n * 16, 128)
+    mod_cols = mm(vecs, wada_ref[...], NT) + bada_ref[...].reshape(1, -1).astype(F32)
+    mod_send[...] = mod_cols.reshape(n, 16, mod_cols.shape[1])[:, 4 : 4 + slots]
     mod_recv[p.f] = mod_send[p.f]
 
-    def mod_copy(i):
-        peer = p.ring_f(i)
-        return push(mod_send.at[peer], mod_recv.at[p.f], ms.at[i], mr.at[i], (peer, p.d))
-
-    for i in range(1, n):
-        mod_copy(i).start()
+    mods = Exchange(p, lambda f: mod_send.at[f], mod_recv, ex.at[2], ex.at[3])
+    mods.start()
     vec_out[...] = vbuf[...]
     vecs_ref[...] = jnp.zeros_like(vecs_ref)
-    mine_up = (iota((ups, pad), 0) == iota((ups, pad), 1) + p.d * hidden_per) & (
-        iota((ups, pad), 1) < hidden_per
-    )
-    b_up = mm(vecs[:, :ups], mine_up.astype(BF16), NN)
+    ups = bup_ref.shape[0]
+    b_up = jnp.zeros((n * 16, pad), F32)
+    for k in range(0, ups, 128):
+        lane = iota((128, pad), 1)
+        chosen = (iota((128, pad), 0) + k == lane + p.d * hidden_per) & (lane < hidden_per)
+        some = mm(vecs, chosen.astype(BF16), NN)
+        b_up = b_up + jnp.where(iota((n * 16, pad), 0) % 16 == 8 + k // 128, some, 0.0)
     for g in range(n):
-        vecs_ref[0:1, g * pad : (g + 1) * pad] = b_up[16 * g : 16 * g + 1]
+        vecs_ref[0:1, g * pad : (g + 1) * pad] = jnp.sum(
+            b_up[16 * g : 16 * (g + 1)], axis=0, keepdims=True
+        )
         rest = vecs[16 * g : 16 * g + 8].astype(F32)
-        for k in range(1, 4):
-            vecs_ref[k : k + 1, g * small : (g + 1) * small] = rest[k : k + 1, :small]
-    qry.step(1)
+        for k in range(3):
+            vecs_ref[k + 1 : k + 2, g * small : (g + 1) * small] = rest[k : k + 1, :small]
+    for k in range(2, p.lines - 1):
+        qry.step(k)
     pass_on(0)
-    for i in range(1, n):
-        mod_copy(i).wait_recv()
+    qry.step(p.lines - 1)
+    out.start()
+    mods.finish()
     cols = mod_cols.shape[1]
     for g in range(n):
         for s in range(slots):
-            mod_ref[s, :, g * cols : (g + 1) * cols] = mod_recv[g, 4 + s : 5 + s]
+            mod_ref[s, :, g * cols : (g + 1) * cols] = mod_recv[g, s : s + 1]
     gain = vecs_ref[1:2, :width]
 
-    for k in range(2, p.lines - 1):
-        qry.step(k)
-    out.start()
     pass_on(1)
-    qry.step(p.lines - 1)
     pass_on(2)
     def cot_copy(s):
         return push(cot_ref.at[s], cotfar_v.at[s], cs.at[s], cr.at[s], p.far)
@@ -580,7 +609,7 @@
     def keeps(i):
         _, s, rows = chunk(i)
         return [
-            pltpu.make_async_copy(src.at[s, rows], dst.at[s, rows], local.at[k, i])
+            pltpu.make_async_copy(src.at[s, rows], dst.at[s, rows], local.at[k])
             for k, (src, dst) in enumerate(((qkv_ref, qkv_out), (normed_ref, normed_out)))
         ]
 
@@ -663,7 +692,7 @@
     for k in range(slots * tiles + 2, p.lines):
         up.step(k)
     stores = [
-        pltpu.make_async_copy(src, dst, local.at[2, 1 + k])
+        pltpu.make_async_copy(src, dst, local.at[3 + k])
         for k, (src, dst) in enumerate(
             (
                 (att_v, att_out),
@@ -698,9 +727,8 @@
             att_copy(kind, s).wait_recv()
     stores[5].start()
 
-    for i in range(1, n):
-        vec_copy(i).wait_send()
-        mod_copy(i).wait_send()
+    vec.drain()
+    mods.drain()
     for item in (qry, out, up):
         item.drain()
     if halves == 2:
@@ -713,10 +741,8 @@
         for kind in range(3):
             att_copy(kind, s).wait_send()
 
-    @pl.loop(0, m * slots)
-    def _(i):
-        for keep in keeps(i):
-            keep.wait()
+    for k, (src, dst) in enumerate(((qkv_ref, qkv_out), (normed_ref, normed_out))):
+        pltpu.make_async_copy(src, dst, local.at[k]).wait()
 
     for copy in stores:
         copy.wait()
@@ -731,7 +757,7 @@
     dma = pltpu.SemaphoreType.DMA
     shape = jax.ShapeDtypeStruct
     vmem = pltpu.VMEM
-    hidden_per = b_up.shape[1] // m
+    hidden_per = b_up.shape[0] // m
     small = width // n
     block = round16(small)
     pad = round16(hidden_per)
@@ -752,7 +778,7 @@
             shape((slots, 1, 6 * width), F32),
             shape((8, max(width, n * pad)), F32),
             shape((3 * part, width), BF16),
-            shape((n, 16, width), BF16),
+            shape((n, 16, 128), BF16),
         ),
         in_specs=[ANY] * 2 + [VM] * (len(args) - 2),
         out_specs=(ANY,) * 8 + (VM,) * 4,
@@ -764,21 +790,18 @@
             vmem(att, BF16),
             vmem((slots, 8, length), F32),
             vmem(rows, BF16),
-            vmem((n, 8, w_ada.shape[0]), F32),
-            vmem((n, 8, w_ada.shape[0]), F32),
-            vmem((16, width), BF16),
-            vmem((n, 16, width), BF16),
+            vmem((n, slots, w_ada.shape[0]), F32),
+            vmem((n, slots, w_ada.shape[0]), F32),
+            vmem((16, 128), BF16),
+            vmem((n, 16, 128), BF16),
             vmem((most, width), BF16),
             vmem((n, most, width), BF16),
             vmem((block, width), BF16),
             vmem((n, halves, block // halves, width), BF16),
             vmem((pad, width), BF16),
             vmem((n, pad, width), BF16),
-            dma((n,)),
-            dma((n,)),
-            dma((n,)),
-            dma((n,)),
-            dma((3, 2, 4, 2, lines)),
+            dma((4,)),
+            dma((4, 4 * lines + 1)),
             dma((3, 2 * slots)),
             dma((3, 2 * slots)),
             dma((1,)),
@@ -787,7 +810,7 @@
             dma((3, slots)),
             dma((slots,)),
             dma((slots,)),
-            dma((3, m * slots)),
+            dma((9,)),
         ],
         compiler_params=pltpu.CompilerParams(
             collective_id=1, has_side_effects=True, vmem_limit_bytes=LIMIT
@@ -905,7 +928,7 @@
         drow[...] = got
 
     greet(list(peers) + p.line_peers(), prepare)
-    down = gather_halves(p, drow, dbuf, gz)
+    down = gather_halves(p, drow, dbuf, gz, 0)
     down.start()
 
     def cot_copy(kind, s):
@@ -1098,6 +1121,8 @@
 
     store(dwu_ref.reshape(n, pad, width), dwu_out)
 
+    for s in range(1, slots):
+        leave(s)
 
     @pl.loop(0, 4 * slots)
     def _(i):
@@ -1128,8 +1153,6 @@
             xsend_ref[s] = (gsc[...] + precv[2, s].astype(F32)).astype(BF16)
 
     store(xsend_ref, xsend_out)
-    for s in range(1, slots):
-        leave(s)
     store(gm_ref, gm_out)
     flat = lambda ref: ref.reshape(slots * quarter, width)
     weight_grad(flat(gba_ref), flat(own_ref), dwo_ref.at[:width])
@@ -1253,12 +1276,12 @@
             dma((3, 2 * slots)),
             dma((2, slots)),
             dma((2, slots)),
-            dma((2, 4, 2, lines)),
+            dma((2, 4 * lines + 1)),
             dma((5, slots)),
             dma((5, slots)),
             dma((3, slots)),
             dma((3, slots)),
-            dma((4, 2, lines)),
+            dma((4 * lines + 1,)),
             dma((1,)),
             dma((1,)),
             dma((16,)),
@@ -1341,6 +1364,11 @@
     side_q,
     total_q,
     zrecv_q,
+    qpair,
+    zrecv_l,
+    lown,
+    lside,
+    l_s,
     spr_d,
     spr_u,
     spr_q,
@@ -1362,12 +1390,7 @@
     d_r,
     s_s,
     s_r,
-    g_s,
-    g_r,
-    v_s,
-    v_r,
-    c_s,
-    c_r,
+    ex,
     x_s,
     x_r,
     local,
@@ -1416,9 +1439,21 @@
     red_u = Reduce(p, lambda f: dwu_v.at[f], side_u, total_u, zrecv_u, rz.at[1])
     red_o = Reduce(p, lambda f: outsum_v.at[f], side_o, total_o, zrecv_o, rz.at[2])
     red_q = Reduce(p, lambda f: qblk.at[f], side_q, total_q, zrecv_q, rz.at[3])
-    down = Spread(p, spr_d, d_s.at[0], d_r.at[0])
-    up = Spread(p, spr_u, d_s.at[1], d_r.at[1])
-    qry = Spread(p, spr_q, d_s.at[2], d_r.at[2])
+    cuts = place_ref.shape[1] // (n * qblk.shape[1])
+    if cuts == 2:
+        red_l = Reduce(p, None, None, qpair, zrecv_l, rz.at[4], summed=True)
+
+        def pair_copy(theirs):
+            rows = pl.ds(pl.multiple_of((p.b if theirs else 1 - p.b) * qrows, 16), qrows)
+            return push(lown.at[rows], lside, l_s.at[0], l_s.at[1], p.side)
+
+    down = Spread(p, lambda r: spr_d.at[r], d_s.at[0], d_r.at[0])
+    up = Spread(p, lambda r: spr_u.at[r], d_s.at[1], d_r.at[1])
+    qrows = qblk.shape[1]
+    qry = [
+        Spread(p, lambda r, h=h: spr_q.at[r, pl.ds(h * qrows, qrows)], d_s.at[2 + h], d_r.at[2 + h])
+        for h in range(cuts)
+    ]
     loads[4].wait()
     red_u.start()
     loads[3].wait()
@@ -1474,18 +1509,20 @@
 
             reductions(0, red_d, range(1, lines - 1))
             reductions(1, red_u, range(1, lines - 1))
-
-        for h in range(heads):
-            at = h * HEAD
-            dk = dk_ref[:, at : at + HEAD]
-            dk = dk * cos_ref[:, :HEAD] - swap_halves(dk) * sin_ref[:, :HEAD]
-            gq_v[s, :, part + at : part + at + HEAD] = dk.astype(BF16)
+            reductions(1, red_o, range(lines - 2))
+
+        for at in range(0, part, 128):
+            size = min(128, part - at)
+            dk = dk_ref[:, at : at + size]
+            other = turned(dk) if size == 128 else swap_halves(dk)
+            dk = dk * cos_ref[:, :size] - other * sin_ref[:, :size]
+            gq_v[s, :, part + at : part + at + size] = dk.astype(BF16)
         gq_v[s, :, 2 * part :] = dv_ref[...].astype(BF16)
 
         @pl.loop(0, 4)
         def _(j):
             q = jnp.where(
-                j < 2, jnp.where(j == 0, p.diag_d, p.far_d), jnp.where(j == 2, p.sib_d, p.d)
+                j < 2, jnp.where(j == 0, p.diag_d, p.sib_d), jnp.where(j == 2, p.far_d, p.d)
             )
             rows = pl.ds(pl.multiple_of(q * quarter, quarter), quarter)
             gsc[...] = mm(gq_v[s, rows, :], wqkvt_ref[...], NN)
@@ -1495,13 +1532,13 @@
                 psend[0, s] = gsc[...].astype(BF16)
                 part_copy(0, s).start()
 
-            @pl.when(j == 1)
+            @pl.when(j == 2)
             def _():
                 part_copy(0, s).wait_recv()
                 xs_ref[s] = (gsc[...] + precv[0, s].astype(F32)).astype(BF16)
                 part_copy(2, s).start()
 
-            @pl.when(j == 2)
+            @pl.when(j == 1)
             def _():
                 psend[1, s] = gsc[...].astype(BF16)
                 part_copy(1, s).start()
@@ -1517,32 +1554,28 @@
             red_d.own(spr_d.at[p.d])
             red_u.step(0)
 
+    red_o.step(lines - 2)
     loads[6].wait()
     every = slots * length
     gq_all = gq_v.reshape(every, gq_v.shape[2])
     normed_all = normed_v.reshape(every, width)
-    whole = gq_v.shape[2] // 128 * 128
-
-    @pl.loop(0, whole // 128)
-    def _(i):
-        at = pl.ds(pl.multiple_of(i * 128, 128), 128)
-        dwq_ref[at, :] = mm(gq_all[:, at], normed_all[...], TN).astype(BF16)
-
-    if whole < gq_v.shape[2]:
-        dwq_ref[whole:, :] = mm(gq_all[:, whole:], normed_all[...], TN).astype(BF16)
-    count = n * qblk.shape[1]
+    for at in range(0, gq_v.shape[2], part):
+        dwq_ref[at : at + part, :] = mm(gq_all[:, at : at + part], normed_all[...], TN).astype(BF16)
+    count = n * cuts * qrows
     placing = (iota((dwq_ref.shape[0], count), 0) == place_ref[pl.ds(p.d, 1), :]).astype(BF16)
-    qblk[...] = mm(placing, dwq_ref[...], TN).astype(BF16).reshape(qblk.shape)
+    blocks = mm(placing, dwq_ref[...], TN).astype(BF16).reshape(n, cuts, qrows, width)
+    qblk[...] = blocks[:, 0]
     red_q.start()
+    if cuts == 2:
+        qpair[...] = blocks[:, 1].reshape(qpair.shape)
+        red_l.step(0)
     down.start()
     red_u.own(spr_u.at[p.d])
     up.start()
-    for k in range(lines - 1):
-        red_o.step(k)
     red_o.own(opiece)
     halved = ofin.shape[0] == 2
     mine = p.c if halved else 0
-    o_far = push(opiece, ofar, d_s.at[3, 0], d_r.at[3, 0], p.far)
+    o_far = push(opiece, ofar, d_s.at[4, 0], d_r.at[4, 0], p.far)
     o_far.start()
 
     def group(s, k):
@@ -1556,8 +1589,7 @@
         loads[k].wait()
     ssend[...] = jnp.zeros_like(ssend)
 
-    @pl.loop(0, slots)
-    def _(s):
+    def leave(s):
         other_copy(s).wait_recv()
         part_copy(1, s).wait_recv()
         part_copy(2, s).wait_recv()
@@ -1575,6 +1607,12 @@
         ssend[s, 6:7, :width] = sums_ref[s, 4:5, :]
 
     ssend[0, 7:8, :wide] = dbup_ref[0:1, :]
+    leave(0)
+    if cuts == 2:
+        for k in range(1, lines - 2):
+            red_l.step(k)
+    for s in range(1, slots):
+        leave(s)
 
     def sums_copy(kind):
         return push(ssend, srecv.at[p.d], s_s.at[kind], s_r.at[kind], peers[kind])
@@ -1591,6 +1629,10 @@
     store(dtok_v, dtok_out)
     store(other_v, other_out)
     red_q.step(0)
+    if cuts == 2:
+        red_l.step(lines - 2)
+    for k in range(1, lines - 2):
+        red_q.step(k)
     for kind in range(3):
         sums_copy(kind).wait_recv()
     total = srecv[0]
@@ -1611,9 +1653,7 @@
             vecs[1] + at(4) * (1.0 + group(s, 4)),
             vecs[2] + at(6),
         ]
-    blank = jnp.zeros((4, 6 * width), F32)
-    tail = jnp.zeros((12 - slots, 6 * width), F32)
-    gmod = jnp.concatenate([blank] + gmod + [tail], axis=0).astype(BF16)
+    gmod = jnp.concatenate(gmod, axis=0).astype(BF16).astype(F32)
     vsend[...] = jnp.zeros_like(vsend)
     pad = round16(hidden_per)
     for g in range(n):
@@ -1623,47 +1663,41 @@
         for r in range(m):
             vsend[g, 3 + r : 4 + r, :hidden_per] = srecv[r, 0, 7:8, g * pad : g * pad + hidden_per]
 
-    def g_copy(i):
-        peer = p.ring_f(i)
-        return push(gsend.at[peer], grecv.at[p.f], g_s.at[i], g_r.at[i], (peer, p.d))
-
-    def v_copy(i):
-        peer = p.ring_f(i)
-        return push(vsend.at[peer], vrecv.at[p.f], v_s.at[i], v_r.at[i], (peer, p.d))
-
-    for i in range(1, n):
-        g_copy(i).start()
-        v_copy(i).start()
+    gmods = Exchange(p, lambda f: gsend.at[f], grecv, ex.at[0], ex.at[1])
+    gvecs = Exchange(p, lambda f: vsend.at[f], vrecv, ex.at[2], ex.at[3])
+    gmods.start()
+    gvecs.start()
     grecv[p.f] = gsend[p.f]
     vrecv[p.f] = vsend[p.f]
-    for k in range(1, lines - 1):
-        red_q.step(k)
+    if cuts == 2:
+        red_l.own(lown)
+        pair_copy(False).start()
+    red_q.step(lines - 2)
     down.forward()
     up.forward()
-    for i in range(1, n):
-        g_copy(i).wait_recv()
-    got = grecv[...].reshape(n * 16, cols)
-    conds = vblk_ref[...].reshape(n * 16, width)[:, : wada_ref.shape[1]]
-    dsend[...] = mm(got, wada_ref[...], NN).reshape(n, 16, conds.shape[1])[:, :8]
-
-    def c_copy(i):
-        peer = p.ring_f(i)
-        return push(dsend.at[peer], drecv.at[p.f], c_s.at[i], c_r.at[i], (peer, p.d))
-
-    for i in range(1, n):
-        c_copy(i).start()
+    gmods.finish()
+    got = jnp.concatenate([grecv[g] for g in range(n)], axis=0).astype(BF16)
+    conds = jnp.concatenate([vblk_ref[g, 4 : 4 + slots] for g in range(n)], axis=0)
+    dsend[...] = mm(got, wada_ref[...], NN).reshape(n, slots, conds.shape[1])
+
+    gconds = Exchange(p, lambda f: dsend.at[f], drecv, ex.at[4], ex.at[5])
+    gconds.start()
     drecv[p.f] = dsend[p.f]
-    red_q.own(spr_q.at[p.d])
-    qry.start()
+    if cuts == 2:
+        pair_copy(True).wait_recv()
+        mine_rows = pl.ds(pl.multiple_of(p.b * qrows, 16), qrows)
+        qry[1].slot(p.d)[...] = (lown[mine_rows].astype(F32) + lside[...].astype(F32)).astype(BF16)
+        qry[1].start()
+    red_q.own(qry[0].slot(p.d))
+    qry[0].start()
     o_far.wait_recv()
     ofin[mine] = (opiece[...].astype(F32) + ofar[...].astype(F32)).astype(BF16)
     if halved:
-        o_sib = push(ofin.at[mine], ofin.at[mine], d_s.at[3, 1], d_r.at[3, 1], p.sib)
+        o_sib = push(ofin.at[mine], ofin.at[mine], d_s.at[4, 1], d_r.at[4, 1], p.sib)
         o_sib.start()
     dwada_ref[...] = mm(got, conds, TN)
     dbada_ref[...] = jnp.sum(got.astype(F32), axis=0, keepdims=True)
-    for i in range(1, n):
-        v_copy(i).wait_recv()
+    gvecs.finish()
     total = vrecv[0]
     for g in range(1, n):
         total = total + vrecv[g]
@@ -1673,16 +1707,17 @@
     up.finish()
     store(spr_u, up_out)
     if halved:
-        push(ofin.at[1 - mine], ofin.at[1 - mine], d_s.at[3, 1], d_r.at[3, 1], p.sib).wait_recv()
+        push(ofin.at[1 - mine], ofin.at[1 - mine], d_s.at[4, 1], d_r.at[4, 1], p.sib).wait_recv()
     store(ofin, wo_out)
-    for i in range(1, n):
-        c_copy(i).wait_recv()
+    gconds.finish()
     total = drecv[0]
     for g in range(1, n):
         total = total + drecv[g]
-    dcond_ref[...] = total[4 : 4 + slots]
-    qry.forward()
-    qry.finish()
+    dcond_ref[...] = total
+    for spread in qry:
+        spread.forward()
+    for spread in qry:
+        spread.finish()
     store(spr_q, q_out)
 
     for s in range(slots):
@@ -1691,17 +1726,18 @@
             part_copy(kind, s).wait_send()
     for red in (red_d, red_u, red_o, red_q):
         red.drain()
-    for spread in (down, up, qry):
+    if cuts == 2:
+        red_l.drain()
+        pair_copy(False).wait_send()
+    for spread in (down, up, *qry):
         spread.drain()
     o_far.wait_send()
     if halved:
         o_sib.wait_send()
     for kind in range(3):
         sums_copy(kind).wait_send()
-    for i in range(1, n):
-        g_copy(i).wait_send()
-        v_copy(i).wait_send()
-        c_copy(i).wait_send()
+    for exchange in (gmods, gvecs, gconds):
+        exchange.drain()
     for copy in stores:
         copy.wait()
 
@@ -1724,6 +1760,9 @@
     orows = outsum.shape[1]
     halves = 2 if orows < block else 1
     most = place.shape[1] // n
+    qrows = most // 2 if most % 32 == 0 else most
+    pair = most if qrows < most else 32
+    pair_lines = lines if qrows < most else 1
     cols, cond = w_ada.shape
     lanes = max(per)
 
@@ -1766,14 +1805,21 @@
             vmem(rows, BF16),
             vmem(rows, F32),
             vmem((qkv.shape[2], width), BF16),
-            vmem((n, most, width), BF16),
+            vmem((n, qrows, width), BF16),
             vmem(dwu.shape, BF16),
             vmem(outsum.shape, BF16),
         ]
         + reduced(block, inner)[1:]
         + reduced(pad, width)
         + reduced(orows, width)
-        + reduced(most, width)
+        + reduced(qrows, width)
+        + [
+            vmem((pair_lines, pair, width), BF16),
+            vmem((pair_lines + 1, pair, width), BF16),
+            vmem((pair, width), BF16),
+            vmem((pair // 2, width), BF16),
+            dma((2,)),
+        ]
         + [
             vmem((m, block, inner), BF16),
             vmem((m, pad, width), BF16),
@@ -1783,25 +1829,20 @@
             vmem((halves, orows, width), BF16),
             vmem((slots, 8, wide), F32),
             vmem((m, slots, 8, wide), F32),
-            vmem((n, 16, cols), BF16),
-            vmem((n, 16, cols), BF16),
+            vmem((n, slots, cols), F32),
+            vmem((n, slots, cols), F32),
             vmem((n, 8, lanes), F32),
             vmem((n, 8, lanes), F32),
-            vmem((n, 8, cond), F32),
-            vmem((n, 8, cond), F32),
+            vmem((n, slots, cond), F32),
+            vmem((n, slots, cond), F32),
             dma((3, slots)),
             dma((3, slots)),
-            dma((4, 4, 2, lines)),
-            dma((4, 3)),
-            dma((4, 3)),
+            dma((5, 4 * lines + 1)),
+            dma((5, 3)),
+            dma((5, 3)),
             dma((3,)),
             dma((3,)),
-            dma((n,)),
-            dma((n,)),
-            dma((n,)),
-            dma((n,)),
-            dma((n,)),
-            dma((n,)),
+            dma((6,)),
             dma((slots,)),
             dma((slots,)),
             dma((24,)),
@@ -1854,11 +1895,13 @@
     dtok_out[...] = dtok_ref[...]
     dcond_out[...] = dcond_ref[...].astype(BF16)
     dwada_out[...] = dwada_ref[...]
-    dbada_out[...] = dbada_ref[...]
+    dbada_out[...] = dbada_ref[0, :]
     for row, ref in ((0, dga_out), (1, dgm_out), (2, dbdown_out)):
-        ref[...] = dvec_ref[row : row + 1, :small]
+        ref[...] = dvec_ref[row, :small]
+    dbup_out[...] = jnp.concatenate(
+        [dvec_ref[3 + r : 4 + r, :hidden_per] for r in range(m)], axis=1
+    ).reshape(-1)
     for r in range(m):
-        dbup_out[:, r * hidden_per : (r + 1) * hidden_per] = dvec_ref[3 + r : 4 + r, :hidden_per]
         piece = down_ref[r, :small].astype(F32)
         for g in range(n):
             at = (g * m + r) * hidden_per
@@ -1889,15 +1932,15 @@
             shape(rows, BF16),
             shape(dcond.shape, BF16),
             shape(dwada.shape, F32),
-            shape(dbada.shape, F32),
-            shape((1, small), F32),
+            shape(dbada.shape[1:], F32),
+            shape((small,), F32),
             shape((columns, width), F32),
             shape((small, width), F32),
-            shape((1, small), F32),
+            shape((small,), F32),
             shape((width, m * hidden_per), F32),
-            shape((1, m * hidden_per), F32),
+            shape((m * hidden_per,), F32),
             shape((small, n * m * hidden_per), F32),
-            shape((1, small), F32),
+            shape((small,), F32),
         ),
         in_specs=[VM] * len(args),
         out_specs=(VM,) * 13,
@@ -1956,7 +1999,6 @@
     most, take, place, home = column_plan(n, m, columns * n)
     place = jnp.asarray(place)
     cosine, sine = [jnp.asarray(np.concatenate([v, v], axis=1)) for v in rope_table(length)]
-    row = lambda v: v[None]
 
     (
         qkv,
@@ -1983,11 +2025,11 @@
             condition,
             segments,
             w_ada.T,
-            row(b_ada),
-            row(b_up),
-            row(gain_attn),
-            row(gain_mlp),
-            row(b_down),
+            b_ada,
+            b_up,
+            gain_attn,
+            gain_mlp,
+            b_down,
             w_qkv.T,
             w_out.T,
             w_up,
@@ -2055,10 +2097,8 @@
             jnp.asarray(home),
         ),
     )
-    flat, turned_back = (4, 5, 8, 10, 12), (3, 6, 7, 11)
-    return tuple(
-        v.reshape(-1) if i in flat else v.T if i in turned_back else v for i, v in enumerate(done)
-    )
+    turned_back = (3, 6, 7, 11)
+    return tuple(v.T if i in turned_back else v for i, v in enumerate(done))
 
 
 def solution(mesh):

time: 208 us -> 187 us (0.90)
  Pallas kernels: 202 us -> 186 us
  other arithmetic: 2.56 us -> 0 us
  local copies, waits for them, and re-layouts: 2.51 us -> 0 us
    pallas_call x1, Pallas kernels: 78.5 us -> 67.5 us  [back(): pl.pallas_call(functools.partial(back_kernel, n, m, per, tile), out_shape...]
    pallas_call x1, Pallas kernels: 59.9 us -> 54.7 us  [front(): pl.pallas_call(functools.partial(front_kernel, n, m, (hidden_per, small),...]
    pallas_call x2 -> x0, other arithmetic: 2.56 us -> none  [finish(): pl.pallas_call(functools.partial(finish_kernel, n, m, per), out_shape=(sh...]
    broadcast_in_dim x2 -> x0, local copies, waits for them, and re-layouts: 2.51 us -> none  [shards(): row = lambda v: v[None]]
where the time goes in v4:
time: 187 us
  Pallas kernels  186 us (99%)
    pallas_call x1, Pallas kernels, back(): pl.pallas_call(functools.partial(back_kernel, n, m, per, tile), out_shape...  67.5 us
    pallas_call x1, Pallas kernels, middle(): pl.pallas_call(functools.partial(middle_kernel, n, m), out_shape=(shape(r...  58.5 us
    pallas_call x1, Pallas kernels, front(): pl.pallas_call(functools.partial(front_kernel, n, m, (hidden_per, small),...  54.7 us
    pallas_call x1, Pallas kernels, finish(): pl.pallas_call(functools.partial(finish_kernel, n, m, per), out_shape=(sh...  5.27 us

profile of v4, /device:TPU:1, one launch (start us, length us, event | category | flops | bytes accessed | tf_op | source)
XLA Modules:
  0.0 186.8 jit_solution(3771617942665208239)
XLA Ops:
  0.6 54.7 %front.1 = (bf16[2,1024,576]{2,1,0:T(8,128)(2,1)}, bf16[2,1024,768]{2,1,0:T(8,128)(2,1)}, bf16[2,4,128,384]{3,2,1,0:T(8,128)(2,1)}, bf16[2,4,128,384]{3,2,1,0:T(...) custom-call(bf16[2,256,768]{2,1,0:T(8,128)(2,1)} %tok_ref.5, ...), custom_call_target="tpu_custom_call" | custom-call | tf_op jit(solution)/shard_map/front/pallas_call | solution.py:767
  55.3 58.5 %middle.1 = (f32[2,256,768]{2,1,0:T(8,128)}, f32[2,256,768]{2,1,0:T(8,128)}, bf16[2,256,768]{2,1,0:T(8,128)(2,1)}, bf16[2,4,128,384]{3,2,1,0:T(8,128)(2,1)}, bf1...) custom-call(bf16[2,256,768]{2,1,0:T(8,128)(2,1)} %tok_ref.5, ...), custom_call_target="tpu_custom_call" | custom-call | tf_op jit(solution)/shard_map/middle/pallas_call | solution.py:1224
  113.8 67.5 %back.1 = (bf16[2,256,768]{2,1,0:T(8,128)(2,1)}, bf16[2,256,768]{2,1,0:T(8,128)(2,1)}, bf16[4,96,768]{2,1,0:T(8,128)(2,1)}, bf16[4,96,768]{2,1,0:T(8,128)(2,1)},...) custom-call(bf16[2,1024,576]{2,1,0:T(8,128)(2,1)} %get-tuple-element, ...), custom_call_target="tpu_custom_call" | custom-call | tf_op jit(solution)/shard_map/back/pallas_call | solution.py:1772
  181.4 5.3 %finish.1 = (bf16[2,256,768]{2,1,0:T(8,128)(2,1)}, bf16[2,256,768]{2,1,0:T(8,128)(2,1)}, bf16[2,128]{1,0:T(2,128)(2,1)}, f32[576,128]{1,0:T(8,128)}, f32[576]{0:...) custom-call(f32[2,256,768]{2,1,0:T(8,128)} %get-tuple-element.63.bas, ...), custom_call_target="tpu_custom_call" | custom-call | tf_op jit(solution)/shard_map/finish/pallas_call | solution.py:1928

commit v5 on v4

--- a/solution.py
+++ b/solution.py
@@ -41,7 +41,7 @@
 MESH = pl.DeviceIdType.MESH
 VM = pl.BlockSpec(memory_space=pltpu.VMEM)
 ANY = pl.BlockSpec(memory_space=pl.ANY)
-LIMIT = 63 << 20
+LIMIT = (63 << 20) + (768 << 10)
 
 
 def round16(size):
@@ -216,12 +216,14 @@
 
 
 class Reduce:
-    def __init__(self, p, src, side, total, zrecv, sems, summed=False):
+    def __init__(self, p, src, side, total, zrecv, sems, summed=False, only=None):
         self.p, self.src, self.side, self.total = p, src, side, total
-        self.zrecv, self.sems, self.summed = zrecv, sems, summed
+        self.zrecv, self.sems, self.summed, self.only = zrecv, sems, summed, only
 
     def order(self):
         lines = self.p.lines
+        if self.only is not None:
+            return [self.only]
         return [j for k in range(lines // 2) for j in (lines - 1 - k, k)]
 
     def side_copy(self, j):
@@ -273,6 +275,8 @@
             j = t - (p.lines - 1 - p.a) if way else p.lines - 1 - (t - p.a)
             ahead = (j >= 0) & (j < p.a) if way else (j < p.lines) & (j > p.a)
             behind = p.has_right if way else p.has_left
+            if self.only is not None:
+                ahead &= j == self.only
 
             @pl.when(ahead)
             def _(way=way, j=j, behind=behind):
@@ -285,18 +289,26 @@
 
     def own(self, out):
         p = self.p
+        held = True if self.only is None else p.a == self.only
         for way in range(2):
 
-            @pl.when(p.has_right if way else p.has_left)
+            @pl.when(held & (p.has_right if way else p.has_left))
             def _(way=way):
                 arrived = self.line_wait(way, p.a)
                 self.total[p.a] = (self.total[p.a].astype(F32) + arrived).astype(BF16)
 
-        out[...] = self.total[p.a]
+        if self.only is None:
+            out[...] = self.total[p.a]
+        else:
+            out[...] = jnp.zeros(out.shape, BF16)
+
+            @pl.when(held)
+            def _():
+                out[...] = self.total[p.a]
 
     def drain(self):
         p = self.p
-        for j in range(p.lines):
+        for j in range(p.lines) if self.only is None else [self.only]:
             if not self.summed:
                 self.side_copy(j).wait_send()
             for way in range(2):
@@ -410,11 +422,12 @@
     bada_ref,
     bup_ref,
     ga_ref,
-    gm_ref,
+    gmlp_ref,
     bdown_ref,
     wqkv_ref,
     wout_ref,
     wup_ref,
+    wdown_ref,
     take_ref,
     place_ref,
     cos_ref,
@@ -422,22 +435,24 @@
     qkv_out,
     normed_out,
     att_out,
-    own_out,
     log_out,
-    cotfar_out,
-    wout_out,
-    up_out,
+    gm_out,
+    base_out,
+    xsend_out,
+    gatt_out,
+    dwu_out,
+    downtotal_out,
+    outsum_out,
     mod_ref,
     vecs_ref,
     wqkvt_ref,
     vec_out,
+    dbup_ref,
+    sums_ref,
     qkv_ref,
-    normed_ref,
-    tall_ref,
     att_v,
     arecv,
     log_v,
-    cotfar_v,
     mod_send,
     mod_recv,
     vsrc,
@@ -448,6 +463,35 @@
     obuf,
     usrc,
     ubuf,
+    dsrc,
+    dbuf,
+    cot_v,
+    own_ref,
+    br_ref,
+    mid_ref,
+    nrm_ref,
+    inv_ref,
+    nm_ref,
+    ct_ref,
+    act_ref,
+    gp_ref,
+    gsc,
+    psend,
+    precv,
+    xs_ref,
+    xr_ref,
+    gn_ref,
+    bo_ref,
+    gba_ref,
+    gm_ref,
+    gsend,
+    grecv,
+    dwd_ref,
+    dwu_ref,
+    dwo_ref,
+    oswap,
+    side_d,
+    total_d,
     ex,
     gz,
     ts,
@@ -458,6 +502,15 @@
     ar,
     cs,
     cr,
+    n_s,
+    n_r,
+    p_s,
+    p_r,
+    g_s,
+    g_r,
+    rz,
+    o_s,
+    o_r,
     local,
 ):
     p = Place(n, m)
@@ -466,18 +519,30 @@
     part = width // m
     heads = part // HEAD
     hidden_per, small = per
-    pad = round16(hidden_per)
+    pad = usrc.shape[0]
+    inner = n * hidden_per
     halves = obuf.shape[1]
     length = m * quarter
+    tall_ref = gp_ref
+    normed_ref = act_ref.reshape(slots, length, width)
+    filled = pad > hidden_per or qbuf.shape[0] * osrc.shape[0] > width
+    spare = qbuf.reshape(n * qsrc.shape[0], width)
+    dense = [spare.at[pl.ds(k * width, width)] for k in range(3 if filled else 0)]
     peers = (p.sib, p.far, p.diag)
     ranks = (p.sib_d, p.far_d, p.diag_d)
     own_tokens = pltpu.make_async_copy(tok_ref, tall_ref.at[p.d], local.at[2])
     own_tokens.start()
+    own_cots = [
+        pltpu.make_async_copy(cot_ref, dst, local.at[3 + k])
+        for k, dst in enumerate((cot_v, ct_ref.at[p.d]))
+    ]
+    for copy in own_cots:
+        copy.start()
     log_v[...] = jnp.zeros_like(log_v)
 
     def prepare():
         vsrc[...] = jnp.zeros_like(vsrc)
-        for row, ref in enumerate((ga_ref, gm_ref, bdown_ref)):
+        for row, ref in enumerate((ga_ref, gmlp_ref, bdown_ref)):
             vsrc[row : row + 1, : ref.shape[0]] = ref[...].reshape(1, -1)
         vsrc[4 : 4 + slots, :] = cond_ref[...]
         b_up = bup_ref[...].reshape(1, -1)
@@ -518,8 +583,8 @@
     qbuf[p.f] = qsrc[...]
 
     lane = iota((1, width), 1)
-    rank, inner = lane // part, lane % part
-    want = (inner // HEAD * m + rank) * HEAD + inner % HEAD
+    rank, rest = lane // part, lane % part
+    want = (rest // HEAD * m + rank) * HEAD + rest % HEAD
     chosen = (iota((width, width), 0) == want).astype(BF16)
     got = mm(wout_ref[...], chosen, NN).astype(BF16)
     if small < osrc.shape[0]:
@@ -542,6 +607,19 @@
     usrc[...] = mm(chosen, wup_ref[...], NT).astype(BF16)
     ubuf[p.f] = usrc[...]
     up = Gather(p, usrc, lambda f: ubuf.at[f], gz.at[3])
+    block = dsrc.shape[0]
+    lane = iota((1, inner), 1)
+    want = (lane // hidden_per * m + p.d) * hidden_per + lane % hidden_per
+    got = jnp.zeros((small, inner), F32)
+    for at in range(0, wdown_ref.shape[1], width):
+        chosen = (iota((width, inner), 0) + at == want).astype(BF16)
+        got = got + mm(wdown_ref[:, at : at + width], chosen, NN)
+    got = got.astype(BF16)
+    if small < block:
+        got = jnp.concatenate([got, jnp.zeros((block - small, inner), BF16)])
+    dsrc[...] = got
+    dbuf[p.f] = got
+    down = Gather(p, dsrc, lambda f: dbuf.at[f], gz.at[4])
 
     def pass_on(k):
         token_copy(1, k).wait_recv()
@@ -566,9 +644,9 @@
         some = mm(vecs, chosen.astype(BF16), NN)
         b_up = b_up + jnp.where(iota((n * 16, pad), 0) % 16 == 8 + k // 128, some, 0.0)
     for g in range(n):
-        vecs_ref[0:1, g * pad : (g + 1) * pad] = jnp.sum(
+        vecs_ref[0:1, g * hidden_per : (g + 1) * hidden_per] = jnp.sum(
             b_up[16 * g : 16 * (g + 1)], axis=0, keepdims=True
-        )
+        )[:, :hidden_per]
         rest = vecs[16 * g : 16 * g + 8].astype(F32)
         for k in range(3):
             vecs_ref[k + 1 : k + 2, g * small : (g + 1) * small] = rest[k : k + 1, :small]
@@ -586,17 +664,31 @@
 
     pass_on(1)
     pass_on(2)
-    def cot_copy(s):
-        return push(cot_ref.at[s], cotfar_v.at[s], cs.at[s], cr.at[s], p.far)
+    def cot_copy(kind, s):
+        if kind == 2:
+            block = ct_ref.at[p.far_d, s]
+            return push(block, block, cs.at[kind, s], cr.at[kind, s], p.sib)
+        return push(
+            cot_ref.at[s],
+            ct_ref.at[p.d, s],
+            cs.at[kind, s],
+            cr.at[kind, s],
+            p.sib if kind else p.far,
+        )
 
     for s in range(slots):
-        cot_copy(s).start()
+        cot_copy(0, s).start()
 
     qry.finish()
     up.start()
     count = n * qsrc.shape[0]
-    placing = (iota((3 * part, count), 0) == place_ref[pl.ds(p.d, 1), :]).astype(BF16)
-    wqkvt_ref[...] = mm(placing, qbuf[...].reshape(count, width), NN).astype(BF16)
+    flat_rows = qbuf[...].reshape(count, width)
+    got = jnp.zeros((3 * part, width), F32)
+    for at in range(0, count, width):
+        some = place_ref[pl.ds(p.d, 1), at : at + width]
+        placing = (iota((3 * part, some.shape[1]), 0) == some).astype(BF16)
+        got = got + mm(placing, flat_rows[at : at + width], NN)
+    wqkvt_ref[...] = got.astype(BF16)
     own_tokens.wait()
 
     def chunk(i):
@@ -653,6 +745,72 @@
         return push(
             att_v.at[s, ranks[kind]], arecv.at[s, p.d], as_.at[kind, s], ar.at[kind, s], peers[kind]
         )
+
+    def swap(h):
+        return push(obuf.at[:, h], obuf.at[:, h], os_.at[0], or_.at[0], p.sib)
+
+    def weight_ready():
+        out.finish()
+        if halves == 2:
+            swap(p.c).start()
+            swap(1 - p.c).wait_recv()
+        if filled:
+            qry.drain()
+        if small < osrc.shape[0]:
+            dense[0][...] = compact(obuf[:, 0], small)
+
+    def group(s, k):
+        return mod_ref[s, :, k * width : (k + 1) * width]
+
+    gain_mlp = vecs_ref[2:3, :width]
+    b_down = vecs_ref[3:4, :width]
+    if small < osrc.shape[0]:
+        w_out = lambda: dense[0][...]
+    else:
+        w_out = lambda: obuf[...].reshape(width, width)
+    if pad > hidden_per:
+        w_up = lambda: dense[1][...]
+    else:
+        w_up = lambda: ubuf[...].reshape(inner, width)
+    if small < block:
+        w_down = lambda: dense[2][...]
+    else:
+        w_down = lambda: dbuf[...].reshape(width, inner)
+
+    def nm_copy(kind, s, h):
+        k = s * 2 + h
+        rows = nm_ref.at[p.far_d if kind == 2 else p.d, s, pl.ds(h * half, half)]
+        return push(rows, rows, n_s.at[kind, k], n_r.at[kind, k], p.far if kind == 1 else p.sib)
+
+    def enter(s):
+        for kind in range(3):
+            att_copy(kind, s).wait_recv()
+        arecv[s, p.d] = att_v[s, p.d]
+        for r in range(m):
+            for h in range(2):
+                own_ref[s, h * half : (h + 1) * half, r * part : (r + 1) * part] = arecv[
+                    s, r, :, h * part : (h + 1) * part
+                ]
+        branch = mm(own_ref[s], w_out(), NT)
+        br_ref[s] = branch
+        middle = tall_ref[p.d, s].astype(F32) + group(s, 2) * branch
+        mid_ref[s] = middle
+        normal, inverse = norm_rows(middle)
+        nrm_ref[s] = normal
+        inv_ref[s] = inverse
+        nm_ref[p.d, s] = (normal * (gain_mlp * (1.0 + group(s, 4))) + group(s, 3)).astype(BF16)
+        for kind in (1, 0):
+            for h in range(2):
+                nm_copy(kind, s, h).start()
+
+    def pass_rows(s):
+        for h in range(2):
+            nm_copy(1, s, h).wait_recv()
+            nm_copy(2, s, h).start()
+
+    def arrived(kind, s):
+        for h in range(2):
+            nm_copy(kind, s, h).wait_recv()
 
     for k in range(2, p.lines):
         out.step(k)
@@ -682,310 +840,63 @@
                 )
         for k in range(2, p.lines):
             pl.when(i == k - 2)(lambda k=k: up.step(k))
-        for k in range(slots):
-
-            @pl.when(i == (k + 1) * tiles - 1)
-            def _(k=k):
+
+        @pl.when(i == tiles - 1)
+        def _():
+            for kind in (2, 1, 0):
+                att_copy(kind, 0).start()
+            weight_ready()
+            down.start()
+
+        @pl.when(i == tiles)
+        def _():
+            enter(0)
+            down.step(1)
+
+        @pl.when(i == slots * tiles - 1)
+        def _():
+            for s in range(1, slots):
                 for kind in (2, 1, 0):
-                    att_copy(kind, k).start()
+                    att_copy(kind, s).start()
 
     for k in range(slots * tiles + 2, p.lines):
         up.step(k)
-    stores = [
-        pltpu.make_async_copy(src, dst, local.at[3 + k])
-        for k, (src, dst) in enumerate(
-            (
-                (att_v, att_out),
-                (log_v, log_out),
-                (obuf, wout_out),
-                (ubuf, up_out),
-                (cotfar_v, cotfar_out),
-                (arecv, own_out),
-            )
-        )
-    ]
-    for k in range(2):
-        stores[k].start()
-    for s in range(slots):
-        arecv[s, p.d] = att_v[s, p.d]
-    out.finish()
-    if halves == 2:
-
-        def swap(h):
-            return push(obuf.at[:, h], obuf.at[:, h], os_.at[0], or_.at[0], p.sib)
-
-        swap(p.c).start()
-        swap(1 - p.c).wait_recv()
-    stores[2].start()
-    up.finish()
-    stores[3].start()
-    for s in range(slots):
-        cot_copy(s).wait_recv()
-    stores[4].start()
-    for s in range(slots):
-        for kind in range(3):
-            att_copy(kind, s).wait_recv()
-    stores[5].start()
-
-    vec.drain()
-    mods.drain()
-    for item in (qry, out, up):
-        item.drain()
-    if halves == 2:
-        swap(p.c).wait_send()
-    for k in range(2 * slots):
-        for kind in range(3):
-            token_copy(kind, k).wait_send()
-    for s in range(slots):
-        cot_copy(s).wait_send()
-        for kind in range(3):
-            att_copy(kind, s).wait_send()
-
+    stores = []
+
+    def store(src, dst):
+        stores.append(pltpu.make_async_copy(src, dst, local.at[5 + len(stores)]))
+        stores[-1].start()
+
+    store(att_v, att_out)
+    store(log_v, log_out)
     for k, (src, dst) in enumerate(((qkv_ref, qkv_out), (normed_ref, normed_out))):
         pltpu.make_async_copy(src, dst, local.at[k]).wait()
-
-    for copy in stores:
+    for k in range(2 * slots):
+        token_copy(2, k).wait_send()
+    for copy in own_cots:
         copy.wait()
-
-
-def front(n, m, length, tile, most, args):
-    tokens, cond = args[0], args[2]
-    w_ada, b_up, w_up = args[4], args[6], args[12]
-    slots, quarter, width = tokens.shape
-    part = width // m
-    lines = n // 2
-    dma = pltpu.SemaphoreType.DMA
-    shape = jax.ShapeDtypeStruct
-    vmem = pltpu.VMEM
-    hidden_per = b_up.shape[0] // m
-    small = width // n
-    block = round16(small)
-    pad = round16(hidden_per)
-    halves = 2 if block % 32 == 0 else 1
-    rows = (slots, quarter, width)
-    att = (slots, m, quarter // 2, 2 * part)
-    return pl.pallas_call(
-        functools.partial(front_kernel, n, m, (hidden_per, small), tile),
-        out_shape=(
-            shape((slots, length, 3 * part), BF16),
-            shape((slots, length, width), BF16),
-            shape(att, BF16),
-            shape(att, BF16),
-            shape((slots, 8, length), F32),
-            shape(rows, BF16),
-            shape((n, halves, block // halves, width), BF16),
-            shape((n, pad, width), BF16),
-            shape((slots, 1, 6 * width), F32),
-            shape((8, max(width, n * pad)), F32),
-            shape((3 * part, width), BF16),
-            shape((n, 16, 128), BF16),
-        ),
-        in_specs=[ANY] * 2 + [VM] * (len(args) - 2),
-        out_specs=(ANY,) * 8 + (VM,) * 4,
-        scratch_shapes=[
-            vmem((slots, length, 3 * part), BF16),
-            vmem((slots, length, width), BF16),
-            vmem((m,) + rows, BF16),
-            vmem(att, BF16),
-            vmem(att, BF16),
-            vmem((slots, 8, length), F32),
-            vmem(rows, BF16),
-            vmem((n, slots, w_ada.shape[0]), F32),
-            vmem((n, slots, w_ada.shape[0]), F32),
-            vmem((16, 128), BF16),
-            vmem((n, 16, 128), BF16),
-            vmem((most, width), BF16),
-            vmem((n, most, width), BF16),
-            vmem((block, width), BF16),
-            vmem((n, halves, block // halves, width), BF16),
-            vmem((pad, width), BF16),
-            vmem((n, pad, width), BF16),
-            dma((4,)),
-            dma((4, 4 * lines + 1)),
-            dma((3, 2 * slots)),
-            dma((3, 2 * slots)),
-            dma((1,)),
-            dma((1,)),
-            dma((3, slots)),
-            dma((3, slots)),
-            dma((slots,)),
-            dma((slots,)),
-            dma((9,)),
-        ],
-        compiler_params=pltpu.CompilerParams(
-            collective_id=1, has_side_effects=True, vmem_limit_bytes=LIMIT
-        ),
-        name="front",
-    )(*args)
-
-
-def middle_kernel(
-    n,
-    m,
-    tok_ref,
-    cot_ref,
-    cotfar_ref,
-    att_ref,
-    wout_ref,
-    up_ref,
-    mod_ref,
-    vec_ref,
-    wdown_ref,
-    gm_out,
-    base_out,
-    xsend_out,
-    gatt_out,
-    dwu_out,
-    downtotal_out,
-    outsum_out,
-    dbup_ref,
-    sums_ref,
-    tok_v,
-    cot_v,
-    wout_v,
-    arecv,
-    own_ref,
-    br_ref,
-    mid_ref,
-    nrm_ref,
-    inv_ref,
-    nm_ref,
-    ct_ref,
-    act_ref,
-    gp_ref,
-    drow,
-    ubuf,
-    dbuf,
-    down_v,
-    gsc,
-    psend,
-    precv,
-    xs_ref,
-    xr_ref,
-    gn_ref,
-    bo_ref,
-    gba_ref,
-    gm_ref,
-    xsend_ref,
-    gsend,
-    grecv,
-    dwd_ref,
-    dwu_ref,
-    dwo_ref,
-    oswap,
-    side_d,
-    total_d,
-    n_s,
-    n_r,
-    c_s,
-    c_r,
-    gz,
-    p_s,
-    p_r,
-    g_s,
-    g_r,
-    rz,
-    o_s,
-    o_r,
-    local,
-):
-    p = Place(n, m)
-    slots, quarter, width = tok_ref.shape
-    half = quarter // 2
-    part = width // m
-    small = wdown_ref.shape[0]
-    block, inner = drow.shape
-    pad = ubuf.shape[1]
-    hidden_per = wdown_ref.shape[1] // (n * m)
-    peers = (p.sib, p.far, p.diag)
-    ranks = (p.sib_d, p.far_d, p.diag_d)
-
-    loads = [
-        pltpu.make_async_copy(src, dst, local.at[k])
-        for k, (src, dst) in enumerate(
-            (
-                (att_ref, arecv),
-                (wout_ref, wout_v),
-                (tok_ref, tok_v),
-                (up_ref, ubuf),
-                (cot_ref, ct_ref.at[p.d]),
-                (cotfar_ref, ct_ref.at[p.far_d]),
-                (cot_ref, cot_v),
-            )
-        )
-    ]
-    for load in loads:
-        load.start()
-
-    def prepare():
-        row, lane = iota((wdown_ref.shape[1], inner), 0), iota((1, inner), 1)
-        want = jnp.where(
-            lane % pad < hidden_per, (lane // pad * m + p.d) * hidden_per + lane % pad, -1
-        )
-        got = mm(wdown_ref[...], (row == want).astype(BF16), NN).astype(BF16)
-        if small < block:
-            got = jnp.concatenate([got, jnp.zeros((block - small, inner), BF16)])
-        drow[...] = got
-
-    greet(list(peers) + p.line_peers(), prepare)
-    down = gather_halves(p, drow, dbuf, gz, 0)
-    down.start()
-
-    def cot_copy(kind, s):
-        src = cot_ref if kind == 0 else cotfar_ref
-        at = p.d if kind == 0 else p.far_d
-        return push(src.at[s], ct_ref.at[at, s], c_s.at[kind, s], c_r.at[kind, s], p.sib)
-
-    dbuf[p.f] = drow[...]
-
-    def group(s, k):
-        return mod_ref[s, :, k * width : (k + 1) * width]
-
-    gain = vec_ref[2:3, :width]
-    b_down = vec_ref[3:4, :width]
-    b_up = vec_ref[0:1, :inner]
-
-    def nm_copy(kind, s, h):
-        k = s * 2 + h
-        at = p.far_d if kind == 2 else p.d
-        block = nm_ref.at[at, s, pl.ds(h * half, half)]
-        return push(block, block, n_s.at[kind, k], n_r.at[kind, k], p.far if kind == 1 else p.sib)
-
-    for k in range(3):
-        loads[k].wait()
-
-    @pl.loop(0, slots)
-    def _(s):
-        for r in range(m):
-            for h in range(2):
-                own_ref[s, h * half : (h + 1) * half, r * part : (r + 1) * part] = arecv[
-                    s, r, :, h * part : (h + 1) * part
-                ]
-        branch = mm(own_ref[s], wout_v[...], NT)
-        br_ref[s] = branch
-        middle = tok_v[s].astype(F32) + group(s, 2) * branch
-        mid_ref[s] = middle
-        normal, inverse = norm_rows(middle)
-        nrm_ref[s] = normal
-        inv_ref[s] = inverse
-        nm_ref[p.d, s] = (normal * (gain * (1.0 + group(s, 4))) + group(s, 3)).astype(BF16)
-        for kind in (1, 0):
-            for h in range(2):
-                nm_copy(kind, s, h).start()
-
-    def pass_on(s):
-        for h in range(2):
-            nm_copy(1, s, h).wait_recv()
-            nm_copy(2, s, h).start()
-
-    def arrived(kind, s):
-        for h in range(2):
-            nm_copy(kind, s, h).wait_recv()
-
-    w_up = lambda: ubuf[...].reshape(-1, width)
+    for k in range(2, p.lines):
+        down.step(k)
+    pass_rows(0)
+    for s in range(slots):
+        cot_copy(0, s).wait_recv()
+        cot_copy(2, s).start()
+        cot_copy(1, s).start()
+    for s in range(1, slots):
+        enter(s)
+    up.finish()
+    if pad > hidden_per:
+        dense[1][...] = compact(ubuf[...], hidden_per)
+    down.finish()
+    if small < block:
+        dense[2][...] = compact(dbuf[...], small)
+    for s in range(slots):
+        cot_copy(1, s).wait_recv()
+        cot_copy(2, s).wait_recv()
+        cot_copy(2, s).wait_send()
 
     def expand(q, s):
-        hidden = mm(nm_ref[q, s], w_up(), NT) + b_up
+        hidden = mm(nm_ref[q, s], w_up(), NT) + vecs_ref[0:1, :inner]
         value, slope = gelu_parts(hidden)
         act_ref[q, s] = value.astype(BF16)
         gp_ref[q, s] = slope.astype(BF16)
@@ -995,7 +906,7 @@
     def pull(q, s):
         g = (ct_ref[q, s].astype(F32) * group(s, 5)).astype(BF16)
         ct_ref[q, s] = g
-        grad = (mm(g, down_v[...], NN) * gp_ref[q, s].astype(F32)).astype(BF16)
+        grad = (mm(g, w_down(), NN) * gp_ref[q, s].astype(F32)).astype(BF16)
         gp_ref[q, s] = grad
         dbup_ref[0:1, :] += jnp.sum(grad.astype(F32), axis=0, keepdims=True)
         gsc[...] = mm(grad, w_up(), NN)
@@ -1005,11 +916,27 @@
             return push(xs_ref.at[s], xr_ref.at[s], p_s.at[4, s], p_r.at[4, s], p.far)
         return push(psend.at[kind, s], precv.at[kind, s], p_s.at[kind, s], p_r.at[kind, s], p.sib)
 
-    for k in range(3, 7):
-        loads[k].wait()
-    for s in range(slots):
-        for kind in range(2):
-            cot_copy(kind, s).start()
+    def far_rows(s):
+        @pl.loop(0, 2)
+        def _(i):
+            first = i == 0
+            pl.when(first)(lambda: arrived(2, s))
+            q = jnp.where(first, p.diag_d, p.far_d)
+            expand(q, s)
+            pull(q, s)
+
+            @pl.when(first)
+            def _():
+                psend[0, s] = gsc[...].astype(BF16)
+                part_copy(0, s).start()
+
+            @pl.when(jnp.logical_not(first))
+            def _():
+                part_copy(0, s).wait_recv()
+                xs_ref[s] = (gsc[...] + precv[0, s].astype(F32)).astype(BF16)
+                part_copy(4, s).start()
+
+    far_rows(0)
 
     @pl.loop(0, 2 * slots)
     def _(i):
@@ -1017,37 +944,9 @@
         pl.when(i >= slots)(lambda: arrived(0, s))
         expand(jnp.where(i < slots, p.d, p.sib_d), s)
 
-    down.step(1)
-    for s in range(slots):
-        for kind in range(2):
-            cot_copy(kind, s).wait_recv()
-    pass_on(0)
-    for t in range(2, p.lines):
-        down.step(t)
-    down.finish()
-    down_v[...] = compact(dbuf[...], small)
-
-    @pl.loop(0, 2 * slots)
-    def _(i):
-        s = i // 2
-        first = i % 2 == 0
-        pl.when(first & (s > 0))(lambda: pass_on(s))
-        pl.when(first)(lambda: arrived(2, s))
-        q = jnp.where(first, p.diag_d, p.far_d)
-        expand(q, s)
-        pull(q, s)
-
-        @pl.when(first)
-        def _():
-            psend[0, s] = gsc[...].astype(BF16)
-            part_copy(0, s).start()
-
-        @pl.when(jnp.logical_not(first))
-        def _():
-            part_copy(0, s).wait_recv()
-            xs_ref[s] = (gsc[...] + precv[0, s].astype(F32)).astype(BF16)
-            part_copy(4, s).start()
-
+    for s in range(1, slots):
+        pass_rows(s)
+        far_rows(s)
 
     @pl.loop(0, 2 * slots)
     def _(i):
@@ -1064,8 +963,7 @@
         def _():
             gn_ref[s] = gsc[...]
 
-    def weight_grad(left, right, out_ref):
-        step = 256
+    def weight_grad(left, right, out_ref, step=128):
 
         @pl.loop(0, left.shape[1] // step)
         def _(i):
@@ -1073,7 +971,7 @@
             out_ref[at, :] = mm(left[:, at], right[...], TN).astype(BF16)
 
     every = lambda ref: ref.reshape(m * slots * quarter, ref.shape[3])
-    weight_grad(every(ct_ref), every(act_ref), dwd_ref.at[:width])
+    weight_grad(every(ct_ref), every(act_ref), dwd_ref.at[:width], 256)
     if small < block:
         dwd_ref[...] = padded(dwd_ref[:width], n, block)
     dwd = dwd_ref.reshape(n, block, inner)
@@ -1090,11 +988,11 @@
         cot = cot_v[s].astype(F32)
         gn = gn_ref[s] + precv[1, s].astype(F32) + xr_ref[s].astype(F32)
         normal = nrm_ref[s]
-        grad_middle = cot + norm_back(gn, normal, inv_ref[s], gain * (1.0 + group(s, 4)))
+        grad_middle = cot + norm_back(gn, normal, inv_ref[s], gain_mlp * (1.0 + group(s, 4)))
         gm_ref[s] = grad_middle
         gba = (grad_middle * group(s, 2)).astype(BF16)
         gba_ref[s] = gba
-        gatt = mm(gba, wout_v[...], NN).astype(BF16)
+        gatt = mm(gba, w_out(), NN).astype(BF16)
         for r in range(m):
             for h in range(2):
                 gsend[s, r, :, h * part : (h + 1) * part] = gatt[
@@ -1111,13 +1009,9 @@
         sums_ref[s, 5:8, :] = jnp.zeros((3, width), F32)
 
     leave(0)
-    weight_grad(every(gp_ref), every(nm_ref), dwu_ref)
-
-    stores = []
-
-    def store(src, dst):
-        stores.append(pltpu.make_async_copy(src, dst, local.at[7 + len(stores)]))
-        stores[-1].start()
+    weight_grad(every(gp_ref), every(nm_ref), dwu_ref.at[:inner])
+    if pad > hidden_per:
+        dwu_ref[...] = padded(dwu_ref[:inner], n, pad)
 
     store(dwu_ref.reshape(n, pad, width), dwu_out)
 
@@ -1131,7 +1025,7 @@
         q = jnp.where(
             j < 2, jnp.where(j == 0, p.diag_d, p.sib_d), jnp.where(j == 2, p.d, p.far_d)
         )
-        gsc[...] = mm(act_ref[q, s], down_v[...], NT)
+        gsc[...] = mm(act_ref[q, s], w_down(), NT)
 
         @pl.when(j == 0)
         def _():
@@ -1150,9 +1044,10 @@
         @pl.when(j == 3)
         def _():
             part_copy(2, s).wait_recv()
-            xsend_ref[s] = (gsc[...] + precv[2, s].astype(F32)).astype(BF16)
-
-    store(xsend_ref, xsend_out)
+            part_copy(4, s).wait_send()
+            xs_ref[s] = (gsc[...] + precv[2, s].astype(F32)).astype(BF16)
+
+    store(xs_ref, xsend_out)
     store(gm_ref, gm_out)
     flat = lambda ref: ref.reshape(slots * quarter, width)
     weight_grad(flat(gba_ref), flat(own_ref), dwo_ref.at[:width])
@@ -1162,8 +1057,8 @@
     dwo = dwo_ref.reshape(n, block // rows, rows, width)
     mine = p.c if rows < block else 0
     theirs = 1 - p.c if rows < block else 0
-    swap = push(dwo.at[:, theirs], oswap, o_s.at[0], o_r.at[0], p.sib)
-    swap.start()
+    dwo_swap = push(dwo.at[:, theirs], oswap, o_s.at[0], o_r.at[0], p.sib)
+    dwo_swap.start()
 
     @pl.loop(0, slots)
     def _(s):
@@ -1176,7 +1071,7 @@
     for j in red_down.order():
         red_down.side_sum(j)
     store(total_d, downtotal_out)
-    swap.wait_recv()
+    dwo_swap.wait_recv()
     oswap[...] = (dwo[:, mine].astype(F32) + oswap[...].astype(F32)).astype(BF16)
     store(oswap, outsum_out)
     for s in range(slots):
@@ -1184,18 +1079,27 @@
             grad_copy(kind, s).wait_recv()
     store(grecv, gatt_out)
 
-    down.drain()
+    vec.drain()
+    mods.drain()
+    for item in (out, up, down) if filled else (qry, out, up, down):
+        item.drain()
+    if halves == 2:
+        swap(p.c).wait_send()
+    for k in range(2 * slots):
+        for kind in range(2):
+            token_copy(kind, k).wait_send()
     for j in range(p.lines):
         red_down.side_copy(j).wait_send()
-    swap.wait_send()
+    dwo_swap.wait_send()
     for s in range(slots):
+        for kind in range(2):
+            cot_copy(kind, s).wait_send()
         for kind in range(3):
+            att_copy(kind, s).wait_send()
             grad_copy(kind, s).wait_send()
             for h in range(2):
                 nm_copy(kind, s, h).wait_send()
-        for kind in range(2):
-            cot_copy(kind, s).wait_send()
-        for kind in range(5):
+        for kind in range(4):
             part_copy(kind, s).wait_send()
     for copy in stores:
         copy.wait()
@@ -1209,38 +1113,66 @@
     return mm(chosen.astype(BF16), rows, NN).astype(BF16)
 
 
-def middle(n, m, args):
-    tokens, att, up_t, w_down = args[0], args[3], args[5], args[8]
+def front(n, m, length, tile, most, args):
+    tokens, cond = args[0], args[2]
+    w_ada, b_up = args[4], args[6]
     slots, quarter, width = tokens.shape
+    part = width // m
+    lines = n // 2
     dma = pltpu.SemaphoreType.DMA
     shape = jax.ShapeDtypeStruct
+    vmem = pltpu.VMEM
+    hidden_per = b_up.shape[0] // m
+    small = width // n
+    block = round16(small)
+    pad = round16(hidden_per)
+    inner = n * hidden_per
+    halves = 2 if block % 32 == 0 else 1
+    swapped = block // halves
     rows = (slots, quarter, width)
-    lines = n // 2
-    pad = up_t.shape[1]
-    block = round16(w_down.shape[0])
-    inner = n * pad
-    swapped = block // 2 if block % 32 == 0 else block
-    vmem = pltpu.VMEM
+    att = (slots, m, quarter // 2, 2 * part)
+    assert inner == width
     return pl.pallas_call(
-        functools.partial(middle_kernel, n, m),
+        functools.partial(front_kernel, n, m, (hidden_per, small), tile),
         out_shape=(
+            shape((slots, length, 3 * part), BF16),
+            shape((slots, length, width), BF16),
+            shape(att, BF16),
+            shape((slots, 8, length), F32),
             shape(rows, F32),
             shape(rows, F32),
             shape(rows, BF16),
-            shape(att.shape, BF16),
+            shape(att, BF16),
             shape((n, pad, width), BF16),
             shape((lines, block, inner), BF16),
             shape((n, swapped, width), BF16),
+            shape((slots, 1, 6 * width), F32),
+            shape((8, width), F32),
+            shape((3 * part, width), BF16),
+            shape((n, 16, 128), BF16),
             shape((8, inner), F32),
             shape((slots, 8, width), F32),
         ),
-        in_specs=[ANY] * 6 + [VM] * 3,
-        out_specs=(ANY,) * 7 + (VM,) * 2,
+        in_specs=[ANY] * 2 + [VM] * (len(args) - 2),
+        out_specs=(ANY,) * 11 + (VM,) * 6,
         scratch_shapes=[
+            vmem((slots, length, 3 * part), BF16),
+            vmem(att, BF16),
+            vmem(att, BF16),
+            vmem((slots, 8, length), F32),
+            vmem((n, slots, w_ada.shape[0]), F32),
+            vmem((n, slots, w_ada.shape[0]), F32),
+            vmem((16, 128), BF16),
+            vmem((n, 16, 128), BF16),
+            vmem((most, width), BF16),
+            vmem((n, most, width), BF16),
+            vmem((block, width), BF16),
+            vmem((n, halves, swapped, width), BF16),
+            vmem((pad, width), BF16),
+            vmem((n, pad, width), BF16),
+            vmem((block, inner), BF16),
+            vmem((n, block, inner), BF16),
             vmem(rows, BF16),
-            vmem(rows, BF16),
-            vmem((width, width), BF16),
-            vmem(att.shape, BF16),
             vmem(rows, BF16),
             vmem(rows, F32),
             vmem(rows, F32),
@@ -1248,12 +1180,8 @@
             vmem((slots, quarter, 1), F32),
             vmem((m,) + rows, BF16),
             vmem((m,) + rows, BF16),
-            vmem((m, slots, quarter, inner), BF16),
-            vmem((m, slots, quarter, inner), BF16),
-            vmem((block, inner), BF16),
-            vmem((n, pad, width), BF16),
-            vmem((n, block, inner), BF16),
-            vmem((width, inner), BF16),
+            vmem((m,) + rows, BF16),
+            vmem((m,) + rows, BF16),
             vmem((quarter, width), F32),
             vmem((4,) + rows, BF16),
             vmem((4,) + rows, BF16),
@@ -1263,20 +1191,26 @@
             vmem(rows, F32),
             vmem(rows, BF16),
             vmem(rows, F32),
-            vmem(rows, BF16),
-            vmem(att.shape, BF16),
-            vmem(att.shape, BF16),
+            vmem(att, BF16),
+            vmem(att, BF16),
             vmem((n * block, inner), BF16),
-            vmem((inner, width), BF16),
+            vmem((n * pad, width), BF16),
             vmem((n * block, width), BF16),
             vmem((n, swapped, width), BF16),
             vmem((lines, block, inner), BF16),
             vmem((lines, block, inner), BF16),
+            dma((4,)),
+            dma((5, 4 * lines + 1)),
             dma((3, 2 * slots)),
             dma((3, 2 * slots)),
-            dma((2, slots)),
-            dma((2, slots)),
-            dma((2, 4 * lines + 1)),
+            dma((1,)),
+            dma((1,)),
+            dma((3, slots)),
+            dma((3, slots)),
+            dma((3, slots)),
+            dma((3, slots)),
+            dma((3, 2 * slots)),
+            dma((3, 2 * slots)),
             dma((5, slots)),
             dma((5, slots)),
             dma((3, slots)),
@@ -1287,9 +1221,9 @@
             dma((16,)),
         ],
         compiler_params=pltpu.CompilerParams(
-            collective_id=2, has_side_effects=True, vmem_limit_bytes=LIMIT
+            collective_id=1, has_side_effects=True, vmem_limit_bytes=LIMIT
         ),
-        name="middle",
+        name="front",
     )(*args)
 
 
@@ -1298,6 +1232,7 @@
     m,
     per,
     tile,
+    q_few,
     qkv_ref,
     grad_ref,
     att_ref,
@@ -1350,7 +1285,6 @@
     xr_ref,
     gn_ref,
     dwq_ref,
-    qblk,
     dwu_v,
     outsum_v,
     total_d,
@@ -1361,14 +1295,10 @@
     side_o,
     total_o,
     zrecv_o,
-    side_q,
-    total_q,
-    zrecv_q,
-    qpair,
-    zrecv_l,
-    lown,
-    lside,
-    l_s,
+    q_parts,
+    q_sides,
+    q_totals,
+    q_zrecvs,
     spr_d,
     spr_u,
     spr_q,
@@ -1438,21 +1368,30 @@
     red_d = Reduce(p, None, None, total_d, zrecv_d, rz.at[0], summed=True)
     red_u = Reduce(p, lambda f: dwu_v.at[f], side_u, total_u, zrecv_u, rz.at[1])
     red_o = Reduce(p, lambda f: outsum_v.at[f], side_o, total_o, zrecv_o, rz.at[2])
-    red_q = Reduce(p, lambda f: qblk.at[f], side_q, total_q, zrecv_q, rz.at[3])
-    cuts = place_ref.shape[1] // (n * qblk.shape[1])
-    if cuts == 2:
-        red_l = Reduce(p, None, None, qpair, zrecv_l, rz.at[4], summed=True)
-
-        def pair_copy(theirs):
-            rows = pl.ds(pl.multiple_of((p.b if theirs else 1 - p.b) * qrows, 16), qrows)
-            return push(lown.at[rows], lside, l_s.at[0], l_s.at[1], p.side)
-
+    cuts = [ref.shape[1] for ref in q_parts]
+    red_q = [
+        Reduce(
+            p,
+            (lambda f, k=k: q_parts[k].at[f % 2]) if few else (lambda f, k=k: q_parts[k].at[f]),
+            q_sides[k],
+            q_totals[k],
+            q_zrecvs[k],
+            rz.at[3 + k],
+            only=p.d if few else None,
+        )
+        for k, few in enumerate(q_few)
+    ]
     down = Spread(p, lambda r: spr_d.at[r], d_s.at[0], d_r.at[0])
     up = Spread(p, lambda r: spr_u.at[r], d_s.at[1], d_r.at[1])
-    qrows = qblk.shape[1]
+    firsts = [sum(cuts[:k]) for k in range(len(cuts))]
     qry = [
-        Spread(p, lambda r, h=h: spr_q.at[r, pl.ds(h * qrows, qrows)], d_s.at[2 + h], d_r.at[2 + h])
-        for h in range(cuts)
+        Spread(
+            p,
+            lambda r, k=k: spr_q.at[r, pl.ds(firsts[k], cuts[k])],
+            d_s.at[2 + k],
+            d_r.at[2 + k],
+        )
+        for k in range(len(cuts))
     ]
     loads[4].wait()
     red_u.start()
@@ -1510,6 +1449,7 @@
             reductions(0, red_d, range(1, lines - 1))
             reductions(1, red_u, range(1, lines - 1))
             reductions(1, red_o, range(lines - 2))
+            pl.when((s == 1) & (i == 0))(down.start)
 
         for at in range(0, part, 128):
             size = min(128, part - at)
@@ -1519,33 +1459,22 @@
             gq_v[s, :, part + at : part + at + size] = dk.astype(BF16)
         gq_v[s, :, 2 * part :] = dv_ref[...].astype(BF16)
 
-        @pl.loop(0, 4)
-        def _(j):
-            q = jnp.where(
-                j < 2, jnp.where(j == 0, p.diag_d, p.sib_d), jnp.where(j == 2, p.far_d, p.d)
-            )
-            rows = pl.ds(pl.multiple_of(q * quarter, quarter), quarter)
+        theirs = pl.ds(pl.multiple_of((1 - p.c) * quarter, quarter), quarter)
+        ours = pl.ds(pl.multiple_of(p.c * quarter, quarter), quarter)
+
+        def pull(j, chip):
+            rows = pl.ds(pl.multiple_of(chip * 2 * quarter, 2 * quarter), 2 * quarter)
             gsc[...] = mm(gq_v[s, rows, :], wqkvt_ref[...], NN)
-
-            @pl.when(j == 0)
-            def _():
-                psend[0, s] = gsc[...].astype(BF16)
-                part_copy(0, s).start()
-
-            @pl.when(j == 2)
-            def _():
-                part_copy(0, s).wait_recv()
-                xs_ref[s] = (gsc[...] + precv[0, s].astype(F32)).astype(BF16)
-                part_copy(2, s).start()
-
-            @pl.when(j == 1)
-            def _():
-                psend[1, s] = gsc[...].astype(BF16)
-                part_copy(1, s).start()
-
-            @pl.when(j == 3)
-            def _():
-                gn_ref[s] = gsc[...]
+            psend[j, s] = gsc[theirs].astype(BF16)
+            part_copy(j, s).start()
+
+        pull(0, 1 - p.x)
+        gn_ref[s] = gsc[ours]
+        pull(1, p.x)
+        part_copy(0, s).wait_recv()
+        xs_ref[s] = (gn_ref[s] + precv[0, s].astype(F32)).astype(BF16)
+        part_copy(2, s).start()
+        gn_ref[s] = gsc[ours]
 
         @pl.when(s == 0)
         def _():
@@ -1561,22 +1490,23 @@
     normed_all = normed_v.reshape(every, width)
     for at in range(0, gq_v.shape[2], part):
         dwq_ref[at : at + part, :] = mm(gq_all[:, at : at + part], normed_all[...], TN).astype(BF16)
-    count = n * cuts * qrows
+    count = place_ref.shape[1]
     placing = (iota((dwq_ref.shape[0], count), 0) == place_ref[pl.ds(p.d, 1), :]).astype(BF16)
-    blocks = mm(placing, dwq_ref[...], TN).astype(BF16).reshape(n, cuts, qrows, width)
-    qblk[...] = blocks[:, 0]
-    red_q.start()
-    if cuts == 2:
-        qpair[...] = blocks[:, 1].reshape(qpair.shape)
-        red_l.step(0)
-    down.start()
+    blocks = mm(placing, dwq_ref[...], TN).astype(BF16)
+    at = 0
+    for ref in q_parts:
+        size = ref.shape[0] * ref.shape[1]
+        ref[...] = blocks[at : at + size].reshape(ref.shape)
+        at += size
+    for red in (*red_q[2:], red_q[0]):
+        red.start()
     red_u.own(spr_u.at[p.d])
-    up.start()
     red_o.own(opiece)
     halved = ofin.shape[0] == 2
     mine = p.c if halved else 0
-    o_far = push(opiece, ofar, d_s.at[4, 0], d_r.at[4, 0], p.far)
-    o_far.start()
+    o_far = push(opiece, ofar, d_s.at[5, 0], d_r.at[5, 0], p.far)
+    for red in red_q[1:2]:
+        red.start()
 
     def group(s, k):
         return mod_ref[s, :, k * width : (k + 1) * width]
@@ -1608,17 +1538,19 @@
 
     ssend[0, 7:8, :wide] = dbup_ref[0:1, :]
     leave(0)
-    if cuts == 2:
-        for k in range(1, lines - 2):
-            red_l.step(k)
+    hops = [(k, t) for t in range(lines - 1) for k in reversed(range(len(cuts)))]
+    hops = hops[: -len(cuts)], hops[-len(cuts) :]
+    red_q[-1].step(0)
     for s in range(1, slots):
         leave(s)
 
     def sums_copy(kind):
         return push(ssend, srecv.at[p.d], s_s.at[kind], s_r.at[kind], peers[kind])
 
-    for kind in range(3):
+    for kind in (2, 1, 0):
         sums_copy(kind).start()
+    o_far.start()
+    up.start()
     srecv[p.d] = ssend[...]
     stores = []
 
@@ -1628,11 +1560,8 @@
 
     store(dtok_v, dtok_out)
     store(other_v, other_out)
-    red_q.step(0)
-    if cuts == 2:
-        red_l.step(lines - 2)
-    for k in range(1, lines - 2):
-        red_q.step(k)
+    for k, t in hops[0][1:]:
+        red_q[k].step(t)
     for kind in range(3):
         sums_copy(kind).wait_recv()
     total = srecv[0]
@@ -1655,7 +1584,7 @@
         ]
     gmod = jnp.concatenate(gmod, axis=0).astype(BF16).astype(F32)
     vsend[...] = jnp.zeros_like(vsend)
-    pad = round16(hidden_per)
+    pad = hidden_per
     for g in range(n):
         gsend[g] = gmod[:, g * cols : (g + 1) * cols]
         for k, v in enumerate(vecs):
@@ -1669,12 +1598,13 @@
     gvecs.start()
     grecv[p.f] = gsend[p.f]
     vrecv[p.f] = vsend[p.f]
-    if cuts == 2:
-        red_l.own(lown)
-        pair_copy(False).start()
-    red_q.step(lines - 2)
     down.forward()
+    for k, t in hops[1]:
+        red_q[k].step(t)
     up.forward()
+    for k in reversed(range(len(cuts))):
+        red_q[k].own(qry[k].slot(p.d))
+        qry[k].start()
     gmods.finish()
     got = jnp.concatenate([grecv[g] for g in range(n)], axis=0).astype(BF16)
     conds = jnp.concatenate([vblk_ref[g, 4 : 4 + slots] for g in range(n)], axis=0)
@@ -1683,17 +1613,10 @@
     gconds = Exchange(p, lambda f: dsend.at[f], drecv, ex.at[4], ex.at[5])
     gconds.start()
     drecv[p.f] = dsend[p.f]
-    if cuts == 2:
-        pair_copy(True).wait_recv()
-        mine_rows = pl.ds(pl.multiple_of(p.b * qrows, 16), qrows)
-        qry[1].slot(p.d)[...] = (lown[mine_rows].astype(F32) + lside[...].astype(F32)).astype(BF16)
-        qry[1].start()
-    red_q.own(qry[0].slot(p.d))
-    qry[0].start()
     o_far.wait_recv()
     ofin[mine] = (opiece[...].astype(F32) + ofar[...].astype(F32)).astype(BF16)
     if halved:
-        o_sib = push(ofin.at[mine], ofin.at[mine], d_s.at[4, 1], d_r.at[4, 1], p.sib)
+        o_sib = push(ofin.at[mine], ofin.at[mine], d_s.at[5, 1], d_r.at[5, 1], p.sib)
         o_sib.start()
     dwada_ref[...] = mm(got, conds, TN)
     dbada_ref[...] = jnp.sum(got.astype(F32), axis=0, keepdims=True)
@@ -1707,7 +1630,7 @@
     up.finish()
     store(spr_u, up_out)
     if halved:
-        push(ofin.at[1 - mine], ofin.at[1 - mine], d_s.at[4, 1], d_r.at[4, 1], p.sib).wait_recv()
+        push(ofin.at[1 - mine], ofin.at[1 - mine], d_s.at[5, 1], d_r.at[5, 1], p.sib).wait_recv()
     store(ofin, wo_out)
     gconds.finish()
     total = drecv[0]
@@ -1724,11 +1647,8 @@
         other_copy(s).wait_send()
         for kind in range(3):
             part_copy(kind, s).wait_send()
-    for red in (red_d, red_u, red_o, red_q):
+    for red in (red_d, red_u, red_o, *red_q):
         red.drain()
-    if cuts == 2:
-        red_l.drain()
-        pair_copy(False).wait_send()
     for spread in (down, up, *qry):
         spread.drain()
     o_far.wait_send()
@@ -1742,7 +1662,7 @@
         copy.wait()
 
 
-def back(n, m, per, tile, args):
+def back(n, m, per, tile, parts, args):
     qkv, grad, att, normed, tokens = args[:5]
     dwu, downtotal, outsum = args[8:11]
     vblk, w_ada, dbup, place = args[19:23]
@@ -1759,10 +1679,7 @@
     pad = dwu.shape[1]
     orows = outsum.shape[1]
     halves = 2 if orows < block else 1
-    most = place.shape[1] // n
-    qrows = most // 2 if most % 32 == 0 else most
-    pair = most if qrows < most else 32
-    pair_lines = lines if qrows < most else 1
+    most = sum(rows_k for rows_k, _ in parts)
     cols, cond = w_ada.shape
     lanes = max(per)
 
@@ -1770,7 +1687,7 @@
         return [vmem((lines, rows, wide), BF16)] * 2 + [vmem((lines + 1, rows, wide), BF16)]
 
     return pl.pallas_call(
-        functools.partial(back_kernel, n, m, per, tile),
+        functools.partial(back_kernel, n, m, per, tile, [few for _, few in parts]),
         out_shape=(
             shape(rows, BF16),
             shape(rows, BF16),
@@ -1798,27 +1715,24 @@
             vmem(rows, BF16),
             vmem(rows, BF16),
             vmem(rows, BF16),
-            vmem((quarter, width), F32),
+            vmem((2 * quarter, width), F32),
             vmem((2,) + rows, BF16),
             vmem((2,) + rows, BF16),
             vmem(rows, BF16),
             vmem(rows, BF16),
             vmem(rows, F32),
             vmem((qkv.shape[2], width), BF16),
-            vmem((n, qrows, width), BF16),
             vmem(dwu.shape, BF16),
             vmem(outsum.shape, BF16),
         ]
         + reduced(block, inner)[1:]
         + reduced(pad, width)
         + reduced(orows, width)
-        + reduced(qrows, width)
         + [
-            vmem((pair_lines, pair, width), BF16),
-            vmem((pair_lines + 1, pair, width), BF16),
-            vmem((pair, width), BF16),
-            vmem((pair // 2, width), BF16),
-            dma((2,)),
+            [vmem((2 if few else n, rows_k, width), BF16) for rows_k, few in parts],
+            [vmem((lines, rows_k, width), BF16) for rows_k, _ in parts],
+            [vmem((lines, rows_k, width), BF16) for rows_k, _ in parts],
+            [vmem((lines + 1, rows_k, width), BF16) for rows_k, _ in parts],
         ]
         + [
             vmem((m, block, inner), BF16),
@@ -1837,9 +1751,9 @@
             vmem((n, slots, cond), F32),
             dma((3, slots)),
             dma((3, slots)),
-            dma((5, 4 * lines + 1)),
-            dma((5, 3)),
-            dma((5, 3)),
+            dma((6, 4 * lines + 1)),
+            dma((6, 3)),
+            dma((6, 3)),
             dma((3,)),
             dma((3,)),
             dma((6,)),
@@ -1860,90 +1774,151 @@
     per,
     base_ref,
     other_ref,
-    mod_ref,
     dtok_ref,
-    dcond_ref,
     dwada_ref,
-    dbada_ref,
-    dvec_ref,
     down_ref,
     up_ref,
     wo_ref,
     q_ref,
+    mod_ref,
+    dcond_ref,
+    dbada_ref,
+    dvec_ref,
     home_ref,
     out_ref,
     dtok_out,
+    dwada_out,
+    dwqkv_ref,
+    dwout_ref,
+    dwup_ref,
+    dwdown_ref,
     dcond_out,
-    dwada_out,
     dbada_out,
     dga_out,
-    dwqkv_out,
-    dwout_out,
     dgm_out,
-    dwup_out,
     dbup_out,
-    dwdown_out,
     dbdown_out,
+    up_v,
+    down_v,
+    q_v,
+    wo_v,
+    base_v,
+    other_v,
+    dtok_v,
+    dwada_v,
+    dwup_v,
+    dwdown_v,
+    dwqkv_v,
+    dwout_v,
+    out_v,
+    local,
 ):
     hidden_per, small = per
     slots, _, width = base_ref.shape
-    pad = round16(hidden_per)
+    pad = hidden_per
     part = width // m
+    sources = (up_ref, down_ref, q_ref, wo_ref, base_ref, other_ref, dtok_ref, dwada_ref)
+    places = (up_v, down_v, q_v, wo_v, base_v, other_v, dtok_v, dwada_v)
+    loads = [
+        pltpu.make_async_copy(src, dst, local.at[k])
+        for k, (src, dst) in enumerate(zip(sources, places))
+    ]
+    for load in loads:
+        load.start()
+    stores = []
+
+    def store(src, dst):
+        stores.append(pltpu.make_async_copy(src, dst, local.at[8 + len(stores)]))
+        stores[-1].start()
+
+    loads[0].wait()
+    dwup_v[...] = jnp.concatenate([up_v[r][:hidden_per] for r in range(m)]).astype(F32).T
+    store(dwup_v, dwup_ref)
+    loads[1].wait()
+    for r in range(m):
+        piece = down_v[r, :small].astype(F32)
+        for g in range(n):
+            at = (g * m + r) * hidden_per
+            dwdown_v[:, at : at + hidden_per] = piece[:, g * pad : g * pad + hidden_per]
+    store(dwdown_v, dwdown_ref)
+    loads[2].wait()
+    count = q_v.shape[0] * q_v.shape[1]
+    f = lax.axis_index("fsdp")
+    homing = (iota((dwqkv_ref.shape[0], count), 0) == home_ref[pl.ds(f, 1), :]).astype(BF16)
+    dwqkv_v[...] = mm(homing, q_v[...].reshape(count, width), NN)
+    store(dwqkv_v, dwqkv_ref)
+    for k in (4, 5):
+        loads[k].wait()
     for s in range(slots):
         gate = mod_ref[s, :, 5 * width :]
-        out_ref[s] = (base_ref[s] + gate * other_ref[s].astype(F32)).astype(BF16)
-    dtok_out[...] = dtok_ref[...]
+        out_v[s] = (base_v[s] + gate * other_v[s].astype(F32)).astype(BF16)
+    store(out_v, out_ref)
+    for k, src, dst in ((6, dtok_v, dtok_out), (7, dwada_v, dwada_out)):
+        loads[k].wait()
+        store(src, dst)
+    loads[3].wait()
+    piece = wo_v[...].reshape(-1, width)[:small].astype(F32)
+    heads = part // HEAD
+    for r in range(m):
+        for h in range(heads):
+            at = r * part + h * HEAD
+            dwout_v[:, (h * m + r) * HEAD : (h * m + r + 1) * HEAD] = piece[:, at : at + HEAD]
+    store(dwout_v, dwout_ref)
     dcond_out[...] = dcond_ref[...].astype(BF16)
-    dwada_out[...] = dwada_ref[...]
     dbada_out[...] = dbada_ref[0, :]
     for row, ref in ((0, dga_out), (1, dgm_out), (2, dbdown_out)):
         ref[...] = dvec_ref[row, :small]
     dbup_out[...] = jnp.concatenate(
         [dvec_ref[3 + r : 4 + r, :hidden_per] for r in range(m)], axis=1
     ).reshape(-1)
-    for r in range(m):
-        piece = down_ref[r, :small].astype(F32)
-        for g in range(n):
-            at = (g * m + r) * hidden_per
-            dwdown_out[:, at : at + hidden_per] = piece[:, g * pad : g * pad + hidden_per]
-    dwup_out[...] = jnp.concatenate([up_ref[r][:hidden_per] for r in range(m)]).astype(F32).T
-    piece = wo_ref[...].reshape(-1, width)[:small].astype(F32)
-    heads = part // HEAD
-    for r in range(m):
-        for h in range(heads):
-            at = r * part + h * HEAD
-            dwout_out[:, (h * m + r) * HEAD : (h * m + r + 1) * HEAD] = piece[:, at : at + HEAD]
-    count = q_ref.shape[0] * q_ref.shape[1]
-    f = lax.axis_index("fsdp")
-    homing = (iota((dwqkv_out.shape[0], count), 0) == home_ref[pl.ds(f, 1), :]).astype(BF16)
-    dwqkv_out[...] = mm(homing, q_ref[...].reshape(count, width), NN)
+    for copy in stores:
+        copy.wait()
 
 
 def finish(n, m, per, columns, args):
-    base, dcond, dwada, dbada = args[0], args[4], args[5], args[6]
+    base, other, dtok, dwada, down, up, wo, q, _, dcond, dbada = args[:11]
     hidden_per, small = per
     rows = base.shape
     width = rows[2]
     shape = jax.ShapeDtypeStruct
+    vmem = pltpu.VMEM
+    sizes = (
+        (width, m * hidden_per),
+        (small, n * m * hidden_per),
+        (columns, width),
+        (small, width),
+    )
     return pl.pallas_call(
         functools.partial(finish_kernel, n, m, per),
         out_shape=(
             shape(rows, BF16),
             shape(rows, BF16),
+            shape(dwada.shape, F32),
+            shape(sizes[2], F32),
+            shape(sizes[3], F32),
+            shape(sizes[0], F32),
+            shape(sizes[1], F32),
             shape(dcond.shape, BF16),
-            shape(dwada.shape, F32),
             shape(dbada.shape[1:], F32),
             shape((small,), F32),
-            shape((columns, width), F32),
-            shape((small, width), F32),
             shape((small,), F32),
-            shape((width, m * hidden_per), F32),
             shape((m * hidden_per,), F32),
-            shape((small, n * m * hidden_per), F32),
             shape((small,), F32),
         ),
-        in_specs=[VM] * len(args),
-        out_specs=(VM,) * 13,
+        in_specs=[ANY] * 8 + [VM] * 5,
+        out_specs=(ANY,) * 7 + (VM,) * 6,
+        scratch_shapes=[
+            vmem(up.shape, BF16),
+            vmem(down.shape, BF16),
+            vmem(q.shape, BF16),
+            vmem(wo.shape, BF16),
+            vmem(rows, F32),
+            vmem(rows, BF16),
+            vmem(rows, BF16),
+            vmem(dwada.shape, F32),
+        ]
+        + [vmem(size, F32) for size in sizes]
+        + [vmem(rows, BF16), pltpu.SemaphoreType.DMA((15,))],
         compiler_params=pltpu.CompilerParams(vmem_limit_bytes=LIMIT),
         name="finish",
     )(*args)
@@ -1971,6 +1946,47 @@
     return most, take, place, home
 
 
+def row_parts(shards_n, ranks, columns):
+    per = columns // shards_n
+    rank_of = (np.arange(columns) // HEAD) % ranks
+    lists = [
+        [[c for c in range(per) if rank_of[f * per + c] == r] for r in range(ranks)]
+        for f in range(shards_n)
+    ]
+    most = max(len(l) for row in lists for l in row)
+    least = min(len(l) for row in lists for l in row)
+    uneven = all(
+        len(lists[f][r]) == (most if f // 2 == r else least)
+        for f in range(shards_n)
+        for r in range(ranks)
+    )
+    if uneven and least % 32 == 0 and (most - least) % 16 == 0 and most > least and shards_n == 2 * ranks:
+        parts = [(least // 2, False), (least // 2, False), (most - least, True)]
+    else:
+        parts = [(round16(most), False)]
+    place = []
+    for r in range(ranks):
+        order = {c: i for i, c in enumerate(np.flatnonzero(rank_of == r))}
+        row, first = [], 0
+        for rows, few in parts:
+            for f in (2 * r, 2 * r + 1) if few else range(shards_n):
+                own = lists[f][r][first : first + rows]
+                row += [order[f * per + c] for c in own] + [-1] * (rows - len(own))
+            first += rows
+        place.append(row)
+    home = []
+    for f in range(shards_n):
+        row = []
+        for r in range(ranks):
+            first = 0
+            for rows, few in parts:
+                own = lists[f][r][first : first + rows]
+                row += own + [-1] * (rows - len(own))
+                first += rows
+        home.append(row)
+    return parts, np.asarray(place, np.int32), np.asarray(home, np.int32)
+
+
 def shards(
     tokens,
     condition,
@@ -1991,28 +2007,35 @@
     length = segments.shape[1]
     n = lax.axis_size("fsdp")
     m = lax.axis_size("dp")
-    tile = 2 * quarter
     hidden_per = b_up.shape[0] // m
     small = gain_attn.shape[0]
     per = (hidden_per, small)
     columns = w_qkv.shape[1]
-    most, take, place, home = column_plan(n, m, columns * n)
+    most, take, place, _ = column_plan(n, m, columns * n)
     place = jnp.asarray(place)
+    tile = 2 * quarter if n * most <= 2 * width else quarter
+    parts, place_back, home = row_parts(n, m, columns * n)
+    place_back = jnp.asarray(place_back)
     cosine, sine = [jnp.asarray(np.concatenate([v, v], axis=1)) for v in rope_table(length)]
 
     (
         qkv,
         normed,
         attended,
-        own_attended,
         logs,
-        cot_far,
-        out_blocks,
-        up_blocks,
+        grad_middle,
+        base,
+        far_part,
+        grad_attended,
+        dw_up,
+        down_total,
+        out_sum,
         mod,
         vec,
         w_qkv_t,
         vec_blocks,
+        db_up,
+        sums,
     ) = front(
         n,
         m,
@@ -2033,23 +2056,19 @@
             w_qkv.T,
             w_out.T,
             w_up,
+            w_down.T,
             jnp.asarray(take.reshape(n * m, most)),
             place,
             cosine,
             sine,
         ),
     )
-    w_out_t = out_blocks.reshape(n, -1, width)[:, :small].reshape(width, width)
-    grad_middle, base, far_part, grad_attended, dw_up, down_total, out_sum, db_up, sums = middle(
-        n,
-        m,
-        (tokens, cotangent, cot_far, own_attended, w_out_t, up_blocks, mod, vec, w_down.T),
-    )
     d_tokens, other_part, down_all, up_all, out_all, qkv_all, d_cond, d_w_ada, d_b_ada, d_vec = back(
         n,
         m,
         per,
         tile,
+        parts,
         (
             qkv,
             grad_attended,
@@ -2073,10 +2092,24 @@
             vec_blocks,
             w_ada.T,
             db_up,
-            place,
+            place_back,
         ),
     )
-    done = finish(
+    (
+        outputs,
+        d_tokens,
+        d_w_ada,
+        d_w_qkv,
+        d_w_out,
+        d_w_up,
+        d_w_down,
+        d_cond,
+        d_b_ada,
+        d_gain_attn,
+        d_gain_mlp,
+        d_b_up,
+        d_b_down,
+    ) = finish(
         n,
         m,
         per,
@@ -2084,21 +2117,34 @@
         (
             base,
             other_part,
-            mod,
             d_tokens,
-            d_cond,
             d_w_ada,
-            d_b_ada,
-            d_vec,
             down_all,
             up_all,
             out_all,
             qkv_all,
+            mod,
+            d_cond,
+            d_b_ada,
+            d_vec,
             jnp.asarray(home),
         ),
     )
-    turned_back = (3, 6, 7, 11)
-    return tuple(v.T if i in turned_back else v for i, v in enumerate(done))
+    return (
+        outputs,
+        d_tokens,
+        d_cond,
+        d_w_ada.T,
+        d_b_ada,
+        d_gain_attn,
+        d_w_qkv.T,
+        d_w_out.T,
+        d_gain_mlp,
+        d_w_up,
+        d_b_up,
+        d_w_down.T,
+        d_b_down,
+    )
 
 
 def solution(mesh):

time: 187 us -> 179 us (0.957)
  Pallas kernels: 186 us -> 178 us
    pallas_call x2 -> x1, Pallas kernels: 126 us -> 67.5 us  [back(): pl.pallas_call(functools.partial(back_kernel, n, m, per, tile, [few for _...]
    pallas_call x1, Pallas kernels: 54.7 us -> 105 us  [front(): pl.pallas_call(functools.partial(front_kernel, n, m, (hidden_per, small),...]
where the time goes in v5:
time: 179 us
  Pallas kernels  178 us (99%)
    pallas_call x1, Pallas kernels, front(): pl.pallas_call(functools.partial(front_kernel, n, m, (hidden_per, small),...  105 us
    pallas_call x1, Pallas kernels, back(): pl.pallas_call(functools.partial(back_kernel, n, m, per, tile, [few for _...  67.5 us
    pallas_call x1, Pallas kernels, finish(): pl.pallas_call(functools.partial(finish_kernel, n, m, per), out_shape=(sh...  5.55 us

profile of v5, /device:TPU:1, one launch (start us, length us, event | category | flops | bytes accessed | tf_op | source)
XLA Modules:
  0.0 178.8 jit_solution(11036549727400936514)
XLA Ops:
  0.6 104.9 %front.1 = (bf16[2,1024,576]{2,1,0:T(8,128)(2,1)}, bf16[2,1024,768]{2,1,0:T(8,128)(2,1)}, bf16[2,4,128,384]{3,2,1,0:T(8,128)(2,1)}, f32[2,8,1024]{2,1,0:T(8,128)...) custom-call(bf16[2,256,768]{2,1,0:T(8,128)(2,1)} %tok_ref.3, ...), custom_call_target="tpu_custom_call" | custom-call | tf_op jit(solution)/shard_map/front/pallas_call | solution.py:1135
  105.5 67.5 %back.1 = (bf16[2,256,768]{2,1,0:T(8,128)(2,1)}, bf16[2,256,768]{2,1,0:T(8,128)(2,1)}, bf16[4,96,768]{2,1,0:T(8,128)(2,1)}, bf16[4,96,768]{2,1,0:T(8,128)(2,1)},...) custom-call(bf16[2,1024,576]{2,1,0:T(8,128)(2,1)} %get-tuple-element, ...), custom_call_target="tpu_custom_call" | custom-call | tf_op jit(solution)/shard_map/back/pallas_call | solution.py:1689
  173.1 5.5 %finish.1 = (bf16[2,256,768]{2,1,0:T(8,128)(2,1)}, bf16[2,256,768]{2,1,0:T(8,128)(2,1)}, f32[576,128]{1,0:T(8,128)}, f32[288,768]{1,0:T(8,128)}, f32[96,768]{1,0...) custom-call(f32[2,256,768]{2,1,0:T(8,128)} %get-tuple-element.53.bas, ...), custom_call_target="tpu_custom_call" | custom-call | tf_op jit(solution)/shard_map/finish/pallas_call | solution.py:1891

commit v6 on v5

--- a/solution.py
+++ b/solution.py
@@ -859,6 +859,12 @@
                 for kind in (2, 1, 0):
                     att_copy(kind, s).start()
 
+    def expand(q, s):
+        hidden = mm(nm_ref[q, s], w_up(), NT) + vecs_ref[0:1, :inner]
+        value, slope = gelu_parts(hidden)
+        act_ref[q, s] = value.astype(BF16)
+        gp_ref[q, s] = slope.astype(BF16)
+
     for k in range(slots * tiles + 2, p.lines):
         up.step(k)
     stores = []
@@ -882,11 +888,19 @@
         cot_copy(0, s).wait_recv()
         cot_copy(2, s).start()
         cot_copy(1, s).start()
-    for s in range(1, slots):
-        enter(s)
     up.finish()
     if pad > hidden_per:
         dense[1][...] = compact(ubuf[...], hidden_per)
+
+    def near_rows(s):
+        @pl.loop(0, 2)
+        def _(i):
+            pl.when(i > 0)(lambda: arrived(0, s))
+            expand(jnp.where(i == 0, p.d, p.sib_d), s)
+
+    near_rows(0)
+    for s in range(1, slots):
+        enter(s)
     down.finish()
     if small < block:
         dense[2][...] = compact(dbuf[...], small)
@@ -894,12 +908,6 @@
         cot_copy(1, s).wait_recv()
         cot_copy(2, s).wait_recv()
         cot_copy(2, s).wait_send()
-
-    def expand(q, s):
-        hidden = mm(nm_ref[q, s], w_up(), NT) + vecs_ref[0:1, :inner]
-        value, slope = gelu_parts(hidden)
-        act_ref[q, s] = value.astype(BF16)
-        gp_ref[q, s] = slope.astype(BF16)
 
     dbup_ref[...] = jnp.zeros_like(dbup_ref)
 
@@ -937,13 +945,8 @@
                 part_copy(4, s).start()
 
     far_rows(0)
-
-    @pl.loop(0, 2 * slots)
-    def _(i):
-        s = i % slots
-        pl.when(i >= slots)(lambda: arrived(0, s))
-        expand(jnp.where(i < slots, p.d, p.sib_d), s)
-
+    for s in range(1, slots):
+        near_rows(s)
     for s in range(1, slots):
         pass_rows(s)
         far_rows(s)
@@ -971,7 +974,7 @@
             out_ref[at, :] = mm(left[:, at], right[...], TN).astype(BF16)
 
     every = lambda ref: ref.reshape(m * slots * quarter, ref.shape[3])
-    weight_grad(every(ct_ref), every(act_ref), dwd_ref.at[:width], 256)
+    weight_grad(every(ct_ref), every(act_ref), dwd_ref.at[:width])
     if small < block:
         dwd_ref[...] = padded(dwd_ref[:width], n, block)
     dwd = dwd_ref.reshape(n, block, inner)
@@ -1241,6 +1244,7 @@
     gm_ref,
     xsend_ref,
     cot_ref,
+    base_ref,
     dwu_ref,
     downtotal_ref,
     outsum_ref,
@@ -1257,7 +1261,7 @@
     dbup_ref,
     place_ref,
     dtok_out,
-    other_out,
+    out_out,
     down_out,
     up_out,
     wo_out,
@@ -1559,7 +1563,8 @@
         stores[-1].start()
 
     store(dtok_v, dtok_out)
-    store(other_v, other_out)
+    base_load = pltpu.make_async_copy(base_ref, gn_ref, local.at[23])
+    base_load.start()
     for k, t in hops[0][1:]:
         red_q[k].step(t)
     for kind in range(3):
@@ -1598,6 +1603,10 @@
     gvecs.start()
     grecv[p.f] = gsend[p.f]
     vrecv[p.f] = vsend[p.f]
+    base_load.wait()
+    for s in range(slots):
+        other_v[s] = (gn_ref[s] + group(s, 5) * other_v[s].astype(F32)).astype(BF16)
+    store(other_v, out_out)
     down.forward()
     for k, t in hops[1]:
         red_q[k].step(t)
@@ -1664,8 +1673,8 @@
 
 def back(n, m, per, tile, parts, args):
     qkv, grad, att, normed, tokens = args[:5]
-    dwu, downtotal, outsum = args[8:11]
-    vblk, w_ada, dbup, place = args[19:23]
+    dwu, downtotal, outsum = args[9:12]
+    vblk, w_ada, dbup, place = args[20:24]
     slots, quarter, width = tokens.shape
     dma = pltpu.SemaphoreType.DMA
     shape = jax.ShapeDtypeStruct
@@ -1700,7 +1709,7 @@
             shape((1, cols), F32),
             shape((8, lanes), F32),
         ),
-        in_specs=[ANY] * 11 + [VM] * (len(args) - 11),
+        in_specs=[ANY] * 12 + [VM] * (len(args) - 12),
         out_specs=(ANY,) * 6 + (VM,) * 4,
         scratch_shapes=[
             vmem(qkv.shape, BF16),
@@ -1772,15 +1781,13 @@
     n,
     m,
     per,
-    base_ref,
-    other_ref,
+    outs_ref,
     dtok_ref,
     dwada_ref,
     down_ref,
     up_ref,
     wo_ref,
     q_ref,
-    mod_ref,
     dcond_ref,
     dbada_ref,
     dvec_ref,
@@ -1802,8 +1809,6 @@
     down_v,
     q_v,
     wo_v,
-    base_v,
-    other_v,
     dtok_v,
     dwada_v,
     dwup_v,
@@ -1814,11 +1819,11 @@
     local,
 ):
     hidden_per, small = per
-    slots, _, width = base_ref.shape
+    width = outs_ref.shape[2]
     pad = hidden_per
     part = width // m
-    sources = (up_ref, down_ref, q_ref, wo_ref, base_ref, other_ref, dtok_ref, dwada_ref)
-    places = (up_v, down_v, q_v, wo_v, base_v, other_v, dtok_v, dwada_v)
+    sources = (up_ref, down_ref, q_ref, wo_ref, outs_ref, dtok_ref, dwada_ref)
+    places = (up_v, down_v, q_v, wo_v, out_v, dtok_v, dwada_v)
     loads = [
         pltpu.make_async_copy(src, dst, local.at[k])
         for k, (src, dst) in enumerate(zip(sources, places))
@@ -1828,7 +1833,7 @@
     stores = []
 
     def store(src, dst):
-        stores.append(pltpu.make_async_copy(src, dst, local.at[8 + len(stores)]))
+        stores.append(pltpu.make_async_copy(src, dst, local.at[7 + len(stores)]))
         stores[-1].start()
 
     loads[0].wait()
@@ -1847,13 +1852,7 @@
     homing = (iota((dwqkv_ref.shape[0], count), 0) == home_ref[pl.ds(f, 1), :]).astype(BF16)
     dwqkv_v[...] = mm(homing, q_v[...].reshape(count, width), NN)
     store(dwqkv_v, dwqkv_ref)
-    for k in (4, 5):
-        loads[k].wait()
-    for s in range(slots):
-        gate = mod_ref[s, :, 5 * width :]
-        out_v[s] = (base_v[s] + gate * other_v[s].astype(F32)).astype(BF16)
-    store(out_v, out_ref)
-    for k, src, dst in ((6, dtok_v, dtok_out), (7, dwada_v, dwada_out)):
+    for k, src, dst in ((4, out_v, out_ref), (5, dtok_v, dtok_out), (6, dwada_v, dwada_out)):
         loads[k].wait()
         store(src, dst)
     loads[3].wait()
@@ -1876,9 +1875,9 @@
 
 
 def finish(n, m, per, columns, args):
-    base, other, dtok, dwada, down, up, wo, q, _, dcond, dbada = args[:11]
+    outs, dtok, dwada, down, up, wo, q, dcond, dbada = args[:9]
     hidden_per, small = per
-    rows = base.shape
+    rows = outs.shape
     width = rows[2]
     shape = jax.ShapeDtypeStruct
     vmem = pltpu.VMEM
@@ -1905,20 +1904,18 @@
             shape((m * hidden_per,), F32),
             shape((small,), F32),
         ),
-        in_specs=[ANY] * 8 + [VM] * 5,
+        in_specs=[ANY] * 7 + [VM] * 4,
         out_specs=(ANY,) * 7 + (VM,) * 6,
         scratch_shapes=[
             vmem(up.shape, BF16),
             vmem(down.shape, BF16),
             vmem(q.shape, BF16),
             vmem(wo.shape, BF16),
-            vmem(rows, F32),
-            vmem(rows, BF16),
             vmem(rows, BF16),
             vmem(dwada.shape, F32),
         ]
         + [vmem(size, F32) for size in sizes]
-        + [vmem(rows, BF16), pltpu.SemaphoreType.DMA((15,))],
+        + [vmem(rows, BF16), pltpu.SemaphoreType.DMA((14,))],
         compiler_params=pltpu.CompilerParams(vmem_limit_bytes=LIMIT),
         name="finish",
     )(*args)
@@ -2063,7 +2060,7 @@
             sine,
         ),
     )
-    d_tokens, other_part, down_all, up_all, out_all, qkv_all, d_cond, d_w_ada, d_b_ada, d_vec = back(
+    d_tokens, outputs, down_all, up_all, out_all, qkv_all, d_cond, d_w_ada, d_b_ada, d_vec = back(
         n,
         m,
         per,
@@ -2078,6 +2075,7 @@
             grad_middle,
             far_part,
             cotangent,
+            base,
             dw_up,
             down_total,
             out_sum,
@@ -2115,15 +2113,13 @@
         per,
         columns,
         (
-            base,
-            other_part,
+            outputs,
             d_tokens,
             d_w_ada,
             down_all,
             up_all,
             out_all,
             qkv_all,
-            mod,
             d_cond,
             d_b_ada,
             d_vec,

time: 179 us -> 179 us (level)
  no operation moved by 1% of the time
where the time goes in v6:
time: 179 us
  Pallas kernels  178 us (99%)
    pallas_call x1, Pallas kernels, front(): pl.pallas_call(functools.partial(front_kernel, n, m, (hidden_per, small),...  106 us
    pallas_call x1, Pallas kernels, back(): pl.pallas_call(functools.partial(back_kernel, n, m, per, tile, [few for _...  66.9 us
    pallas_call x1, Pallas kernels, finish(): pl.pallas_call(functools.partial(finish_kernel, n, m, per), out_shape=(sh...  5.12 us

profile of v6, /device:TPU:1, one launch (start us, length us, event | category | flops | bytes accessed | tf_op | source)
XLA Modules:
  0.0 178.5 jit_solution(5808151100240960239)
XLA Ops:
  0.6 105.6 %front.1 = (bf16[2,1024,576]{2,1,0:T(8,128)(2,1)}, bf16[2,1024,768]{2,1,0:T(8,128)(2,1)}, bf16[2,4,128,384]{3,2,1,0:T(8,128)(2,1)}, f32[2,8,1024]{2,1,0:T(8,128)...) custom-call(bf16[2,256,768]{2,1,0:T(8,128)(2,1)} %tok_ref.3, ...), custom_call_target="tpu_custom_call" | custom-call | tf_op jit(solution)/shard_map/front/pallas_call | solution.py:1138
  106.2 66.9 %back.1 = (bf16[2,256,768]{2,1,0:T(8,128)(2,1)}, bf16[2,256,768]{2,1,0:T(8,128)(2,1)}, bf16[4,96,768]{2,1,0:T(8,128)(2,1)}, bf16[4,96,768]{2,1,0:T(8,128)(2,1)},...) custom-call(bf16[2,1024,576]{2,1,0:T(8,128)(2,1)} %get-tuple-element, ...), custom_call_target="tpu_custom_call" | custom-call | tf_op jit(solution)/shard_map/back/pallas_call | solution.py:1698
  173.2 5.1 %finish.1 = (bf16[2,256,768]{2,1,0:T(8,128)(2,1)}, bf16[2,256,768]{2,1,0:T(8,128)(2,1)}, f32[576,128]{1,0:T(8,128)}, f32[288,768]{1,0:T(8,128)}, f32[96,768]{1,0...) custom-call(bf16[2,256,768]{2,1,0:T(8,128)(2,1)} %get-tuple-element., ...), custom_call_target="tpu_custom_call" | custom-call | tf_op jit(solution)/shard_map/finish/pallas_call | solution.py:1890

commit v7 on v6

--- a/solution.py
+++ b/solution.py
@@ -1611,6 +1611,11 @@
     for k, t in hops[1]:
         red_q[k].step(t)
     up.forward()
+    o_far.wait_recv()
+    ofin[mine] = (opiece[...].astype(F32) + ofar[...].astype(F32)).astype(BF16)
+    if halved:
+        o_sib = push(ofin.at[mine], ofin.at[mine], d_s.at[5, 1], d_r.at[5, 1], p.sib)
+        o_sib.start()
     for k in reversed(range(len(cuts))):
         red_q[k].own(qry[k].slot(p.d))
         qry[k].start()
@@ -1622,11 +1627,6 @@
     gconds = Exchange(p, lambda f: dsend.at[f], drecv, ex.at[4], ex.at[5])
     gconds.start()
     drecv[p.f] = dsend[p.f]
-    o_far.wait_recv()
-    ofin[mine] = (opiece[...].astype(F32) + ofar[...].astype(F32)).astype(BF16)
-    if halved:
-        o_sib = push(ofin.at[mine], ofin.at[mine], d_s.at[5, 1], d_r.at[5, 1], p.sib)
-        o_sib.start()
     dwada_ref[...] = mm(got, conds, TN)
     dbada_ref[...] = jnp.sum(got.astype(F32), axis=0, keepdims=True)
     gvecs.finish()

time: 179 us -> 179 us (level)
  no operation moved by 1% of the time
where the time goes in v7:
time: 179 us
  Pallas kernels  178 us (99%)
    pallas_call x1, Pallas kernels, front(): pl.pallas_call(functools.partial(front_kernel, n, m, (hidden_per, small),...  106 us
    pallas_call x1, Pallas kernels, back(): pl.pallas_call(functools.partial(back_kernel, n, m, per, tile, [few for _...  67 us
    pallas_call x1, Pallas kernels, finish(): pl.pallas_call(functools.partial(finish_kernel, n, m, per), out_shape=(sh...  5.12 us

profile of v7, /device:TPU:1, one launch (start us, length us, event | category | flops | bytes accessed | tf_op | source)
XLA Modules:
  0.0 178.5 jit_solution(6965560238323227585)
XLA Ops:
  0.6 105.6 %front.1 = (bf16[2,1024,576]{2,1,0:T(8,128)(2,1)}, bf16[2,1024,768]{2,1,0:T(8,128)(2,1)}, bf16[2,4,128,384]{3,2,1,0:T(8,128)(2,1)}, f32[2,8,1024]{2,1,0:T(8,128)...) custom-call(bf16[2,256,768]{2,1,0:T(8,128)(2,1)} %tok_ref.3, ...), custom_call_target="tpu_custom_call" | custom-call | tf_op jit(solution)/shard_map/front/pallas_call | solution.py:1138
  106.2 67.0 %back.1 = (bf16[2,256,768]{2,1,0:T(8,128)(2,1)}, bf16[2,256,768]{2,1,0:T(8,128)(2,1)}, bf16[4,96,768]{2,1,0:T(8,128)(2,1)}, bf16[4,96,768]{2,1,0:T(8,128)(2,1)},...) custom-call(bf16[2,1024,576]{2,1,0:T(8,128)(2,1)} %get-tuple-element, ...), custom_call_target="tpu_custom_call" | custom-call | tf_op jit(solution)/shard_map/back/pallas_call | solution.py:1698
  173.2 5.1 %finish.1 = (bf16[2,256,768]{2,1,0:T(8,128)(2,1)}, bf16[2,256,768]{2,1,0:T(8,128)(2,1)}, f32[576,128]{1,0:T(8,128)}, f32[288,768]{1,0:T(8,128)}, f32[96,768]{1,0...) custom-call(bf16[2,256,768]{2,1,0:T(8,128)(2,1)} %get-tuple-element., ...), custom_call_target="tpu_custom_call" | custom-call | tf_op jit(solution)/shard_map/finish/pallas_call | solution.py:1890
